TPU v7x, 32 devices: a whole 2x2x4 slice. The times are simulated.
32 devices in a mesh: blk: 4 (over x, core), uly: 8 (over z, y).
Axes of the slice: x: 2, y: 2, z: 4, core: 2. Of those that a mesh axis runs over, the one named last changes fastest.
Arguments:
- video_tokens: bfloat16 [1536, 3072], P(('blk', 'uly')), may hold values from -6 to 6
- text_tokens: bfloat16 [256, 3072], P('uly'), may hold values from -6 to 6
- video_modulation: bfloat16 [3, 3072], replicated, may hold values from -4 to 4
- text_modulation: bfloat16 [3, 3072], replicated, may hold values from -4 to 4
- video_projection: bfloat16 [3072, 3, 2048], P(None, None, 'uly'), may hold values from -0.109375 to 0.109375
- text_projection: bfloat16 [3072, 3, 2048], P(None, None, 'uly'), may hold values from -0.109375 to 0.109375
- video_output: bfloat16 [2048, 3072], P('uly'), may hold values from -0.125 to 0.125
- text_output: bfloat16 [2048, 3072], P('uly'), may hold values from -0.125 to 0.125
- video_gains: float32 [2, 128], replicated, may hold values from 1 to 12
- text_gains: float32 [2, 128], replicated, may hold values from 1 to 12
Outputs:
- video_attention: bfloat16 [1536, 3072], P(('blk', 'uly'))
- text_attention: bfloat16 [256, 3072], P('uly')
All inputs are finite; a program needn't handle non-finite values.
Results may differ from a plain program's by a relative error of at most 0.025.
The roundings to bfloat16 on the way count: a program that leaves them out, or rounds other values in their place, can miss the bound.
Values may be sent and summed in bfloat16 or wider, within the bound.
No kernel may reach another device: no remote copies, remote signals or barrier semaphores. Data moves between devices by JAX's collectives and lax.ppermute only.
A program may use at most 128 MiB of HBM per device.

v0:
```python
import jax
import jax.numpy as jnp
from jax import lax
from jax.sharding import PartitionSpec as P

HD = 128


EPS_NORM = 1e-06


def from_behind(block, axis, distance):
    devices = range(lax.axis_size(axis))
    route = [((i - distance) % len(devices), i) for i in devices]
    return lax.ppermute(block, axis, route)


def combined_all(x, axis, join):
    gathered = jax.tree.map(
        lambda a, kind: lax.all_gather(a.astype(kind), axis),
        x,
        jax.tree.map(lambda a: jnp.bfloat16 if a.dtype == jnp.float32 else a.dtype, x),
    )

    def take(source):
        return jax.tree.map(
            lambda a, own: lax.dynamic_index_in_dim(a, source, 0, False).astype(own.dtype),
            gathered,
            x,
        )

    return lax.fori_loop(
        1, lax.axis_size(axis), lambda source, state: join(state, take(source)), take(0)
    )


def modulate(rows, factors):
    floats = rows.astype(jnp.float32)
    centre = floats - jnp.mean(floats, axis=-1, keepdims=True)
    spread = jnp.mean(centre * centre, axis=-1, keepdims=True)
    normed = centre / jnp.sqrt(spread + EPS_NORM)
    wide = factors.astype(jnp.float32)
    return (normed * (1.0 + wide[1]) + wide[0]).astype(jnp.bfloat16)


def head_norm(vectors, channel_gain):
    inverse = lax.rsqrt(jnp.mean(vectors * vectors, axis=-1, keepdims=True) + EPS_NORM)
    return (vectors * inverse * channel_gain).astype(jnp.bfloat16)


def project_rows(modded, weights, gains):
    mixture = jnp.einsum("td,dch->tch", modded, weights, preferred_element_type=jnp.float32)
    row_count, col_count = (mixture.shape[0], mixture.shape[2])
    per_head = mixture.reshape(row_count, 3, col_count // HD, HD)
    query_rows = head_norm(per_head[:, 0], gains[0]).reshape(row_count, col_count)
    key_rows = head_norm(per_head[:, 1], gains[1]).reshape(row_count, col_count)
    value_rows = per_head[:, 2].astype(jnp.bfloat16).reshape(row_count, col_count)
    return jnp.stack([query_rows, key_rows, value_rows], axis=1)


def block_scores(query_rows, key_rows):
    heads_here = query_rows.shape[1] // HD
    return jnp.einsum(
        "qhd,khd->hqk",
        query_rows.reshape(-1, heads_here, HD),
        key_rows.reshape(-1, heads_here, HD),
        preferred_element_type=jnp.float32,
    ) * HD ** (-0.5)


def weighted(weights, value_rows):
    heads_here = weights.shape[0]
    return jnp.einsum(
        "hqk,khd->hqd",
        weights.astype(jnp.bfloat16),
        value_rows.reshape(-1, heads_here, HD),
        preferred_element_type=jnp.float32,
    )


def opening(query_rows, key_rows, value_rows):
    scores = block_scores(query_rows, key_rows)
    highest = jnp.max(scores, axis=-1)
    weights = jnp.exp(scores - highest[..., None])
    return (highest, jnp.sum(weights, axis=-1), weighted(weights, value_rows))


def absorb(softmax_state, query_rows, key_rows, value_rows):
    highest, totals, weighted_sums = softmax_state
    scores = block_scores(query_rows, key_rows)
    raised = jnp.maximum(highest, jnp.max(scores, axis=-1))
    shrink = jnp.exp(highest - raised)
    weights = jnp.exp(scores - raised[..., None])
    return (
        raised,
        totals * shrink + jnp.sum(weights, axis=-1),
        weighted_sums * shrink[..., None] + weighted(weights, value_rows),
    )


def combine_states(earlier_state, later_state):
    raised = jnp.maximum(earlier_state[0], later_state[0])
    left_scale = jnp.exp(earlier_state[0] - raised)
    right_scale = jnp.exp(later_state[0] - raised)
    totals = earlier_state[1] * left_scale + later_state[1] * right_scale
    weighted_sums = (
        earlier_state[2] * left_scale[..., None] + later_state[2] * right_scale[..., None]
    )
    return (raised, totals, weighted_sums)


def finalize(softmax_state):
    result = softmax_state[2] / softmax_state[1][..., None]
    return jnp.transpose(result, (1, 0, 2)).reshape(result.shape[1], -1).astype(jnp.bfloat16)


def joint_attention(softmax_state, query_rows, pairs):

    def one_step(turn_index, carried):
        inner_state, current = carried
        arriving = from_behind(current, "blk", 1)
        return (absorb(inner_state, query_rows, current[:, 0], current[:, 1]), arriving)

    inner_state, current = lax.fori_loop(
        0, lax.axis_size("blk") - 1, one_step, (softmax_state, pairs)
    )
    return absorb(inner_state, query_rows, current[:, 0], current[:, 1])


def local(
    video_tokens,
    text_tokens,
    video_modulation,
    text_modulation,
    video_projection,
    text_projection,
    video_output,
    text_output,
    video_gains,
    text_gains,
):
    video_proj = project_rows(
        lax.all_gather(modulate(video_tokens, video_modulation), "uly", axis=0, tiled=True),
        video_projection,
        video_gains,
    )
    text_proj = project_rows(
        lax.all_gather(modulate(text_tokens, text_modulation), "uly", axis=0, tiled=True),
        text_projection,
        text_gains,
    )
    video_pairs = video_proj[:, 1:]
    video_state = opening(video_proj[:, 0], text_proj[:, 1], text_proj[:, 2])
    video_heads = finalize(joint_attention(video_state, video_proj[:, 0], video_pairs))
    text_state = opening(text_proj[:, 0], video_proj[:, 1], video_proj[:, 2])
    text_state = combined_all(text_state, "blk", combine_states)
    text_heads = finalize(absorb(text_state, text_proj[:, 0], text_proj[:, 1], text_proj[:, 2]))
    video_summed = lax.psum_scatter(
        jnp.dot(video_heads, video_output, preferred_element_type=jnp.float32).astype(jnp.bfloat16),
        "uly",
        scatter_dimension=0,
        tiled=True,
    ).astype(jnp.float32)
    text_summed = lax.psum_scatter(
        jnp.dot(text_heads, text_output, preferred_element_type=jnp.float32).astype(jnp.bfloat16),
        "uly",
        scatter_dimension=0,
        tiled=True,
    ).astype(jnp.float32)
    video_attention = (video_summed * video_modulation[2].astype(jnp.float32)).astype(jnp.bfloat16)
    text_attention = (text_summed * text_modulation[2].astype(jnp.float32)).astype(jnp.bfloat16)
    return (video_attention, text_attention)


def solution(mesh):
    placed = (
        P(("blk", "uly"), None),
        P("uly", None),
        P(),
        P(),
        P(None, None, "uly"),
        P(None, None, "uly"),
        P("uly", None),
        P("uly", None),
        P(),
        P(),
    )
    return jax.shard_map(
        local,
        mesh=mesh,
        in_specs=placed,
        out_specs=(P(("blk", "uly"), None), P("uly", None)),
        check_vma=False,
    )
```

profile of v0, /device:TPU:0, one launch (start us, length us, event | category | flops | bytes accessed | tf_op | source)
XLA Modules:
  0.0 294.5 jit_solution(13296669816412640557)
XLA Ops:
  10.0 1.2 fusion.33
  11.1 1.8 fusion.36
  14.5 1.1 convert_reduce_fusion
  17.9 42.0 %all-gather.10.cloned.1.call-done = bf16[256,3072]{1,0:T(8,128)(2,1)} async-done(((bf16[32,3072]{1,0:T(8,128)(2,1)}), bf16[256,3072]{1,0:T(8,128)(2,1)}) %all-gather.10.cloned.1.call-update) | async-done | bytes 1572880 | tf_op jit(solution)/shard_map/all_gather | solution.py:148
  59.9 4.8 %fusion.9 = f32[256,3,256]{0,2,1:T(8,128)S(1)} fusion(bf16[3072,3,256]{2,0,1:T(8,128)(2,1)} %param.19, bf16[256,3072]{1,0:T(8,128)(2,1)} %all-gather.10.cloned.1.call-done), kind=kOutput, calls=%fused_computation.21 | convolution fusion | flops 1207959552 | bytes 7077888 | tf_op jit(solution)/shard_map/td,dch->tch/dot_general | solution.py:52
  66.1 1.7 fusion.81
  67.9 45.8 %all-gather.8.cloned.1.call-done = bf16[384,3072]{1,0:T(8,128)(2,1)} async-done(((bf16[48,3072]{1,0:T(8,128)(2,1)}), bf16[384,3072]{1,0:T(8,128)(2,1)}) %all-gather.8.cloned.1.call-update) | async-done | bytes 2359312 | tf_op jit(solution)/shard_map/all_gather | solution.py:143
  113.6 5.3 %fusion.7 = f32[384,3,256]{0,2,1:T(8,128)S(1)} fusion(bf16[3072,3,256]{2,0,1:T(8,128)(2,1)} %param.18, bf16[384,3072]{1,0:T(8,128)(2,1)} %all-gather.8.cloned.1.call-done), kind=kOutput, calls=%fused_computation.19 | convolution fusion | flops 1811939328 | bytes 8257536 | tf_op jit(solution)/shard_map/td,dch->tch/dot_general | solution.py:52
  124.2 5.1 %all-gather.3 = bf16[4,2,256]{2,1,0:T(2,128)(2,1)S(1)} all-gather(bf16[1,2,256]{2,1,0:T(2,128)(2,1)S(1)} %copy-done.12), channel_id=2, replica_groups=mesh['blk'=4,'uly'=8] {'blk'}, dimensions={0}, use_global_device_ids=true | all-gather | bytes 5120 | tf_op jit(solution)/shard_map/all_gather | solution.py:20
  129.9 5.1 %all-gather.4 = bf16[4,2,256]{2,1,0:T(2,128)(2,1)S(1)} all-gather(bf16[1,2,256]{2,1,0:T(2,128)(2,1)S(1)} %bitcast.177), channel_id=3, replica_groups=mesh['blk'=4,'uly'=8] {'blk'}, dimensions={0}, use_global_device_ids=true | all-gather | bytes 5120 | tf_op jit(solution)/shard_map/all_gather | solution.py:20
  134.9 7.3 %all-gather.2 = bf16[8,256,128]{2,1,0:T(8,128)(2,1)S(1)} all-gather(bf16[2,256,128]{2,1,0:T(8,128)(2,1)S(1)} %copy-done.4), channel_id=4, replica_groups=mesh['blk'=4,'uly'=8] {'blk'}, dimensions={0}, use_global_device_ids=true | all-gather | bytes 655360 | tf_op jit(solution)/shard_map/all_gather | solution.py:20
  142.2 3.0 %while.36 = (s32[]{:T(128)}, f32[2,256]{1,0:T(2,128)S(1)}, f32[2,256]{1,0:T(2,128)S(1)}, f32[2,256,128]{2,1,0:T(8,128)S(1)}, bf16[4,2,256]{2,1,0:T(2,128)(2,1)},...) while((s32[]{:T(128)}, f32[2,256]{1,0:T(2,128)S(1)}, ...), condition=%wide.region_20.21_spmd, body=%wide.region_19.20_spmd.sunk | while | flops 266245 | bytes 673943 | solution.py:32
  146.2 1.1 fusion.31
  147.3 1.3 fusion.14
  148.7 1.8 convolution_convert_fusion.1
  151.3 21.9 %while.35 = (s32[]{:T(128)}, f32[2,384]{1,0:T(2,128)S(1)}, f32[2,384]{1,0:T(2,128)S(1)}, f32[2,384,128]{2,1,0:T(8,128)S(1)}, bf16[384,2,256]{0,2,1:T(8,128)(2,1)...) while((s32[]{:T(128)}, f32[2,384]{1,0:T(2,128)S(1)}, f32[2,384]{1,0:T(2,128)S(1)}, ...), condition=%wide.region_12.13_spmd, body=%wide.region_9.12_spmd.sunk | while | flops 152962560 | bytes 8110197 | solution.py:124
  152.9 5.7 %collective-permute-done = bf16[384,2,256]{0,2,1:T(8,128)(2,1)S(1)} collective-permute-done((bf16[384,2,256]{0,2,1:T(8,128)(2,1)S(1)}, bf16[384,2,256]{0,2,1:T(8,128)(2,1)S(1)}, u32[]{:S(2)}, u32[]{:S(2)}) %collective-permute-start) | collective-permute-done | bytes 393248 | tf_op jit(solution)/shard_map/while/body/eval_jaxpr/ppermute | solution.py:15
  159.9 6.0 %collective-permute-done = bf16[384,2,256]{0,2,1:T(8,128)(2,1)S(1)} collective-permute-done((bf16[384,2,256]{0,2,1:T(8,128)(2,1)S(1)}, bf16[384,2,256]{0,2,1:T(8,128)(2,1)S(1)}, u32[]{:S(2)}, u32[]{:S(2)}) %collective-permute-start) | collective-permute-done | bytes 393248 | tf_op jit(solution)/shard_map/while/body/eval_jaxpr/ppermute | solution.py:15
  167.2 6.0 %collective-permute-done = bf16[384,2,256]{0,2,1:T(8,128)(2,1)S(1)} collective-permute-done((bf16[384,2,256]{0,2,1:T(8,128)(2,1)S(1)}, bf16[384,2,256]{0,2,1:T(8,128)(2,1)S(1)}, u32[]{:S(2)}, u32[]{:S(2)}) %collective-permute-start) | collective-permute-done | bytes 393248 | tf_op jit(solution)/shard_map/while/body/eval_jaxpr/ppermute | solution.py:15
  174.4 2.2 convolution_convert_fusion
  177.4 36.8 %reduce-scatter.5.cloned.1.call-done = bf16[32,3072]{1,0:T(8,128)(2,1)} async-done(((bf16[256,3072]{1,0:T(8,128)(2,1)}), bf16[32,3072]{1,0:T(8,128)(2,1)}) %reduce-scatter.5.cloned.1.call-update) | async-done | bytes 196624 | tf_op jit(solution)/shard_map/reduce_scatter | solution.py:164
  214.2 1.6 multiply_convert_fusion.1
  215.8 70.4 %reduce-scatter.3.cloned.1.call-done = bf16[48,3072]{1,0:T(8,128)(2,1)} async-done(((bf16[384,3072]{1,0:T(8,128)(2,1)}), bf16[48,3072]{1,0:T(8,128)(2,1)}) %reduce-scatter.3.cloned.1.call-update) | async-done | bytes 294928 | tf_op jit(solution)/shard_map/reduce_scatter | solution.py:158
  286.2 1.7 multiply_convert_fusion
  (134 shorter events, 24.4 us)
Async XLA Ops:
  7.2 167.2 %copy-start = (bf16[256,3072]{1,0:T(8,128)(2,1)S(1)}, bf16[256,3072]{1,0:T(8,128)(2,1)}, u32[]{:S(2)}) copy-start(bf16[256,3072]{1,0:T(8,128)(2,1)} %param.20) | copy-start | bytes 4718596
  7.2 8.4 %copy-start.1 = (bf16[48,3072]{1,0:T(8,128)(2,1)S(1)}, bf16[48,3072]{1,0:T(8,128)(2,1)}, u32[]{:S(2)}) copy-start(bf16[48,3072]{1,0:T(8,128)(2,1)} %param.14) | copy-start | bytes 884740
  7.2 9.6 %copy-start.15 = (f32[2,128]{1,0:T(2,128)S(1)}, f32[2,128]{1,0:T(2,128)}, u32[]{:S(2)}) copy-start(f32[2,128]{1,0:T(2,128)} %param.23) | copy-start | bytes 3076
  7.2 9.6 %copy-start.16 = (f32[2,128]{1,0:T(2,128)S(1)}, f32[2,128]{1,0:T(2,128)}, u32[]{:S(2)}) copy-start(f32[2,128]{1,0:T(2,128)} %param.22) | copy-start | bytes 3076
  7.2 52.7 %all-gather.10.cloned.1.call-start = ((), (), s32[]{:S(2)}) async-start(), calls=%async_computation.3 | async-start | bytes 1769472 | tf_op jit(solution)/shard_map/all_gather | solution.py:148
  12.9 100.7 %all-gather.8.cloned.1.call-start = ((), (), s32[]{:S(2)}) async-start(), calls=%async_computation.2 | async-start | bytes 2654208 | tf_op jit(solution)/shard_map/all_gather | solution.py:143
  16.8 197.4 %reduce-scatter.5.cloned.1.call-start = ((), (), s32[]{:S(2)}) async-start(), calls=%async_computation.5 | async-start | bytes 1769472 | tf_op jit(solution)/shard_map/reduce_scatter | solution.py:164
  120.4 2.4 copy-start.8
  120.9 1.9 copy-start.3
  120.9 2.3 copy-start.13
  123.0 0.9 copy-start.5
  123.4 0.8 copy-start.12
  123.4 11.6 %copy-start.4 = (bf16[2,256,128]{2,1,0:T(8,128)(2,1)S(1)}, bf16[2,256,128]{2,1,0:T(8,128)(2,1)}, u32[]{:S(2)}) copy-start(bf16[2,256,128]{2,1,0:T(8,128)(2,1)} %convolution_convert_fusion.2) | copy-start | bytes 393220
  129.3 0.6 copy-start.10
  134.9 7.3 %copy-start.11 = (bf16[4,2,256]{2,1,0:T(2,128)(2,1)}, bf16[4,2,256]{2,1,0:T(2,128)(2,1)S(1)}, u32[]{:S(2)}) copy-start(bf16[4,2,256]{2,1,0:T(2,128)(2,1)S(1)} %all-gather.4) | copy-start | bytes 12292
  145.4 3.3 %copy-start.2 = (bf16[256,3072]{1,0:T(8,128)(2,1)S(1)}, bf16[256,3072]{1,0:T(8,128)(2,1)}, u32[]{:S(2)}) copy-start(bf16[256,3072]{1,0:T(8,128)(2,1)} %param.21) | copy-start | bytes 4718596
  150.4 0.7 copy-start.9
  150.4 0.7 copy-start.14
  150.5 135.8 %reduce-scatter.3.cloned.1.call-start = ((), (), s32[]{:S(2)}) async-start(), calls=%async_computation.4 | async-start | bytes 2654208 | tf_op jit(solution)/shard_map/reduce_scatter | solution.py:158
  151.4 7.3 %collective-permute-start = (bf16[384,2,256]{0,2,1:T(8,128)(2,1)S(1)}, bf16[384,2,256]{0,2,1:T(8,128)(2,1)S(1)}, u32[]{:S(2)}, u32[]{:S(2)}) collective-permute-start(bf16[384,2,256]{0,2,1:T(8,128)(2,1)S(1)} %copy.98), channel_id=1, source_target_pairs={{24,0},{0,8},{8,16},{16,24},{25,1},{1,9},{9,17},{17,25},{26,2},{2,... | collective-permute-start | bytes 1179656 | tf_op jit(solution)/shard_map/while/body/eval_jaxpr/ppermute | solution.py:15
  158.7 7.3 %collective-permute-start = (bf16[384,2,256]{0,2,1:T(8,128)(2,1)S(1)}, bf16[384,2,256]{0,2,1:T(8,128)(2,1)S(1)}, u32[]{:S(2)}, u32[]{:S(2)}) collective-permute-start(bf16[384,2,256]{0,2,1:T(8,128)(2,1)S(1)} %copy.98), channel_id=1, source_target_pairs={{24,0},{0,8},{8,16},{16,24},{25,1},{1,9},{9,17},{17,25},{26,2},{2,... | collective-permute-start | bytes 1179656 | tf_op jit(solution)/shard_map/while/body/eval_jaxpr/ppermute | solution.py:15
  166.0 7.3 %collective-permute-start = (bf16[384,2,256]{0,2,1:T(8,128)(2,1)S(1)}, bf16[384,2,256]{0,2,1:T(8,128)(2,1)S(1)}, u32[]{:S(2)}, u32[]{:S(2)}) collective-permute-start(bf16[384,2,256]{0,2,1:T(8,128)(2,1)S(1)} %copy.98), channel_id=1, source_target_pairs={{24,0},{0,8},{8,16},{16,24},{25,1},{1,9},{9,17},{17,25},{26,2},{2,... | collective-permute-start | bytes 1179656 | tf_op jit(solution)/shard_map/while/body/eval_jaxpr/ppermute | solution.py:15
  176.6 0.7 copy-start.6
  176.6 0.8 copy-start.7
Sparse Core Ops, SparseCore 0:
  13.0 46.8 all-gather.9
  62.7 50.8 all-gather.7
  150.6 63.5 reduce-scatter.4
  217.9 68.2 reduce-scatter.2
where the time goes:
time: 295 us; the launch traced here: 294 us
  waiting for transfers between devices  213 us (72%)
  matrix products  22.6 us (8%)
  other arithmetic  18.9 us (6%)
  blocking collectives  17.4 us (6%)
  between operations  14.2 us (5%)
  local copies, waits for them, and re-layouts  7.65 us (3%)
    reduce_scatter x1, waiting for transfers between devices, local(): lax.psum_scatter(jnp.dot(video_heads, video_output, preferred_element_typ...  70.4 us
    all_gather x1, waiting for transfers between devices, local(): lax.all_gather(modulate(video_tokens, video_modulation), 'uly', axis=0, t...  45.8 us
    all_gather x1, waiting for transfers between devices, local(): lax.all_gather(modulate(text_tokens, text_modulation), 'uly', axis=0, til...  42 us
    reduce_scatter x1, waiting for transfers between devices, local(): lax.psum_scatter(jnp.dot(text_heads, text_output, preferred_element_type=...  36.8 us
    ppermute x3, waiting for transfers between devices, from_behind(): return lax.ppermute(block, axis, route)  17.7 us
    all_gather x3, blocking collectives, combined_all(): lax.all_gather(a.astype(kind), axis)  17.4 us
    dot_general x2, matrix products, project_rows(): jnp.einsum('td,dch->tch', modded, weights, preferred_element_type=jnp.flo...  10 us
  transfers between devices with their start and end apart: 7, of which 7 were waited for; matrix products, arithmetic and copies ran while one was open for 7% of the time, Pallas kernels for 0%

commit v1 on v0

v1 whole, which is shorter than its diff:
```python
import functools
import math

import jax
import jax.numpy as jnp
from jax import lax
from jax.experimental import pallas as pl
from jax.experimental.pallas import tpu as pltpu
from jax.sharding import PartitionSpec as P

HD = 128
EPS_NORM = 1e-06
F32 = jnp.float32
BF16 = jnp.bfloat16
VMEM = pl.BlockSpec(memory_space=pltpu.VMEM)
SMEM = pl.BlockSpec(memory_space=pltpu.SMEM)


def call(kernel, outs, args, vmem_mib, scratch=(), flops=0, smem=()):
    moved = sum(a.size * a.dtype.itemsize for a in args)
    return pl.pallas_call(
        kernel,
        out_shape=outs,
        in_specs=[SMEM if i in smem else VMEM for i in range(len(args))],
        out_specs=jax.tree.map(lambda _: VMEM, outs),
        scratch_shapes=list(scratch),
        compiler_params=pltpu.CompilerParams(vmem_limit_bytes=vmem_mib << 20),
        cost_estimate=pl.CostEstimate(flops=flops, bytes_accessed=moved, transcendentals=0),
    )(*args)


def ring_routes(axis):
    n = lax.axis_size(axis)
    order = list(range(0, n, 2)) + list(range(1, n, 2))[::-1]
    ahead = [(order[i], order[(i + 1) % n]) for i in range(n)]
    return ahead, [(b, a) for a, b in ahead]


def across(block, distance):
    n = lax.axis_size("blk")
    return lax.ppermute(block, "blk", [(i, i ^ distance) for i in range(n)])


def modulated(rows, factors):
    floats = rows.astype(F32)
    centre = floats - jnp.mean(floats, axis=-1, keepdims=True)
    spread = jnp.mean(centre * centre, axis=-1, keepdims=True)
    wide = factors.astype(F32)
    normed = centre / jnp.sqrt(spread + EPS_NORM)
    return normed * (1.0 + wide[1:2]) + wide[0:1]


def modulate_kernel(part_ref, video_ref, text_ref, vmod_ref, tmod_ref, left_ref, right_ref, text_f32):
    text_rows = left_ref.shape[0] - video_ref.shape[0]
    half = left_ref.shape[1]
    text_f32[...] = text_ref[...].astype(F32)
    start = pl.multiple_of(part_ref[0] * text_rows, text_rows)
    own_text = text_f32[pl.ds(start, text_rows), :]
    video = modulated(video_ref[...], vmod_ref[...])
    text = modulated(own_text, tmod_ref[...])
    both = jnp.concatenate([video, text], axis=0).astype(BF16)
    left_ref[...] = both[:, :half]
    right_ref[...] = both[:, half:]


def head_normed(mixture, gain):
    heads = []
    for h in range(mixture.shape[1] // HD):
        vectors = mixture[:, h * HD : (h + 1) * HD]
        inverse = lax.rsqrt(jnp.mean(vectors * vectors, axis=-1, keepdims=True) + EPS_NORM)
        heads.append(vectors * inverse * gain)
    return jnp.concatenate(heads, axis=1)


def project_kernel(shards, video_rows, *refs):
    chunks = refs[: 2 * shards]
    wv_ref, wt_ref, vgain_ref, tgain_ref, q_ref, kv_ref = refs[2 * shards :]
    width = q_ref.shape[1]
    video, text = [], []
    for side in range(2):
        floats = [chunks[2 * i + side][...].astype(F32) for i in range(shards)]
        video.append(jnp.concatenate([f[:video_rows] for f in floats], axis=0).astype(BF16))
        text.append(jnp.concatenate([f[video_rows:] for f in floats], axis=0).astype(BF16))
    half = video[0].shape[1]

    def mixed(sides, w_ref, j):
        total = jnp.dot(sides[0], w_ref[j, :half, :], preferred_element_type=F32)
        return total + jnp.dot(sides[1], w_ref[j, half:, :], preferred_element_type=F32)

    def joined(j, norm):
        v = mixed(video, wv_ref, j)
        t = mixed(text, wt_ref, j)
        if norm:
            v = head_normed(v, vgain_ref[j : j + 1, :])
            t = head_normed(t, tgain_ref[j : j + 1, :])
        return jnp.concatenate([v, t], axis=0).astype(BF16)

    q_ref[...] = joined(0, True)
    kv_ref[:, :width] = joined(1, True)
    kv_ref[:, width:] = joined(2, False)


def attend_kernel(sizes, video_rows, parts, sources, *refs):
    groups = len(sizes)
    queries = [r[...].astype(F32) for r in refs[:groups]]
    pieces = refs[groups : groups + groups * sources]
    wv_ref, wt_ref = refs[groups + groups * sources : groups + groups * sources + 2]
    outs = refs[groups + groups * sources + 2 :]
    query = jnp.concatenate(queries, axis=0).astype(BF16)
    width = query.shape[1]
    heads = width // HD
    factor = HD ** (-0.5) * math.log2(math.e)
    state = [None] * heads
    for s in range(sources):
        for g in range(groups):
            piece = pieces[s * groups + g]
            rows = piece.shape[0] if s < parts else sizes[g] * video_rows
            for h in range(heads):
                keys = piece[:rows, h * HD : (h + 1) * HD]
                values = piece[:rows, width + h * HD : width + (h + 1) * HD]
                scores = lax.dot_general(
                    keys,
                    query[:, h * HD : (h + 1) * HD],
                    (((1,), (1,)), ((), ())),
                    preferred_element_type=F32,
                )
                highest = jnp.max(scores, axis=0, keepdims=True)
                if state[h] is not None:
                    before, totals, sums = state[h]
                    highest = jnp.maximum(before, highest)
                weights = jnp.exp2((scores - highest) * factor)
                total = jnp.sum(weights, axis=0, keepdims=True)
                mixed = lax.dot_general(
                    values,
                    weights.astype(BF16),
                    (((0,), (0,)), ((), ())),
                    preferred_element_type=F32,
                )
                if state[h] is not None:
                    shrink = jnp.exp2((before - highest) * factor)
                    total = totals * shrink + total
                    mixed = sums * shrink + mixed
                state[h] = (highest, total, mixed)
    flat = jnp.concatenate([sums / totals for _, totals, sums in state], axis=0)
    rows_out = jnp.transpose(flat)
    text_rows = outs[0].shape[0] - video_rows
    video, text = [], []
    start = 0
    for size in sizes:
        video.append(rows_out[start : start + size * video_rows])
        start += size * video_rows
        text.append(rows_out[start : start + size * text_rows])
        start += size * text_rows
    video = jnp.concatenate(video, axis=0).astype(BF16)
    text = jnp.concatenate(text, axis=0).astype(BF16)
    half = outs[0].shape[1]
    for side in range(2):
        columns = slice(side * half, (side + 1) * half)
        yv = jnp.dot(video, wv_ref[:, columns], preferred_element_type=F32)
        yt = jnp.dot(text, wt_ref[:, columns], preferred_element_type=F32)
        for i in range(len(outs) // 2):
            part = [yv[i * video_rows : (i + 1) * video_rows], yt[i * text_rows : (i + 1) * text_rows]]
            outs[2 * i + side][...] = jnp.concatenate(part, axis=0).astype(BF16)


def close_kernel(a0, a1, a2, b0, b1, b2, vmod_ref, tmod_ref, video_ref, text_ref):
    video_rows = video_ref.shape[0]
    half = a0.shape[1]
    for side, refs in enumerate(((a0, a1, a2), (b0, b1, b2))):
        columns = slice(side * half, (side + 1) * half)
        total = refs[0][...].astype(F32) + refs[1][...].astype(F32) + refs[2][...].astype(F32)
        vgate = vmod_ref[2:3, columns].astype(F32)
        tgate = tmod_ref[2:3, columns].astype(F32)
        video_ref[:, columns] = (total[:video_rows] * vgate).astype(BF16)
        text_ref[:, columns] = (total[video_rows:] * tgate).astype(BF16)


def place_kernel(part_ref, *refs):
    pieces, out_ref, wide = refs[:-2], refs[-2], refs[-1]
    rows = pieces[0].shape[0]
    for d, piece in enumerate(pieces):
        start = pl.multiple_of((part_ref[0] ^ d) * rows, rows)
        wide[pl.ds(start, rows), :] = piece[...].astype(F32)
    out_ref[...] = wide[...].astype(BF16)


def local(
    video_tokens,
    text_tokens,
    video_modulation,
    text_modulation,
    video_projection,
    text_projection,
    video_output,
    text_output,
    video_gains,
    text_gains,
):
    n_blk, n_uly = lax.axis_size("blk"), lax.axis_size("uly")
    reach = n_uly // 2
    ahead, back = ring_routes("uly")
    video_rows, width = video_tokens.shape
    half = width // 2
    parts = math.gcd(n_blk, text_tokens.shape[0] // 8)
    text_rows = text_tokens.shape[0] // parts
    shard_rows = video_rows + text_rows
    cols = video_output.shape[0]
    part = lax.rem(lax.axis_index("blk"), parts).reshape(1).astype(jnp.int32)

    chunk = jax.ShapeDtypeStruct((shard_rows, half), BF16)
    own = call(
        modulate_kernel,
        [chunk, chunk],
        (part, video_tokens, text_tokens, video_modulation, text_modulation),
        8,
        [pltpu.VMEM(text_tokens.shape, F32)],
        smem=(0,),
    )

    fa, fb = own
    ba, bb = own
    arrived = []
    for step in range(1, reach + 1):
        fa = lax.ppermute(fa, "uly", ahead)
        bb = lax.ppermute(bb, "uly", back)
        if step < reach:
            fb = lax.ppermute(fb, "uly", ahead)
            ba = lax.ppermute(ba, "uly", back)
            arrived.append([(-step, fa, fb), (step, ba, bb)])
        else:
            arrived.append([(reach, fa, bb)])
    groups = [[(0, *own)]]
    for step in range(reach - 2):
        groups[0] += arrived[step]
    groups += arrived[reach - 2 :]

    wv = jnp.transpose(video_projection, (1, 0, 2))
    wt = jnp.transpose(text_projection, (1, 0, 2))
    queries, pieces = [], []
    for group in groups:
        rows = len(group) * shard_rows
        q, kv = call(
            functools.partial(project_kernel, len(group), video_rows),
            [
                jax.ShapeDtypeStruct((rows, cols), BF16),
                jax.ShapeDtypeStruct((rows, 2 * cols), BF16),
            ],
            [c for _, *pair in group for c in pair] + [wv, wt, video_gains, text_gains],
            32,
            flops=2 * rows * width * 3 * cols,
        )
        queries.append(q)
        pieces.append([kv] + [across(kv, d) for d in range(1, n_blk)])

    slots = [r for group in groups for r, *_ in group]
    partial = call(
        functools.partial(attend_kernel, [len(g) for g in groups], video_rows, parts, n_blk),
        [chunk] * (2 * n_uly),
        queries
        + [pieces[g][d] for d in range(n_blk) for g in range(len(groups))]
        + [video_output, text_output],
        48,
        flops=4 * (shard_rows * n_uly) ** 2 * n_blk * cols,
    )
    mine = {r: (partial[2 * i], partial[2 * i + 1]) for i, r in enumerate(slots)}
    mine[-reach] = mine[reach]

    def joined(arriving, own_part):
        return (arriving.astype(F32) + own_part.astype(F32)).astype(BF16)

    fa, bb = mine[reach][0], mine[-reach][1]
    fb, ba = mine[reach - 1][1], mine[1 - reach][0]
    for left in range(reach - 1, -1, -1):
        fa = lax.ppermute(fa, "uly", ahead)
        bb = lax.ppermute(bb, "uly", back)
        if left:
            fa = joined(fa, mine[left][0])
            bb = joined(bb, mine[-left][1])
            fb = lax.ppermute(fb, "uly", ahead)
            ba = lax.ppermute(ba, "uly", back)
            if left > 1:
                fb = joined(fb, mine[left - 1][1])
                ba = joined(ba, mine[1 - left][0])
    video_attention, text_part = call(
        close_kernel,
        [
            jax.ShapeDtypeStruct(video_tokens.shape, BF16),
            jax.ShapeDtypeStruct((text_rows, width), BF16),
        ],
        (fa, ba, mine[0][0], fb, bb, mine[0][1], video_modulation, text_modulation),
        8,
    )
    text_attention = call(
        place_kernel,
        jax.ShapeDtypeStruct(text_tokens.shape, BF16),
        [part, text_part] + [across(text_part, d) for d in range(1, parts)],
        8,
        [pltpu.VMEM(text_tokens.shape, F32)],
        smem=(0,),
    )
    return (video_attention, text_attention)


def solution(mesh):
    placed = (
        P(("blk", "uly"), None),
        P("uly", None),
        P(),
        P(),
        P(None, None, "uly"),
        P(None, None, "uly"),
        P("uly", None),
        P("uly", None),
        P(),
        P(),
    )
    return jax.shard_map(
        local,
        mesh=mesh,
        in_specs=placed,
        out_specs=(P(("blk", "uly"), None), P("uly", None)),
        check_vma=False,
    )
```

time: 295 us -> 104 us (0.35)
  waiting for transfers between devices: 213 us -> 38.2 us
  starting transfers between devices: 0.86 us -> 39.1 us
  matrix products: 22.6 us -> 0 us
  other arithmetic: 18.9 us -> 0.42 us
  blocking collectives: 17.4 us -> 0 us
  Pallas kernels: 0 us -> 16.2 us
  between operations: 14.2 us -> 0.81 us
    reduce_scatter x2 -> x0, waiting for transfers between devices: 107 us -> none  [the longest x1 70.4 us: local(): lax.psum_scatter(jnp.dot(video_heads, video_output, preferred_element_typ...]
    all_gather x2 -> x0, waiting for transfers between devices: 87.8 us -> none  [the longest x1 45.8 us: local(): lax.all_gather(modulate(video_tokens, video_modulation), 'uly', axis=0, t...]
    ppermute x3 -> x40, starting transfers between devices: 0.51 us -> 39.1 us  [the longest x8 10.3 us: local(): fa = lax.ppermute(fa, 'uly', ahead)]
    dot_general x18 -> x0, matrix products: 22.6 us -> none  [the longest x2 10 us: project_rows(): jnp.einsum('td,dch->tch', modded, weights, preferred_element_type=jnp.flo...]
    ppermute x3 -> x40, waiting for transfers between devices: 17.7 us -> 38.2 us  [the longest x12 13.7 us: across(): return lax.ppermute(block, 'blk', [(i, i ^ distance) for i in range(n)])]
    all_gather x3 -> x0, blocking collectives: 17.4 us -> none  [combined_all(): lax.all_gather(a.astype(kind), axis)]
    pallas_call x0 -> x7, Pallas kernels: none -> 16.2 us  [call(): pl.pallas_call(kernel, out_shape=outs, in_specs=[SMEM if i in smem else V...]
    convert_element_type x11 -> x10, other arithmetic: 7.81 us -> 0.42 us  [joined(): return (arriving.astype(F32) + own_part.astype(F32)).astype(BF16)]
  transfers between devices with their start and end apart: 7 -> 40, of which waited for: 7 -> 21; matrix products, arithmetic and copies ran while one was open for 7% -> 0% of each run, Pallas kernels for 0% -> 5%
where the time goes in v1:
time: 104 us
  starting transfers between devices  39.1 us (38%)
  waiting for transfers between devices  38.2 us (37%)
  Pallas kernels  16.2 us (16%)
  local copies, waits for them, and re-layouts  9.4 us (9%)
    pallas_call x7, Pallas kernels, call(): pl.pallas_call(kernel, out_shape=outs, in_specs=[SMEM if i in smem else V...  16.2 us
    ppermute x12, waiting for transfers between devices, across(): return lax.ppermute(block, 'blk', [(i, i ^ distance) for i in range(n)])  13.7 us
    ppermute x8, starting transfers between devices, local(): fa = lax.ppermute(fa, 'uly', ahead)  10.3 us
    unnamed x24, local copies, waits for them, and re-layouts  9.4 us
    ppermute x8, waiting for transfers between devices, local(): bb = lax.ppermute(bb, 'uly', back)  8.84 us
    ppermute x12, starting transfers between devices, across(): return lax.ppermute(block, 'blk', [(i, i ^ distance) for i in range(n)])  8.4 us
    ppermute x8, waiting for transfers between devices, local(): fa = lax.ppermute(fa, 'uly', ahead)  7.95 us
    ppermute x6, starting transfers between devices, local(): ba = lax.ppermute(ba, 'uly', back)  7.17 us
  transfers between devices with their start and end apart: 40, of which 21 were waited for; matrix products, arithmetic and copies ran while one was open for 0% of the time, Pallas kernels for 5%

profile of v1, /device:TPU:0, one launch (start us, length us, event | category | flops | bytes accessed | tf_op | source)
XLA Modules:
  0.0 104.0 jit_solution(10013194452959945058)
XLA Ops:
  4.4 3.0 %collective-permute-start.2 = (bf16[56,1536]{1,0:T(8,128)(2,1)S(1)}, bf16[56,1536]{1,0:T(8,128)(2,1)S(1)}, u32[]{:S(2)}, u32[]{:S(2)}) collective-permute-start(bf16[56,1536]{1,0:T(8,128)(2,1)S(1)} %get-tuple-element.28.refs_0_), channel_id=1, source_target_pairs={{2,0},{4,2},{6,4},{7,6},{5,7},{3,5},{1,3},{0,1},{10,8},{12,10},{14... | collective-permute-start | bytes 516104 | tf_op jit(solution)/shard_map/ppermute | solution.py:228
  9.6 3.1 %collective-permute-done.2.refs_4_ = bf16[56,1536]{1,0:T(8,128)(2,1)S(1)} collective-permute-done((bf16[56,1536]{1,0:T(8,128)(2,1)S(1)}, bf16[56,1536]{1,0:T(8,128)(2,1)S(1)}, u32[]{:S(2)}, u32[]{:S(2)}) %collective-permute-start.2) | collective-permute-done | bytes 172064 | tf_op jit(solution)/shard_map/ppermute | solution.py:228
  12.7 2.0 %collective-permute-start.6 = (bf16[56,1536]{1,0:T(8,128)(2,1)S(1)}, bf16[56,1536]{1,0:T(8,128)(2,1)S(1)}, u32[]{:S(2)}, u32[]{:S(2)}) collective-permute-start(bf16[56,1536]{1,0:T(8,128)(2,1)S(1)} %collective-permute-done.2.refs_4_), channel_id=1, source_target_pairs={{2,0},{4,2},{6,4},{7,6},{5,7},{3,5},{1,3},{0,1},{10,8},{12,10},{14... | collective-permute-start | bytes 516104 | tf_op jit(solution)/shard_map/ppermute | solution.py:228
  16.4 2.0 %collective-permute-start.7 = (bf16[56,1536]{1,0:T(8,128)(2,1)S(1)}, bf16[56,1536]{1,0:T(8,128)(2,1)S(1)}, u32[]{:S(2)}, u32[]{:S(2)}) collective-permute-start(bf16[56,1536]{1,0:T(8,128)(2,1)S(1)} %collective-permute-done.3.refs_5_), channel_id=1, source_target_pairs={{2,0},{4,2},{6,4},{7,6},{5,7},{3,5},{1,3},{0,1},{10,8},{12,10},{14... | collective-permute-start | bytes 516104 | tf_op jit(solution)/shard_map/ppermute | solution.py:225
  20.0 2.0 %collective-permute-start.10 = (bf16[56,1536]{1,0:T(8,128)(2,1)S(1)}, bf16[56,1536]{1,0:T(8,128)(2,1)S(1)}, u32[]{:S(2)}, u32[]{:S(2)}) collective-permute-start(bf16[56,1536]{1,0:T(8,128)(2,1)S(1)} %collective-permute-done.6.refs_8_), channel_id=1, source_target_pairs={{2,0},{4,2},{6,4},{7,6},{5,7},{3,5},{1,3},{0,1},{10,8},{12,10},{14... | collective-permute-start | bytes 516104 | tf_op jit(solution)/shard_map/ppermute | solution.py:228
  23.7 2.0 %collective-permute-start.11 = (bf16[56,1536]{1,0:T(8,128)(2,1)S(1)}, bf16[56,1536]{1,0:T(8,128)(2,1)S(1)}, u32[]{:S(2)}, u32[]{:S(2)}) collective-permute-start(bf16[56,1536]{1,0:T(8,128)(2,1)S(1)} %collective-permute-done.7.refs_9_), channel_id=1, source_target_pairs={{2,0},{4,2},{6,4},{7,6},{5,7},{3,5},{1,3},{0,1},{10,8},{12,10},{14... | collective-permute-start | bytes 516104 | tf_op jit(solution)/shard_map/ppermute | solution.py:225
  25.9 2.3 %copy-done = bf16[3072,3,256]{2,0,1:T(8,128)(2,1)S(1)} copy-done((bf16[3072,3,256]{2,0,1:T(8,128)(2,1)S(1)}, bf16[3072,3,256]{2,0,1:T(8,128)(2,1)}, u32[]{:S(2)}) %copy-start) | copy-done | bytes 4718616
  28.2 2.3 %copy-done.2 = bf16[3072,3,256]{2,0,1:T(8,128)(2,1)S(1)} copy-done((bf16[3072,3,256]{2,0,1:T(8,128)(2,1)S(1)}, bf16[3072,3,256]{2,0,1:T(8,128)(2,1)}, u32[]{:S(2)}) %copy-start.2) | copy-done | bytes 4718616
  31.9 2.0 %shard_map.114 = (bf16[280,256]{1,0:T(8,128)(2,1)S(1)}, bf16[280,512]{1,0:T(8,128)(2,1)S(1)}) custom-call(bf16[56,1536]{1,0:T(8,128)(2,1)S(1)} %get-tuple-element.28.refs_0_, bf16[56,1536]{1,0:T(8,128)(2,1)S(1)} %get-tuple-element.29.refs_1_, bf16[56,1536]{1,0:T(8,128)(2,1)S(1)} %collective-permute-done.refs_2_, ...), custom_call_target="tpu_custom_call" | custom-call | flops 1321205760 | bytes 11159552 | tf_op jit(solution)/shard_map/pallas_call | solution.py:21
  34.0 2.0 %collective-permute-start.17 = (bf16[280,512]{1,0:T(8,128)(2,1)S(1)}, bf16[280,512]{1,0:T(8,128)(2,1)S(1)}, u32[]{:S(2)}, u32[]{:S(2)}) collective-permute-start(bf16[280,512]{1,0:T(8,128)(2,1)S(1)} %get-tuple-element.33.refs_3_), channel_id=1, source_target_pairs={{0,16},{8,24},{16,0},{24,8},{1,17},{9,25},{17,1},{25,9},{2,18},{10... | collective-permute-start | bytes 860168 | tf_op jit(solution)/shard_map/ppermute | solution.py:41
  39.5 3.2 %collective-permute-done.20.refs_12_ = bf16[280,512]{1,0:T(8,128)(2,1)S(1)} collective-permute-done((bf16[280,512]{1,0:T(8,128)(2,1)S(1)}, bf16[280,512]{1,0:T(8,128)(2,1)S(1)}, u32[]{:S(2)}, u32[]{:S(2)}) %collective-permute-start.20) | collective-permute-done | bytes 286752 | tf_op jit(solution)/shard_map/ppermute | solution.py:41
  42.8 2.5 %collective-permute-start.18 = (bf16[112,512]{1,0:T(8,128)(2,1)S(1)}, bf16[112,512]{1,0:T(8,128)(2,1)S(1)}, u32[]{:S(2)}, u32[]{:S(2)}) collective-permute-start(bf16[112,512]{1,0:T(8,128)(2,1)S(1)} %get-tuple-element.34.refs_4_), channel_id=1, source_target_pairs={{0,16},{8,24},{16,0},{24,8},{1,17},{9,25},{17,1},{25,9},{2,18},{10... | collective-permute-start | bytes 344072 | tf_op jit(solution)/shard_map/ppermute | solution.py:41
  46.9 2.8 %collective-permute-done.17.refs_9_ = bf16[280,512]{1,0:T(8,128)(2,1)S(1)} collective-permute-done((bf16[280,512]{1,0:T(8,128)(2,1)S(1)}, bf16[280,512]{1,0:T(8,128)(2,1)S(1)}, u32[]{:S(2)}, u32[]{:S(2)}) %collective-permute-start.17) | collective-permute-done | bytes 286752 | tf_op jit(solution)/shard_map/ppermute | solution.py:41
  51.9 2.6 %collective-permute-done.18.refs_10_ = bf16[112,512]{1,0:T(8,128)(2,1)S(1)} collective-permute-done((bf16[112,512]{1,0:T(8,128)(2,1)S(1)}, bf16[112,512]{1,0:T(8,128)(2,1)S(1)}, u32[]{:S(2)}, u32[]{:S(2)}) %collective-permute-start.18) | collective-permute-done | bytes 114720 | tf_op jit(solution)/shard_map/ppermute | solution.py:41
  56.6 9.2 %shard_map.117 = (bf16[56,1536]{1,0:T(8,128)(2,1)S(1)}, bf16[56,1536]{1,0:T(8,128)(2,1)S(1)}, bf16[56,1536]{1,0:T(8,128)(2,1)S(1)}, bf16[56,1536]{1,0:T(8,128)(2...) custom-call(bf16[280,256]{1,0:T(8,128)(2,1)S(1)} %get-tuple-element., ...), custom_call_target="tpu_custom_call" | custom-call | flops 822083584 | bytes 5210112 | tf_op jit(solution)/shard_map/pallas_call | solution.py:21
  65.9 2.0 %collective-permute-start.23 = (bf16[56,1536]{1,0:T(8,128)(2,1)S(1)}, bf16[56,1536]{1,0:T(8,128)(2,1)S(1)}, u32[]{:S(2)}, u32[]{:S(2)}) collective-permute-start(bf16[56,1536]{1,0:T(8,128)(2,1)S(1)} %get-tuple-element.36), channel_id=1, source_target_pairs={{0,2},{2,4},{4,6},{6,7},{7,5},{5,3},{3,1},{1,0},{8,10},{10,12},{12... | collective-permute-start | bytes 516104 | tf_op jit(solution)/shard_map/ppermute | solution.py:274
  69.9 3.1 %collective-permute-done.23 = bf16[56,1536]{1,0:T(8,128)(2,1)S(1)} collective-permute-done((bf16[56,1536]{1,0:T(8,128)(2,1)S(1)}, bf16[56,1536]{1,0:T(8,128)(2,1)S(1)}, u32[]{:S(2)}, u32[]{:S(2)}) %collective-permute-start.23) | collective-permute-done | bytes 172064 | tf_op jit(solution)/shard_map/ppermute | solution.py:274
  73.1 2.1 %collective-permute-start.24 = (bf16[56,1536]{1,0:T(8,128)(2,1)S(1)}, bf16[56,1536]{1,0:T(8,128)(2,1)S(1)}, u32[]{:S(2)}, u32[]{:S(2)}) collective-permute-start(bf16[56,1536]{1,0:T(8,128)(2,1)S(1)} %add_convert_fusion.9), channel_id=1, source_target_pairs={{0,2},{2,4},{4,6},{6,7},{7,5},{5,3},{3,1},{1,0},{8,10},{10,12},{12... | collective-permute-start | bytes 516104 | tf_op jit(solution)/shard_map/ppermute | solution.py:274
  76.8 2.1 %collective-permute-start.31 = (bf16[56,1536]{1,0:T(8,128)(2,1)S(1)}, bf16[56,1536]{1,0:T(8,128)(2,1)S(1)}, u32[]{:S(2)}, u32[]{:S(2)}) collective-permute-start(bf16[56,1536]{1,0:T(8,128)(2,1)S(1)} %add_convert_fusion.4), channel_id=1, source_target_pairs={{0,2},{2,4},{4,6},{6,7},{7,5},{5,3},{3,1},{1,0},{8,10},{10,12},{12... | collective-permute-start | bytes 516104 | tf_op jit(solution)/shard_map/ppermute | solution.py:279
  80.5 2.1 %collective-permute-start.25 = (bf16[56,1536]{1,0:T(8,128)(2,1)S(1)}, bf16[56,1536]{1,0:T(8,128)(2,1)S(1)}, u32[]{:S(2)}, u32[]{:S(2)}) collective-permute-start(bf16[56,1536]{1,0:T(8,128)(2,1)S(1)} %add_convert_fusion.8), channel_id=1, source_target_pairs={{0,2},{2,4},{4,6},{6,7},{7,5},{5,3},{3,1},{1,0},{8,10},{10,12},{12... | collective-permute-start | bytes 516104 | tf_op jit(solution)/shard_map/ppermute | solution.py:274
  84.2 2.1 %collective-permute-start.32 = (bf16[56,1536]{1,0:T(8,128)(2,1)S(1)}, bf16[56,1536]{1,0:T(8,128)(2,1)S(1)}, u32[]{:S(2)}, u32[]{:S(2)}) collective-permute-start(bf16[56,1536]{1,0:T(8,128)(2,1)S(1)} %add_convert_fusion.3), channel_id=1, source_target_pairs={{0,2},{2,4},{4,6},{6,7},{7,5},{5,3},{3,1},{1,0},{8,10},{10,12},{12... | collective-permute-start | bytes 516104 | tf_op jit(solution)/shard_map/ppermute | solution.py:279
  87.9 2.1 %collective-permute-start.26 = (bf16[56,1536]{1,0:T(8,128)(2,1)S(1)}, bf16[56,1536]{1,0:T(8,128)(2,1)S(1)}, u32[]{:S(2)}, u32[]{:S(2)}) collective-permute-start(bf16[56,1536]{1,0:T(8,128)(2,1)S(1)} %add_convert_fusion.7), channel_id=1, source_target_pairs={{0,2},{2,4},{4,6},{6,7},{7,5},{5,3},{3,1},{1,0},{8,10},{10,12},{12... | collective-permute-start | bytes 516104 | tf_op jit(solution)/shard_map/ppermute | solution.py:274
  90.0 2.4 %collective-permute-done.35 = bf16[56,1536]{1,0:T(8,128)(2,1)S(1)} collective-permute-done((bf16[56,1536]{1,0:T(8,128)(2,1)S(1)}, bf16[56,1536]{1,0:T(8,128)(2,1)S(1)}, u32[]{:S(2)}, u32[]{:S(2)}) %collective-permute-start.35) | collective-permute-done | bytes 172064 | tf_op jit(solution)/shard_map/ppermute | solution.py:275
  94.6 3.3 %collective-permute-done.36.b1 = bf16[56,1536]{1,0:T(8,128)(2,1)S(1)} collective-permute-done((bf16[56,1536]{1,0:T(8,128)(2,1)S(1)}, bf16[56,1536]{1,0:T(8,128)(2,1)S(1)}, u32[]{:S(2)}, u32[]{:S(2)}) %collective-permute-start.36) | collective-permute-done | bytes 172064 | tf_op jit(solution)/shard_map/ppermute | solution.py:275
  (97 shorter events, 38.9 us)
Async XLA Ops:
  4.4 8.3 %collective-permute-start.2 = (bf16[56,1536]{1,0:T(8,128)(2,1)S(1)}, bf16[56,1536]{1,0:T(8,128)(2,1)S(1)}, u32[]{:S(2)}, u32[]{:S(2)}) collective-permute-start(bf16[56,1536]{1,0:T(8,128)(2,1)S(1)} %get-tuple-element.28.refs_0_), channel_id=1, source_target_pairs={{2,0},{4,2},{6,4},{7,6},{5,7},{3,5},{1,3},{0,1},{10,8},{12,10},{14... | collective-permute-start | bytes 516104 | tf_op jit(solution)/shard_map/ppermute | solution.py:228
  7.5 8.8 %collective-permute-start.3 = (bf16[56,1536]{1,0:T(8,128)(2,1)S(1)}, bf16[56,1536]{1,0:T(8,128)(2,1)S(1)}, u32[]{:S(2)}, u32[]{:S(2)}) collective-permute-start(bf16[56,1536]{1,0:T(8,128)(2,1)S(1)} %get-tuple-element.29.refs_1_), channel_id=1, source_target_pairs={{2,0},{4,2},{6,4},{7,6},{5,7},{3,5},{1,3},{0,1},{10,8},{12,10},{14... | collective-permute-start | bytes 516104 | tf_op jit(solution)/shard_map/ppermute | solution.py:225
  9.4 9.0 %collective-permute-start.1 = (bf16[56,1536]{1,0:T(8,128)(2,1)S(1)}, bf16[56,1536]{1,0:T(8,128)(2,1)S(1)}, u32[]{:S(2)}, u32[]{:S(2)}) collective-permute-start(bf16[56,1536]{1,0:T(8,128)(2,1)S(1)} %get-tuple-element.29.refs_1_), channel_id=1, source_target_pairs={{0,2},{2,4},{4,6},{6,7},{7,5},{5,3},{3,1},{1,0},{8,10},{10,12},{12... | collective-permute-start | bytes 516104 | tf_op jit(solution)/shard_map/ppermute | solution.py:227
  12.7 7.4 %collective-permute-start.6 = (bf16[56,1536]{1,0:T(8,128)(2,1)S(1)}, bf16[56,1536]{1,0:T(8,128)(2,1)S(1)}, u32[]{:S(2)}, u32[]{:S(2)}) collective-permute-start(bf16[56,1536]{1,0:T(8,128)(2,1)S(1)} %collective-permute-done.2.refs_4_), channel_id=1, source_target_pairs={{2,0},{4,2},{6,4},{7,6},{5,7},{3,5},{1,3},{0,1},{10,8},{12,10},{14... | collective-permute-start | bytes 516104 | tf_op jit(solution)/shard_map/ppermute | solution.py:228
  14.7 7.4 %collective-permute-start.4 = (bf16[56,1536]{1,0:T(8,128)(2,1)S(1)}, bf16[56,1536]{1,0:T(8,128)(2,1)S(1)}, u32[]{:S(2)}, u32[]{:S(2)}) collective-permute-start(bf16[56,1536]{1,0:T(8,128)(2,1)S(1)} %collective-permute-done.refs_2_), channel_id=1, source_target_pairs={{0,2},{2,4},{4,6},{6,7},{7,5},{5,3},{3,1},{1,0},{8,10},{10,12},{12... | collective-permute-start | bytes 516104 | tf_op jit(solution)/shard_map/ppermute | solution.py:224
  16.4 7.4 %collective-permute-start.7 = (bf16[56,1536]{1,0:T(8,128)(2,1)S(1)}, bf16[56,1536]{1,0:T(8,128)(2,1)S(1)}, u32[]{:S(2)}, u32[]{:S(2)}) collective-permute-start(bf16[56,1536]{1,0:T(8,128)(2,1)S(1)} %collective-permute-done.3.refs_5_), channel_id=1, source_target_pairs={{2,0},{4,2},{6,4},{7,6},{5,7},{3,5},{1,3},{0,1},{10,8},{12,10},{14... | collective-permute-start | bytes 516104 | tf_op jit(solution)/shard_map/ppermute | solution.py:225
  18.4 7.4 %collective-permute-start.5 = (bf16[56,1536]{1,0:T(8,128)(2,1)S(1)}, bf16[56,1536]{1,0:T(8,128)(2,1)S(1)}, u32[]{:S(2)}, u32[]{:S(2)}) collective-permute-start(bf16[56,1536]{1,0:T(8,128)(2,1)S(1)} %collective-permute-done.1.refs_3_), channel_id=1, source_target_pairs={{0,2},{2,4},{4,6},{6,7},{7,5},{5,3},{3,1},{1,0},{8,10},{10,12},{12... | collective-permute-start | bytes 516104 | tf_op jit(solution)/shard_map/ppermute | solution.py:227
  20.0 13.9 %collective-permute-start.10 = (bf16[56,1536]{1,0:T(8,128)(2,1)S(1)}, bf16[56,1536]{1,0:T(8,128)(2,1)S(1)}, u32[]{:S(2)}, u32[]{:S(2)}) collective-permute-start(bf16[56,1536]{1,0:T(8,128)(2,1)S(1)} %collective-permute-done.6.refs_8_), channel_id=1, source_target_pairs={{2,0},{4,2},{6,4},{7,6},{5,7},{3,5},{1,3},{0,1},{10,8},{12,10},{14... | collective-permute-start | bytes 516104 | tf_op jit(solution)/shard_map/ppermute | solution.py:228
  22.1 13.9 %collective-permute-start.8 = (bf16[56,1536]{1,0:T(8,128)(2,1)S(1)}, bf16[56,1536]{1,0:T(8,128)(2,1)S(1)}, u32[]{:S(2)}, u32[]{:S(2)}) collective-permute-start(bf16[56,1536]{1,0:T(8,128)(2,1)S(1)} %collective-permute-done.4.refs_6_), channel_id=1, source_target_pairs={{0,2},{2,4},{4,6},{6,7},{7,5},{5,3},{3,1},{1,0},{8,10},{10,12},{12... | collective-permute-start | bytes 516104 | tf_op jit(solution)/shard_map/ppermute | solution.py:224
  23.7 12.3 %collective-permute-start.11 = (bf16[56,1536]{1,0:T(8,128)(2,1)S(1)}, bf16[56,1536]{1,0:T(8,128)(2,1)S(1)}, u32[]{:S(2)}, u32[]{:S(2)}) collective-permute-start(bf16[56,1536]{1,0:T(8,128)(2,1)S(1)} %collective-permute-done.7.refs_9_), channel_id=1, source_target_pairs={{2,0},{4,2},{6,4},{7,6},{5,7},{3,5},{1,3},{0,1},{10,8},{12,10},{14... | collective-permute-start | bytes 516104 | tf_op jit(solution)/shard_map/ppermute | solution.py:225
  25.8 12.1 %collective-permute-start.9 = (bf16[56,1536]{1,0:T(8,128)(2,1)S(1)}, bf16[56,1536]{1,0:T(8,128)(2,1)S(1)}, u32[]{:S(2)}, u32[]{:S(2)}) collective-permute-start(bf16[56,1536]{1,0:T(8,128)(2,1)S(1)} %collective-permute-done.5.refs_7_), channel_id=1, source_target_pairs={{0,2},{2,4},{4,6},{6,7},{7,5},{5,3},{3,1},{1,0},{8,10},{10,12},{12... | collective-permute-start | bytes 516104 | tf_op jit(solution)/shard_map/ppermute | solution.py:227
  33.9 8.8 %collective-permute-start.20 = (bf16[280,512]{1,0:T(8,128)(2,1)S(1)}, bf16[280,512]{1,0:T(8,128)(2,1)S(1)}, u32[]{:S(2)}, u32[]{:S(2)}) collective-permute-start(bf16[280,512]{1,0:T(8,128)(2,1)S(1)} %get-tuple-element.33.refs_3_), channel_id=1, source_target_pairs={{0,24},{8,16},{16,8},{24,0},{1,25},{9,17},{17,9},{25,1},{2,26},{10... | collective-permute-start | bytes 860168 | tf_op jit(solution)/shard_map/ppermute | solution.py:41
  34.0 15.7 %collective-permute-start.17 = (bf16[280,512]{1,0:T(8,128)(2,1)S(1)}, bf16[280,512]{1,0:T(8,128)(2,1)S(1)}, u32[]{:S(2)}, u32[]{:S(2)}) collective-permute-start(bf16[280,512]{1,0:T(8,128)(2,1)S(1)} %get-tuple-element.33.refs_3_), channel_id=1, source_target_pairs={{0,16},{8,24},{16,0},{24,8},{1,17},{9,25},{17,1},{25,9},{2,18},{10... | collective-permute-start | bytes 860168 | tf_op jit(solution)/shard_map/ppermute | solution.py:41
  36.0 14.9 %collective-permute-start.14 = (bf16[280,512]{1,0:T(8,128)(2,1)S(1)}, bf16[280,512]{1,0:T(8,128)(2,1)S(1)}, u32[]{:S(2)}, u32[]{:S(2)}) collective-permute-start(bf16[280,512]{1,0:T(8,128)(2,1)S(1)} %get-tuple-element.33.refs_3_), channel_id=1, source_target_pairs={{0,8},{8,0},{16,24},{24,16},{1,9},{9,1},{17,25},{25,17},{2,10},{10... | collective-permute-start | bytes 860168 | tf_op jit(solution)/shard_map/ppermute | solution.py:41
  37.8 7.4 %collective-permute-start.13 = (bf16[56,1536]{1,0:T(8,128)(2,1)S(1)}, bf16[56,1536]{1,0:T(8,128)(2,1)S(1)}, u32[]{:S(2)}, u32[]{:S(2)}) collective-permute-start(bf16[56,1536]{1,0:T(8,128)(2,1)S(1)} %collective-permute-done.11.refs_3_), channel_id=1, source_target_pairs={{2,0},{4,2},{6,4},{7,6},{5,7},{3,5},{1,3},{0,1},{10,8},{12,10},{14... | collective-permute-start | bytes 516104 | tf_op jit(solution)/shard_map/ppermute | solution.py:225
  42.7 8.6 %collective-permute-start.21 = (bf16[112,512]{1,0:T(8,128)(2,1)S(1)}, bf16[112,512]{1,0:T(8,128)(2,1)S(1)}, u32[]{:S(2)}, u32[]{:S(2)}) collective-permute-start(bf16[112,512]{1,0:T(8,128)(2,1)S(1)} %get-tuple-element.34.refs_4_), channel_id=1, source_target_pairs={{0,24},{8,16},{16,8},{24,0},{1,25},{9,17},{17,9},{25,1},{2,26},{10... | collective-permute-start | bytes 344072 | tf_op jit(solution)/shard_map/ppermute | solution.py:41
  42.8 11.8 %collective-permute-start.18 = (bf16[112,512]{1,0:T(8,128)(2,1)S(1)}, bf16[112,512]{1,0:T(8,128)(2,1)S(1)}, u32[]{:S(2)}, u32[]{:S(2)}) collective-permute-start(bf16[112,512]{1,0:T(8,128)(2,1)S(1)} %get-tuple-element.34.refs_4_), channel_id=1, source_target_pairs={{0,16},{8,24},{16,0},{24,8},{1,17},{9,25},{17,1},{25,9},{2,18},{10... | collective-permute-start | bytes 344072 | tf_op jit(solution)/shard_map/ppermute | solution.py:41
  45.2 9.3 %collective-permute-start.15 = (bf16[112,512]{1,0:T(8,128)(2,1)S(1)}, bf16[112,512]{1,0:T(8,128)(2,1)S(1)}, u32[]{:S(2)}, u32[]{:S(2)}) collective-permute-start(bf16[112,512]{1,0:T(8,128)(2,1)S(1)} %get-tuple-element.34.refs_4_), channel_id=1, source_target_pairs={{0,8},{8,0},{16,24},{24,16},{1,9},{9,1},{17,25},{25,17},{2,10},{10... | collective-permute-start | bytes 344072 | tf_op jit(solution)/shard_map/ppermute | solution.py:41
  67.9 8.9 %collective-permute-start.30 = (bf16[56,1536]{1,0:T(8,128)(2,1)S(1)}, bf16[56,1536]{1,0:T(8,128)(2,1)S(1)}, u32[]{:S(2)}, u32[]{:S(2)}) collective-permute-start(bf16[56,1536]{1,0:T(8,128)(2,1)S(1)} %get-tuple-element.44), channel_id=1, source_target_pairs={{0,2},{2,4},{4,6},{6,7},{7,5},{5,3},{3,1},{1,0},{8,10},{10,12},{12... | collective-permute-start | bytes 516104 | tf_op jit(solution)/shard_map/ppermute | solution.py:279
  69.9 9.0 %collective-permute-start.33 = (bf16[56,1536]{1,0:T(8,128)(2,1)S(1)}, bf16[56,1536]{1,0:T(8,128)(2,1)S(1)}, u32[]{:S(2)}, u32[]{:S(2)}) collective-permute-start(bf16[56,1536]{1,0:T(8,128)(2,1)S(1)} %get-tuple-element.47), channel_id=1, source_target_pairs={{2,0},{4,2},{6,4},{7,6},{5,7},{3,5},{1,3},{0,1},{10,8},{12,10},{14... | collective-permute-start | bytes 516104 | tf_op jit(solution)/shard_map/ppermute | solution.py:275
  75.3 7.4 %collective-permute-start.28 = (bf16[56,1536]{1,0:T(8,128)(2,1)S(1)}, bf16[56,1536]{1,0:T(8,128)(2,1)S(1)}, u32[]{:S(2)}, u32[]{:S(2)}) collective-permute-start(bf16[56,1536]{1,0:T(8,128)(2,1)S(1)} %add_convert_fusion.6), channel_id=1, source_target_pairs={{2,0},{4,2},{6,4},{7,6},{5,7},{3,5},{1,3},{0,1},{10,8},{12,10},{14... | collective-permute-start | bytes 516104 | tf_op jit(solution)/shard_map/ppermute | solution.py:280
  79.0 7.4 %collective-permute-start.34 = (bf16[56,1536]{1,0:T(8,128)(2,1)S(1)}, bf16[56,1536]{1,0:T(8,128)(2,1)S(1)}, u32[]{:S(2)}, u32[]{:S(2)}) collective-permute-start(bf16[56,1536]{1,0:T(8,128)(2,1)S(1)} %add_convert_fusion.2), channel_id=1, source_target_pairs={{2,0},{4,2},{6,4},{7,6},{5,7},{3,5},{1,3},{0,1},{10,8},{12,10},{14... | collective-permute-start | bytes 516104 | tf_op jit(solution)/shard_map/ppermute | solution.py:275
  82.7 10.1 %collective-permute-start.29 = (bf16[56,1536]{1,0:T(8,128)(2,1)S(1)}, bf16[56,1536]{1,0:T(8,128)(2,1)S(1)}, u32[]{:S(2)}, u32[]{:S(2)}) collective-permute-start(bf16[56,1536]{1,0:T(8,128)(2,1)S(1)} %add_convert_fusion.5), channel_id=1, source_target_pairs={{2,0},{4,2},{6,4},{7,6},{5,7},{3,5},{1,3},{0,1},{10,8},{12,10},{14... | collective-permute-start | bytes 516104 | tf_op jit(solution)/shard_map/ppermute | solution.py:280
  84.2 8.6 %collective-permute-start.32 = (bf16[56,1536]{1,0:T(8,128)(2,1)S(1)}, bf16[56,1536]{1,0:T(8,128)(2,1)S(1)}, u32[]{:S(2)}, u32[]{:S(2)}) collective-permute-start(bf16[56,1536]{1,0:T(8,128)(2,1)S(1)} %add_convert_fusion.3), channel_id=1, source_target_pairs={{0,2},{2,4},{4,6},{6,7},{7,5},{5,3},{3,1},{1,0},{8,10},{10,12},{12... | collective-permute-start | bytes 516104 | tf_op jit(solution)/shard_map/ppermute | solution.py:279
  (28 other events, 201.6 us)

commit v2 on v1

v2 whole, which is shorter than its diff:
```python
import functools
import math

import jax
import jax.numpy as jnp
from jax import lax
from jax.experimental import pallas as pl
from jax.experimental.pallas import tpu as pltpu
from jax.sharding import PartitionSpec as P

HD = 128
EPS_NORM = 1e-06
F32 = jnp.float32
BF16 = jnp.bfloat16
VMEM = pl.BlockSpec(memory_space=pltpu.VMEM)
HBM = pl.BlockSpec(memory_space=pltpu.HBM)
SMEM = pl.BlockSpec(memory_space=pltpu.SMEM)


def call(kernel, outs, args, vmem_mib, scratch=(), flops=0, smem=(), hbm=()):
    moved = sum(a.size * a.dtype.itemsize for a in args)
    args = [pltpu.with_memory_space_constraint(a, pltpu.HBM) if i in hbm else a for i, a in enumerate(args)]
    return pl.pallas_call(
        kernel,
        out_shape=outs,
        in_specs=[SMEM if i in smem else HBM if i in hbm else VMEM for i in range(len(args))],
        out_specs=jax.tree.map(lambda _: VMEM, outs),
        scratch_shapes=list(scratch),
        compiler_params=pltpu.CompilerParams(vmem_limit_bytes=vmem_mib << 20),
        cost_estimate=pl.CostEstimate(flops=flops, bytes_accessed=moved, transcendentals=0),
    )(*args)


def ring_routes(axis):
    n = lax.axis_size(axis)
    order = list(range(0, n, 2)) + list(range(1, n, 2))[::-1]
    ahead = [(order[i], order[(i + 1) % n]) for i in range(n)]
    across_ring = [(order[i], order[(i + n // 2) % n]) for i in range(n)]
    return ahead, [(b, a) for a, b in ahead], across_ring


def across(block, distance):
    n = lax.axis_size("blk")
    return lax.ppermute(block, "blk", [(i, i ^ distance) for i in range(n)])


def tied(block, *others):
    return lax.optimization_barrier((block, *others))[0]


def modulated(rows, factors):
    floats = rows.astype(F32)
    centre = floats - jnp.mean(floats, axis=-1, keepdims=True)
    spread = jnp.mean(centre * centre, axis=-1, keepdims=True)
    wide = factors.astype(F32)
    normed = centre / jnp.sqrt(spread + EPS_NORM)
    return normed * (1.0 + wide[1:2]) + wide[0:1]


def modulate_kernel(part_ref, *refs):
    sources, (left_ref, right_ref), landed = refs[:4], refs[4:6], refs[6:10]
    text_f32, sems = refs[10:]
    copies = [pltpu.make_async_copy(s, d, sems.at[i]) for i, (s, d) in enumerate(zip(sources, landed))]
    for copy in copies:
        copy.start()
    for copy in copies:
        copy.wait()
    video_ref, text_ref, vmod_ref, tmod_ref = landed
    text_rows = left_ref.shape[0] - video_ref.shape[0]
    half = left_ref.shape[1]
    text_f32[...] = text_ref[...].astype(F32)
    start = pl.multiple_of(part_ref[0] * text_rows, text_rows)
    own_text = text_f32[pl.ds(start, text_rows), :]
    video = modulated(video_ref[...], vmod_ref[...])
    text = modulated(own_text, tmod_ref[...])
    both = jnp.concatenate([video, text], axis=0).astype(BF16)
    left_ref[...] = both[:, :half]
    right_ref[...] = both[:, half:]


def fetch_kernel(count, *refs):
    many = (len(refs) - 1) // 2
    sources, landed, sems = refs[:many], refs[many : 2 * many], refs[-1]
    if count:
        step = sources[0].shape[1] // count
        sources = [s.at[:, i * step : (i + 1) * step, :] for s in sources for i in range(count)]
        landed = [s.at[:, i * step : (i + 1) * step, :] for s in landed for i in range(count)]
    copies = [pltpu.make_async_copy(s, d, sems.at[i]) for i, (s, d) in enumerate(zip(sources, landed))]
    for copy in copies:
        copy.start()
    for copy in copies:
        copy.wait()


def head_normed(mixture, gain):
    heads = []
    for h in range(mixture.shape[1] // HD):
        vectors = mixture[:, h * HD : (h + 1) * HD]
        inverse = lax.rsqrt(jnp.mean(vectors * vectors, axis=-1, keepdims=True) + EPS_NORM)
        heads.append(vectors * inverse * gain)
    return jnp.concatenate(heads, axis=1)


def project_kernel(shards, video_rows, *refs):
    chunks = refs[: 2 * shards]
    wv_ref, wt_ref, vgain_ref, tgain_ref, q_ref, kv_ref = refs[2 * shards :]
    width = q_ref.shape[1]
    video, text = [], []
    for side in range(2):
        floats = [chunks[2 * i + side][...].astype(F32) for i in range(shards)]
        video.append(jnp.concatenate([f[:video_rows] for f in floats], axis=0).astype(BF16))
        text.append(jnp.concatenate([f[video_rows:] for f in floats], axis=0).astype(BF16))
    half = video[0].shape[1]

    def mixed(sides, w_ref, j):
        total = jnp.dot(sides[0], w_ref[j, :half, :], preferred_element_type=F32)
        return total + jnp.dot(sides[1], w_ref[j, half:, :], preferred_element_type=F32)

    def joined(j, norm):
        v = mixed(video, wv_ref, j)
        t = mixed(text, wt_ref, j)
        if norm:
            v = head_normed(v, vgain_ref[j : j + 1, :])
            t = head_normed(t, tgain_ref[j : j + 1, :])
        return jnp.concatenate([v, t], axis=0).astype(BF16)

    q_ref[...] = joined(0, True)
    kv_ref[:, :width] = joined(1, True)
    kv_ref[:, width:] = joined(2, False)


def wide_rows(refs, counts):
    return jnp.concatenate([r[...].astype(F32)[:n] for r, n in zip(refs, counts)], axis=0).astype(BF16)


def absorbed(state, query, block):
    width = query.shape[1]
    factor = HD ** (-0.5) * math.log2(math.e)
    raised = []
    for h in range(width // HD):
        mine = slice(h * HD, (h + 1) * HD)
        scores = lax.dot_general(
            block[:, mine], query[:, mine], (((1,), (1,)), ((), ())), preferred_element_type=F32
        )
        highest = jnp.max(scores, axis=0, keepdims=True)
        if state:
            before, totals, sums = state[h]
            highest = jnp.maximum(before, highest)
        weights = jnp.exp2((scores - highest) * factor)
        total = jnp.sum(weights, axis=0, keepdims=True)
        mixed = lax.dot_general(
            block[:, width + h * HD : width + (h + 1) * HD],
            weights.astype(BF16),
            (((0,), (0,)), ((), ())),
            preferred_element_type=F32,
        )
        if state:
            shrink = jnp.exp2((before - highest) * factor)
            total = totals * shrink + total
            mixed = sums * shrink + mixed
        raised.append((highest, total, mixed))
    return raised


def load_state(stats_ref, sums_ref):
    heads = stats_ref.shape[0] // 2
    return [
        (
            stats_ref[h : h + 1, :],
            stats_ref[heads + h : heads + h + 1, :],
            sums_ref[h * HD : (h + 1) * HD, :],
        )
        for h in range(heads)
    ]


def attend_kernel(sizes, video_rows, with_text, fresh, queries, *refs):
    groups, sources = len(sizes), len(with_text)
    query = wide_rows(refs[:queries], [r.shape[0] for r in refs[:queries]])
    refs = refs[queries:]
    state = []
    if not fresh:
        state = load_state(*refs[:2])
        refs = refs[2:]
    pieces, outs = refs[: groups * sources], refs[groups * sources :]
    if fresh:
        outs[0][...] = query
    stats_ref, sums_ref = outs[-2:]
    for s in range(sources):
        held = pieces[s * groups : (s + 1) * groups]
        counts = [p.shape[0] if with_text[s] else n * video_rows for p, n in zip(held, sizes)]
        state = absorbed(state, query, wide_rows(held, counts))
    heads = len(state)
    for h, (highest, totals, sums) in enumerate(state):
        stats_ref[h : h + 1, :] = highest
        stats_ref[heads + h : heads + h + 1, :] = totals
        sums_ref[h * HD : (h + 1) * HD, :] = sums


def finish_kernel(sizes, video_rows, with_text, query_ref, stats_ref, sums_ref, *refs):
    sources = len(with_text)
    pieces, weights = refs[:sources], refs[sources : sources + 2]
    outs = refs[sources + 2 :]
    counts = [p.shape[0] if w else sizes[-1] * video_rows for p, w in zip(pieces, with_text)]
    state = absorbed(load_state(stats_ref, sums_ref), query_ref[...], wide_rows(pieces, counts))
    flat = jnp.concatenate([sums / totals for _, totals, sums in state], axis=0)
    rows_out = jnp.transpose(flat)
    text_rows = rows_out.shape[0] // sum(sizes) - video_rows
    video, text = [], []
    start = 0
    for size in sizes:
        video.append(rows_out[start : start + size * video_rows])
        start += size * video_rows
        text.append(rows_out[start : start + size * text_rows])
        start += size * text_rows
    shards = [jnp.concatenate(rows, axis=0).astype(BF16) for rows in (video, text)]
    put_partials([0] * sum(sizes), outs, shards, weights)


def rest_kernel(sides, video_ref, text_ref, wv_ref, wt_ref, *outs):
    put_partials(sides, outs, [video_ref[...], text_ref[...]], [wv_ref, wt_ref])


def put_partials(sides, outs, heads, weights):
    outs = list(outs)
    half = outs[0].shape[1]
    counts = [h.shape[0] // len(sides) for h in heads]
    mixed = [
        [jnp.dot(h, w[:, s * half : (s + 1) * half], preferred_element_type=F32) for s in range(2)]
        for h, w in zip(heads, weights)
    ]
    for i, side in enumerate(sides):
        parts = [[y[i * n : (i + 1) * n] for y in ys] for n, ys in zip(counts, mixed)]
        rows = [[y] for y in parts[0]]
        if side is None:
            rows.append(parts[1])
        else:
            rows[side] += parts[1]
        for row in rows:
            outs.pop(0)[...] = jnp.concatenate(row, axis=0).astype(BF16)


def text_side(r, n):
    return 0


def close_text_kernel(fa_ref, ba_ref, own_ref, tmod_ref, text_ref):
    text_rows = text_ref.shape[0]
    half = own_ref.shape[1]
    video_rows = own_ref.shape[0] - 2 * text_rows
    total = sum(r[...].astype(F32)[video_rows:] for r in (fa_ref, ba_ref, own_ref))
    for side in range(2):
        columns = slice(side * half, (side + 1) * half)
        gate = tmod_ref[2:3, columns].astype(F32)
        text_ref[:, columns] = (total[side * text_rows : (side + 1) * text_rows] * gate).astype(BF16)


def close_kernel(part_ref, fa, ba, own_a, fb, bb, own_b, vmod_ref, *refs):
    pieces, (video_ref, text_ref, wide) = refs[:-3], refs[-3:]
    video_rows = video_ref.shape[0]
    half = own_a.shape[1]
    for side, arrivals in enumerate(((fa, ba, own_a), (fb, bb, own_b))):
        columns = slice(side * half, (side + 1) * half)
        total = sum(r[...].astype(F32)[:video_rows] for r in arrivals)
        video_ref[:, columns] = (total * vmod_ref[2:3, columns].astype(F32)).astype(BF16)
    rows = pieces[0].shape[0]
    for d, piece in enumerate(pieces):
        start = pl.multiple_of((part_ref[0] ^ d) * rows, rows)
        wide[pl.ds(start, rows), :] = piece[...].astype(F32)
    text_ref[...] = wide[...].astype(BF16)


def local(
    video_tokens,
    text_tokens,
    video_modulation,
    text_modulation,
    video_projection,
    text_projection,
    video_output,
    text_output,
    video_gains,
    text_gains,
):
    n_blk, n_uly = lax.axis_size("blk"), lax.axis_size("uly")
    reach = n_uly // 2
    ahead, back, opposite = ring_routes("uly")
    video_rows, width = video_tokens.shape
    half = width // 2
    parts = math.gcd(n_blk, text_tokens.shape[0] // 8)
    text_rows = text_tokens.shape[0] // parts
    shard_rows = video_rows + text_rows
    cols = video_output.shape[0]
    part = lax.rem(lax.axis_index("blk"), parts).reshape(1).astype(jnp.int32)

    chunk = jax.ShapeDtypeStruct((shard_rows, half), BF16)
    own = call(
        modulate_kernel,
        [chunk, chunk],
        (part, video_tokens, text_tokens, video_modulation, text_modulation),
        8,
        [pltpu.VMEM(a.shape, BF16) for a in (video_tokens, text_tokens, video_modulation, text_modulation)]
        + [pltpu.VMEM(text_tokens.shape, F32), pltpu.SemaphoreType.DMA((4,))],
        smem=(0,),
        hbm=(1, 2, 3, 4),
    )

    def fetched(arrays, after, count=0):
        arrays = [tied(arrays[0], after), *arrays[1:]]
        return call(
            functools.partial(fetch_kernel, count),
            [jax.ShapeDtypeStruct(a.shape, a.dtype) for a in arrays],
            arrays,
            1,
            [pltpu.SemaphoreType.DMA((len(arrays) * max(count, 1),))],
            hbm=range(len(arrays)),
        )

    weights = [jnp.transpose(p, (1, 0, 2)) for p in (video_projection, text_projection)]
    held, ends, waiting = [], [], []
    queries, pieces, groups = [], [], []

    def fetch_all(after):
        held.extend(fetched(weights, after, 4))
        return held[-1]

    def fetch_rest(after):
        ends.extend(fetched([video_output, text_output, video_gains, text_gains], after))
        return ends[0]

    def project(after, direct=False):
        group = list(waiting)
        waiting.clear()
        rows = len(group) * shard_rows
        chunks = [c for _, *pair in group for c in pair]
        q, kv = call(
            functools.partial(project_kernel, len(group), video_rows),
            [
                jax.ShapeDtypeStruct((rows, cols), BF16),
                jax.ShapeDtypeStruct((rows, 2 * cols), BF16),
            ],
            [tied(chunks[0], after), *chunks[1:], *held, *ends[2:]],
            12,
            flops=2 * rows * width * 3 * cols,
        )
        if direct:
            spread = [kv] + [across(kv, d) for d in range(1, n_blk)]
        else:
            spread = {d: across(kv, d) if d else kv for d in (0, 1, *range(2, n_blk, 2))}
        queries.append(q)
        pieces.append(spread)
        groups.append(group)
        return q

    beside = {(1, 1): [fetch_all], (2, 0): [fetch_rest], (2, 1): [project], (3, 1): [project], (4, 1): [project]}
    fa, fb = own
    ba, bb = own
    waiting.append((0, *own))
    due = []
    for step in range(1, reach + 1):
        behind = fa
        fa = lax.ppermute(tied(fa, *due) if due else fa, "uly", ahead)
        bb = lax.ppermute(bb, "uly", back)
        due = [task(behind) for task in beside.get((step, 0), [])]
        if step < reach:
            behind = fb
            fb = lax.ppermute(tied(fb, *due) if due else fb, "uly", ahead)
            ba = lax.ppermute(ba, "uly", back)
            due = [task(behind) for task in beside.get((step, 1), [])]
            waiting += [(-step, fa, fb), (step, ba, bb)]
        else:
            due = [task(fb) for task in beside.get((step, 1), [])]
            waiting += [(reach, fa, bb)]
            project(fa, True)

    for spread in pieces[:-1]:
        for d in range(3, n_blk, 2):
            spread[d] = across(tied(spread[d - 1], queries[-1]), 1)

    sizes = [len(g) for g in groups]
    slots = [r for group in groups for r, *_ in group]
    total_rows = shard_rows * n_uly
    with_text = [d < parts for d in range(n_blk)]
    state = [
        jax.ShapeDtypeStruct((2 * cols // HD, total_rows), F32),
        jax.ShapeDtypeStruct((cols, total_rows), F32),
    ]
    query, *carried = call(
        functools.partial(attend_kernel, sizes[:-1], video_rows, with_text[:2], True, len(queries)),
        [jax.ShapeDtypeStruct((total_rows, cols), BF16), *state],
        queries + [spread[d] for d in range(2) for spread in pieces[:-1]],
        16,
        flops=8 * total_rows * (total_rows - shard_rows) * cols,
    )
    carried = call(
        functools.partial(attend_kernel, sizes[:-1], video_rows, with_text[2:], False, 1),
        state,
        [query, *carried] + [spread[d] for d in range(2, n_blk) for spread in pieces[:-1]],
        16,
        flops=4 * total_rows * (total_rows - shard_rows) * (n_blk - 2) * cols,
    )
    sides = [text_side(r, n_uly) for r in slots]
    shapes = []
    for side in sides:
        rows = [video_rows, video_rows] + ([2 * text_rows] if side is None else [])
        if side is not None:
            rows[side] += 2 * text_rows
        shapes.append([jax.ShapeDtypeStruct((n, half), BF16) for n in rows])
    partial = call(
        functools.partial(finish_kernel, sizes, video_rows, with_text),
        [shape for group in shapes for shape in group],
        [query, *carried] + pieces[-1] + ends[:2],
        16,
        flops=2 * total_rows * cols * width,
    )
    mine = {}
    for r, group in zip(slots, shapes):
        mine[r], partial = partial[: len(group)], partial[len(group) :]
    mine[-reach] = mine[reach]

    def joined(arriving, own_part):
        return (arriving.astype(F32) + own_part.astype(F32)).astype(BF16)

    fa, bb = mine[reach][0], mine[-reach][1]
    fb, ba = mine[reach - 1][1], mine[1 - reach][0]
    for left in range(reach - 1, -1, -1):
        fa = lax.ppermute(fa, "uly", ahead)
        bb = lax.ppermute(bb, "uly", back)
        if left:
            fa = joined(fa, mine[left][0])
            bb = joined(bb, mine[-left][1])
            fb = lax.ppermute(fb, "uly", ahead)
            ba = lax.ppermute(ba, "uly", back)
            if left > 1:
                fb = joined(fb, mine[left - 1][1])
                ba = joined(ba, mine[1 - left][0])
    text_part = call(
        close_text_kernel,
        jax.ShapeDtypeStruct((text_rows, width), BF16),
        (fa, ba, mine[0][0], text_modulation),
        4,
    )
    pieces = [text_part] + [across(text_part, d) for d in range(1, parts)]
    return tuple(
        call(
            close_kernel,
            [jax.ShapeDtypeStruct(t.shape, BF16) for t in (video_tokens, text_tokens)],
            (part, fa, ba, mine[0][0], fb, bb, mine[0][1], video_modulation, *pieces),
            8,
            [pltpu.VMEM(text_tokens.shape, F32)],
            smem=(0,),
        )
    )


def solution(mesh):
    placed = (
        P(("blk", "uly"), None),
        P("uly", None),
        P(),
        P(),
        P(None, None, "uly"),
        P(None, None, "uly"),
        P("uly", None),
        P("uly", None),
        P(),
        P(),
    )
    return jax.shard_map(
        local,
        mesh=mesh,
        in_specs=placed,
        out_specs=(P(("blk", "uly"), None), P("uly", None)),
        check_vma=False,
    )
```

time: 104 us -> 87.6 us (0.84)
  waiting for transfers between devices: 38.2 us -> 27.1 us
  local copies, waits for them, and re-layouts: 9.4 us -> 0.01 us
  Pallas kernels: 16.2 us -> 19.8 us
    ppermute x0 -> x7, starting transfers between devices: none -> 15.1 us  [the longest x4 8.91 us: local(): fa = lax.ppermute(tied(fa, *due) if due else fa, 'uly', ahead)]
    unnamed x24 -> x4, local copies, waits for them, and re-layouts: 9.4 us -> 0.01 us
    ppermute x12 -> x15, waiting for transfers between devices: 13.7 us -> 5.09 us  [across(): return lax.ppermute(block, 'blk', [(i, i ^ distance) for i in range(n)])]
    ppermute x6, starting transfers between devices: 7.17 us -> 1.63 us  [local(): ba = lax.ppermute(ba, 'uly', back)]
    ppermute x8, starting transfers between devices: 6.75 us -> 2.31 us  [local(): bb = lax.ppermute(bb, 'uly', back)]
    ppermute x8 -> x4, starting transfers between devices: 10.3 us -> 6.47 us  [local(): fa = lax.ppermute(fa, 'uly', ahead)]
    pallas_call x7 -> x12, Pallas kernels: 16.2 us -> 19.8 us  [call(): pl.pallas_call(kernel, out_shape=outs, in_specs=[SMEM if i in smem else H...]
    ppermute x8, waiting for transfers between devices: 8.84 us -> 6.86 us  [local(): bb = lax.ppermute(bb, 'uly', back)]
  transfers between devices with their start and end apart: 40 -> 43, of which waited for: 21 -> 16; matrix products, arithmetic and copies ran while one was open for 0% -> 0% of each run, Pallas kernels for 5% -> 18%
where the time goes in v2:
time: 87.6 us; the launch traced here: 87.5 us
  starting transfers between devices  39.2 us (45%)
  waiting for transfers between devices  27.1 us (31%)
  Pallas kernels  19.8 us (23%)
  between operations  0.89 us (1%)
    pallas_call x12, Pallas kernels, call(): pl.pallas_call(kernel, out_shape=outs, in_specs=[SMEM if i in smem else H...  19.8 us
    ppermute x4, starting transfers between devices, local(): fa = lax.ppermute(tied(fa, *due) if due else fa, 'uly', ahead)  8.91 us
    ppermute x15, starting transfers between devices, across(): return lax.ppermute(block, 'blk', [(i, i ^ distance) for i in range(n)])  8.82 us
    ppermute x8, waiting for transfers between devices, local(): bb = lax.ppermute(bb, 'uly', back)  6.86 us
    ppermute x4, starting transfers between devices, local(): fa = lax.ppermute(fa, 'uly', ahead)  6.47 us
    ppermute x4, waiting for transfers between devices, local(): fa = lax.ppermute(fa, 'uly', ahead)  6.46 us
    ppermute x3, starting transfers between devices, local(): fb = lax.ppermute(tied(fb, *due) if due else fb, 'uly', ahead)  6.22 us
    ppermute x15, waiting for transfers between devices, across(): return lax.ppermute(block, 'blk', [(i, i ^ distance) for i in range(n)])  5.09 us
  transfers between devices with their start and end apart: 43, of which 16 were waited for; matrix products, arithmetic and copies ran while one was open for 0% of the time, Pallas kernels for 18%

profile of v2, /device:TPU:0, one launch (start us, length us, event | category | flops | bytes accessed | tf_op | source)
XLA Modules:
  0.0 87.5 jit_solution(6848461018588759962)
XLA Ops:
  2.1 3.1 %collective-permute-start.1 = (bf16[56,1536]{1,0:T(8,128)(2,1)S(1)}, bf16[56,1536]{1,0:T(8,128)(2,1)S(1)}, u32[]{:S(2)}, u32[]{:S(2)}) collective-permute-start(bf16[56,1536]{1,0:T(8,128)(2,1)S(1)} %get-tuple-element.53.refs_0_), channel_id=1, source_target_pairs={{0,2},{2,4},{4,6},{6,7},{7,5},{5,3},{3,1},{1,0},{8,10},{10,12},{12... | collective-permute-start | bytes 516104 | tf_op jit(solution)/shard_map/ppermute | solution.py:362
  5.2 2.0 %collective-permute-start = (bf16[56,1536]{1,0:T(8,128)(2,1)S(1)}, bf16[56,1536]{1,0:T(8,128)(2,1)S(1)}, u32[]{:S(2)}, u32[]{:S(2)}) collective-permute-start(bf16[56,1536]{1,0:T(8,128)(2,1)S(1)} %get-tuple-element.52.refs_1_), channel_id=1, source_target_pairs={{0,2},{2,4},{4,6},{6,7},{7,5},{5,3},{3,1},{1,0},{8,10},{10,12},{12... | collective-permute-start | bytes 516104 | tf_op jit(solution)/shard_map/ppermute | solution.py:367
  7.2 3.8 %shard_map.114 = (bf16[3,3072,256]{2,1,0:T(8,128)(2,1)S(1)}, bf16[3,3072,256]{2,1,0:T(8,128)(2,1)S(1)}) custom-call(bf16[3,3072,256]{2,1,0:T(8,128)(2,1)} %bitcast.3, bf16[3,3072,256]{2,1,0:T(8,128)(2,1)} %bitcast.4), custom_call_target="tpu_custom_call" | custom-call | bytes 9437184 | tf_op jit(solution)/shard_map/pallas_call | solution.py:23
  11.0 2.1 %collective-permute-start.4 = (bf16[56,1536]{1,0:T(8,128)(2,1)S(1)}, bf16[56,1536]{1,0:T(8,128)(2,1)S(1)}, u32[]{:S(2)}, u32[]{:S(2)}) collective-permute-start(bf16[56,1536]{1,0:T(8,128)(2,1)S(1)} %collective-permute-done.1.refs_2_), channel_id=1, source_target_pairs={{0,2},{2,4},{4,6},{6,7},{7,5},{5,3},{3,1},{1,0},{8,10},{10,12},{12... | collective-permute-start | bytes 516104 | tf_op jit(solution)/shard_map/ppermute | solution.py:362
  13.6 1.9 %shard_map.115 = (bf16[256,3072]{1,0:T(8,128)(2,1)S(1)}, bf16[256,3072]{1,0:T(8,128)(2,1)S(1)}, f32[2,128]{1,0:T(2,128)S(1)}, f32[2,128]{1,0:T(2,128)S(1)}) custom-call(bf16[256,3072]{1,0:T(8,128)(2,1)} %refs_0_.2, bf16[256,3072]{1,0:T(8,128)(2,1)} %refs_1_.3, f32[2,128]{1,0:T(2,128)} %refs_2_.3, f32[2,128]{1,0:T(2,128)} %refs_3_.3), custom_call_target="tpu_custom_call" | custom-call | bytes 3147776 | tf_op jit(solution)/shard_map/pallas_call | solution.py:23
  15.6 1.9 %collective-permute-start.5 = (bf16[56,1536]{1,0:T(8,128)(2,1)S(1)}, bf16[56,1536]{1,0:T(8,128)(2,1)S(1)}, u32[]{:S(2)}, u32[]{:S(2)}) collective-permute-start(bf16[56,1536]{1,0:T(8,128)(2,1)S(1)} %collective-permute-done.refs_3_), channel_id=1, source_target_pairs={{0,2},{2,4},{4,6},{6,7},{7,5},{5,3},{3,1},{1,0},{8,10},{10,12},{12... | collective-permute-start | bytes 516104 | tf_op jit(solution)/shard_map/ppermute | solution.py:367
  19.1 1.9 %collective-permute-start.8 = (bf16[56,1536]{1,0:T(8,128)(2,1)S(1)}, bf16[56,1536]{1,0:T(8,128)(2,1)S(1)}, u32[]{:S(2)}, u32[]{:S(2)}) collective-permute-start(bf16[56,1536]{1,0:T(8,128)(2,1)S(1)} %collective-permute-done.4.refs_0_), channel_id=1, source_target_pairs={{0,2},{2,4},{4,6},{6,7},{7,5},{5,3},{3,1},{1,0},{8,10},{10,12},{12... | collective-permute-start | bytes 516104 | tf_op jit(solution)/shard_map/ppermute | solution.py:362
  22.0 2.3 %collective-permute-start.9 = (bf16[56,1536]{1,0:T(8,128)(2,1)S(1)}, bf16[56,1536]{1,0:T(8,128)(2,1)S(1)}, u32[]{:S(2)}, u32[]{:S(2)}) collective-permute-start(bf16[56,1536]{1,0:T(8,128)(2,1)S(1)} %collective-permute-done.5.refs_1_), channel_id=1, source_target_pairs={{0,2},{2,4},{4,6},{6,7},{7,5},{5,3},{3,1},{1,0},{8,10},{10,12},{12... | collective-permute-start | bytes 516104 | tf_op jit(solution)/shard_map/ppermute | solution.py:367
  26.5 1.9 %collective-permute-start.12 = (bf16[56,1536]{1,0:T(8,128)(2,1)S(1)}, bf16[56,1536]{1,0:T(8,128)(2,1)S(1)}, u32[]{:S(2)}, u32[]{:S(2)}) collective-permute-start(bf16[56,1536]{1,0:T(8,128)(2,1)S(1)} %collective-permute-done.8.refs_0_), channel_id=1, source_target_pairs={{0,2},{2,4},{4,6},{6,7},{7,5},{5,3},{3,1},{1,0},{8,10},{10,12},{12... | collective-permute-start | bytes 516104 | tf_op jit(solution)/shard_map/ppermute | solution.py:362
  28.5 1.8 %collective-permute-start.17 = (bf16[168,512]{1,0:T(8,128)(2,1)S(1)}, bf16[168,512]{1,0:T(8,128)(2,1)S(1)}, u32[]{:S(2)}, u32[]{:S(2)}) collective-permute-start(bf16[168,512]{1,0:T(8,128)(2,1)S(1)} %get-tuple-element.71.refs_4_), channel_id=1, source_target_pairs={{0,16},{8,24},{16,0},{24,8},{1,17},{9,25},{17,1},{25,9},{2,18},{10... | collective-permute-start | bytes 516104 | tf_op jit(solution)/shard_map/ppermute | solution.py:44
  30.3 1.7 %collective-permute-done.10.refs_2_ = bf16[56,1536]{1,0:T(8,128)(2,1)S(1)} collective-permute-done((bf16[56,1536]{1,0:T(8,128)(2,1)S(1)}, bf16[56,1536]{1,0:T(8,128)(2,1)S(1)}, u32[]{:S(2)}, u32[]{:S(2)}) %collective-permute-start.10) | collective-permute-done | bytes 172064 | tf_op jit(solution)/shard_map/ppermute | solution.py:368
  37.8 2.0 %collective-permute-done.19.refs_5_ = bf16[112,512]{1,0:T(8,128)(2,1)S(1)} collective-permute-done((bf16[112,512]{1,0:T(8,128)(2,1)S(1)}, bf16[112,512]{1,0:T(8,128)(2,1)S(1)}, u32[]{:S(2)}, u32[]{:S(2)}) %collective-permute-start.19) | collective-permute-done | bytes 114720 | tf_op jit(solution)/shard_map/ppermute | solution.py:44
  42.1 1.9 %shard_map.120 = (bf16[448,256]{1,0:T(8,128)(2,1)S(1)}, f32[4,448]{1,0:T(4,128)S(1)}, f32[256,448]{1,0:T(8,128)S(1)}) custom-call(bf16[168,256]{1,0:T(8,128)(2,1)S(1)} %get-tuple-element.60.refs_0_, bf16[112,256]{1,0:T(8,128)(2,1)S(1)} %get-tuple-element.65.refs_1_, bf16[112,256]{1,0:T(8,128)(2,1)S(1)} %get-tuple-element.68.refs_2_, ...), custom_call_target="tpu_custom_call" | custom-call | flops 359661568 | bytes 1032192 | tf_op jit(solution)/shard_map/pallas_call | solution.py:23
  44.0 2.1 %shard_map.121 = (f32[4,448]{1,0:T(4,128)S(1)}, f32[256,448]{1,0:T(8,128)S(1)}) custom-call(bf16[448,256]{1,0:T(8,128)(2,1)S(1)} %get-tuple-element.74.refs_0_.query_ref, f32[4,448]{1,0:T(4,128)S(1)} %get-tuple-element.75.refs_1_, f32[256,448]{1,0:T(8,128)S(1)} %get-tuple-element.76.refs_2_, bf16[168,512]{1,0:T(8,128)(2,1)S(1)} %collective-permute-done.17.refs_3_, ...), custom_call_target="tpu_custom_call" | custom-call | flops 359661568 | bytes 1498112 | tf_op jit(solution)/shard_map/pallas_call | solution.py:23
  46.2 1.8 %shard_map.122 = (bf16[64,1536]{1,0:T(8,128)(2,1)S(1)}, bf16[48,1536]{1,0:T(8,128)(2,1)S(1)}, bf16[64,1536]{1,0:T(8,128)(2,1)S(1)}, bf16[48,1536]{1,0:T(8,128)(2...) custom-call(bf16[448,256]{1,0:T(8,128)(2,1)S(1)} %get-tuple-element., ...), custom_call_target="tpu_custom_call" | custom-call | flops 704643072 | bytes 4070400 | tf_op jit(solution)/shard_map/pallas_call | solution.py:23
  52.2 2.6 %collective-permute-done.33 = bf16[48,1536]{1,0:T(8,128)(2,1)S(1)} collective-permute-done((bf16[48,1536]{1,0:T(8,128)(2,1)S(1)}, bf16[48,1536]{1,0:T(8,128)(2,1)S(1)}, u32[]{:S(2)}, u32[]{:S(2)}) %collective-permute-start.33) | collective-permute-done | bytes 147488 | tf_op jit(solution)/shard_map/ppermute | solution.py:432
  56.4 4.6 %collective-permute-done.36 = bf16[48,1536]{1,0:T(8,128)(2,1)S(1)} collective-permute-done((bf16[48,1536]{1,0:T(8,128)(2,1)S(1)}, bf16[48,1536]{1,0:T(8,128)(2,1)S(1)}, u32[]{:S(2)}, u32[]{:S(2)}) %collective-permute-start.36) | collective-permute-done | bytes 147488 | tf_op jit(solution)/shard_map/ppermute | solution.py:428
  61.6 1.6 %collective-permute-start.27 = (bf16[64,1536]{1,0:T(8,128)(2,1)S(1)}, bf16[64,1536]{1,0:T(8,128)(2,1)S(1)}, u32[]{:S(2)}, u32[]{:S(2)}) collective-permute-start(bf16[64,1536]{1,0:T(8,128)(2,1)S(1)} %add_convert_fusion.4), channel_id=1, source_target_pairs={{0,2},{2,4},{4,6},{6,7},{7,5},{5,3},{3,1},{1,0},{8,10},{10,12},{12... | collective-permute-start | bytes 589832 | tf_op jit(solution)/shard_map/ppermute | solution.py:427
  63.8 1.6 %collective-permute-start.35 = (bf16[48,1536]{1,0:T(8,128)(2,1)S(1)}, bf16[48,1536]{1,0:T(8,128)(2,1)S(1)}, u32[]{:S(2)}, u32[]{:S(2)}) collective-permute-start(bf16[48,1536]{1,0:T(8,128)(2,1)S(1)} %add_convert_fusion.8), channel_id=1, source_target_pairs={{0,2},{2,4},{4,6},{6,7},{7,5},{5,3},{3,1},{1,0},{8,10},{10,12},{12... | collective-permute-start | bytes 442376 | tf_op jit(solution)/shard_map/ppermute | solution.py:432
  65.5 2.3 %collective-permute-done.37 = bf16[48,1536]{1,0:T(8,128)(2,1)S(1)} collective-permute-done((bf16[48,1536]{1,0:T(8,128)(2,1)S(1)}, bf16[48,1536]{1,0:T(8,128)(2,1)S(1)}, u32[]{:S(2)}, u32[]{:S(2)}) %collective-permute-start.37) | collective-permute-done | bytes 147488 | tf_op jit(solution)/shard_map/ppermute | solution.py:428
  69.6 1.6 %collective-permute-start.28 = (bf16[64,1536]{1,0:T(8,128)(2,1)S(1)}, bf16[64,1536]{1,0:T(8,128)(2,1)S(1)}, u32[]{:S(2)}, u32[]{:S(2)}) collective-permute-start(bf16[64,1536]{1,0:T(8,128)(2,1)S(1)} %add_convert_fusion.3), channel_id=1, source_target_pairs={{0,2},{2,4},{4,6},{6,7},{7,5},{5,3},{3,1},{1,0},{8,10},{10,12},{12... | collective-permute-start | bytes 589832 | tf_op jit(solution)/shard_map/ppermute | solution.py:427
  72.5 3.1 %collective-permute-done.28 = bf16[64,1536]{1,0:T(8,128)(2,1)S(1)} collective-permute-done((bf16[64,1536]{1,0:T(8,128)(2,1)S(1)}, bf16[64,1536]{1,0:T(8,128)(2,1)S(1)}, u32[]{:S(2)}, u32[]{:S(2)}) %collective-permute-start.28) | collective-permute-done | bytes 196640 | tf_op jit(solution)/shard_map/ppermute | solution.py:427
  79.2 2.1 %collective-permute-done.29.fa_ref.fa = bf16[64,1536]{1,0:T(8,128)(2,1)S(1)} collective-permute-done((bf16[64,1536]{1,0:T(8,128)(2,1)S(1)}, bf16[64,1536]{1,0:T(8,128)(2,1)S(1)}, u32[]{:S(2)}, u32[]{:S(2)}) %collective-permute-start.29) | collective-permute-done | bytes 196640 | tf_op jit(solution)/shard_map/ppermute | solution.py:427
  83.4 2.5 %collective-permute-done.41.refs_2_ = bf16[8,3072]{1,0:T(8,128)(2,1)S(1)} collective-permute-done((bf16[8,3072]{1,0:T(8,128)(2,1)S(1)}, bf16[8,3072]{1,0:T(8,128)(2,1)S(1)}, u32[]{:S(2)}, u32[]{:S(2)}) %collective-permute-start.41) | collective-permute-done | bytes 49184 | tf_op jit(solution)/shard_map/ppermute | solution.py:44
  (88 shorter events, 32.3 us)
Async XLA Ops:
  2.1 8.9 %collective-permute-start.1 = (bf16[56,1536]{1,0:T(8,128)(2,1)S(1)}, bf16[56,1536]{1,0:T(8,128)(2,1)S(1)}, u32[]{:S(2)}, u32[]{:S(2)}) collective-permute-start(bf16[56,1536]{1,0:T(8,128)(2,1)S(1)} %get-tuple-element.53.refs_0_), channel_id=1, source_target_pairs={{0,2},{2,4},{4,6},{6,7},{7,5},{5,3},{3,1},{1,0},{8,10},{10,12},{12... | collective-permute-start | bytes 516104 | tf_op jit(solution)/shard_map/ppermute | solution.py:362
  5.2 7.9 %collective-permute-start.3 = (bf16[56,1536]{1,0:T(8,128)(2,1)S(1)}, bf16[56,1536]{1,0:T(8,128)(2,1)S(1)}, u32[]{:S(2)}, u32[]{:S(2)}) collective-permute-start(bf16[56,1536]{1,0:T(8,128)(2,1)S(1)} %get-tuple-element.52.refs_1_), channel_id=1, source_target_pairs={{2,0},{4,2},{6,4},{7,6},{5,7},{3,5},{1,3},{0,1},{10,8},{12,10},{14... | collective-permute-start | bytes 516104 | tf_op jit(solution)/shard_map/ppermute | solution.py:363
  5.2 8.5 %collective-permute-start = (bf16[56,1536]{1,0:T(8,128)(2,1)S(1)}, bf16[56,1536]{1,0:T(8,128)(2,1)S(1)}, u32[]{:S(2)}, u32[]{:S(2)}) collective-permute-start(bf16[56,1536]{1,0:T(8,128)(2,1)S(1)} %get-tuple-element.52.refs_1_), channel_id=1, source_target_pairs={{0,2},{2,4},{4,6},{6,7},{7,5},{5,3},{3,1},{1,0},{8,10},{10,12},{12... | collective-permute-start | bytes 516104 | tf_op jit(solution)/shard_map/ppermute | solution.py:367
  7.2 10.3 %collective-permute-start.2 = (bf16[56,1536]{1,0:T(8,128)(2,1)S(1)}, bf16[56,1536]{1,0:T(8,128)(2,1)S(1)}, u32[]{:S(2)}, u32[]{:S(2)}) collective-permute-start(bf16[56,1536]{1,0:T(8,128)(2,1)S(1)} %get-tuple-element.53.refs_0_), channel_id=1, source_target_pairs={{2,0},{4,2},{6,4},{7,6},{5,7},{3,5},{1,3},{0,1},{10,8},{12,10},{14... | collective-permute-start | bytes 516104 | tf_op jit(solution)/shard_map/ppermute | solution.py:368
  11.0 8.1 %collective-permute-start.4 = (bf16[56,1536]{1,0:T(8,128)(2,1)S(1)}, bf16[56,1536]{1,0:T(8,128)(2,1)S(1)}, u32[]{:S(2)}, u32[]{:S(2)}) collective-permute-start(bf16[56,1536]{1,0:T(8,128)(2,1)S(1)} %collective-permute-done.1.refs_2_), channel_id=1, source_target_pairs={{0,2},{2,4},{4,6},{6,7},{7,5},{5,3},{3,1},{1,0},{8,10},{10,12},{12... | collective-permute-start | bytes 516104 | tf_op jit(solution)/shard_map/ppermute | solution.py:362
  13.1 8.0 %collective-permute-start.7 = (bf16[56,1536]{1,0:T(8,128)(2,1)S(1)}, bf16[56,1536]{1,0:T(8,128)(2,1)S(1)}, u32[]{:S(2)}, u32[]{:S(2)}) collective-permute-start(bf16[56,1536]{1,0:T(8,128)(2,1)S(1)} %collective-permute-done.3.refs_5_), channel_id=1, source_target_pairs={{2,0},{4,2},{6,4},{7,6},{5,7},{3,5},{1,3},{0,1},{10,8},{12,10},{14... | collective-permute-start | bytes 516104 | tf_op jit(solution)/shard_map/ppermute | solution.py:363
  17.5 7.1 %collective-permute-start.6 = (bf16[56,1536]{1,0:T(8,128)(2,1)S(1)}, bf16[56,1536]{1,0:T(8,128)(2,1)S(1)}, u32[]{:S(2)}, u32[]{:S(2)}) collective-permute-start(bf16[56,1536]{1,0:T(8,128)(2,1)S(1)} %collective-permute-done.2.refs_4_), channel_id=1, source_target_pairs={{2,0},{4,2},{6,4},{7,6},{5,7},{3,5},{1,3},{0,1},{10,8},{12,10},{14... | collective-permute-start | bytes 516104 | tf_op jit(solution)/shard_map/ppermute | solution.py:368
  19.1 7.4 %collective-permute-start.8 = (bf16[56,1536]{1,0:T(8,128)(2,1)S(1)}, bf16[56,1536]{1,0:T(8,128)(2,1)S(1)}, u32[]{:S(2)}, u32[]{:S(2)}) collective-permute-start(bf16[56,1536]{1,0:T(8,128)(2,1)S(1)} %collective-permute-done.4.refs_0_), channel_id=1, source_target_pairs={{0,2},{2,4},{4,6},{6,7},{7,5},{5,3},{3,1},{1,0},{8,10},{10,12},{12... | collective-permute-start | bytes 516104 | tf_op jit(solution)/shard_map/ppermute | solution.py:362
  21.0 7.3 %collective-permute-start.11 = (bf16[56,1536]{1,0:T(8,128)(2,1)S(1)}, bf16[56,1536]{1,0:T(8,128)(2,1)S(1)}, u32[]{:S(2)}, u32[]{:S(2)}) collective-permute-start(bf16[56,1536]{1,0:T(8,128)(2,1)S(1)} %collective-permute-done.7.refs_3_), channel_id=1, source_target_pairs={{2,0},{4,2},{6,4},{7,6},{5,7},{3,5},{1,3},{0,1},{10,8},{12,10},{14... | collective-permute-start | bytes 516104 | tf_op jit(solution)/shard_map/ppermute | solution.py:363
  22.0 8.3 %collective-permute-start.9 = (bf16[56,1536]{1,0:T(8,128)(2,1)S(1)}, bf16[56,1536]{1,0:T(8,128)(2,1)S(1)}, u32[]{:S(2)}, u32[]{:S(2)}) collective-permute-start(bf16[56,1536]{1,0:T(8,128)(2,1)S(1)} %collective-permute-done.5.refs_1_), channel_id=1, source_target_pairs={{0,2},{2,4},{4,6},{6,7},{7,5},{5,3},{3,1},{1,0},{8,10},{10,12},{12... | collective-permute-start | bytes 516104 | tf_op jit(solution)/shard_map/ppermute | solution.py:367
  24.5 7.5 %collective-permute-start.10 = (bf16[56,1536]{1,0:T(8,128)(2,1)S(1)}, bf16[56,1536]{1,0:T(8,128)(2,1)S(1)}, u32[]{:S(2)}, u32[]{:S(2)}) collective-permute-start(bf16[56,1536]{1,0:T(8,128)(2,1)S(1)} %collective-permute-done.6.refs_2_), channel_id=1, source_target_pairs={{2,0},{4,2},{6,4},{7,6},{5,7},{3,5},{1,3},{0,1},{10,8},{12,10},{14... | collective-permute-start | bytes 516104 | tf_op jit(solution)/shard_map/ppermute | solution.py:368
  26.5 8.4 %collective-permute-start.12 = (bf16[56,1536]{1,0:T(8,128)(2,1)S(1)}, bf16[56,1536]{1,0:T(8,128)(2,1)S(1)}, u32[]{:S(2)}, u32[]{:S(2)}) collective-permute-start(bf16[56,1536]{1,0:T(8,128)(2,1)S(1)} %collective-permute-done.8.refs_0_), channel_id=1, source_target_pairs={{0,2},{2,4},{4,6},{6,7},{7,5},{5,3},{3,1},{1,0},{8,10},{10,12},{12... | collective-permute-start | bytes 516104 | tf_op jit(solution)/shard_map/ppermute | solution.py:362
  28.3 7.2 %collective-permute-start.13 = (bf16[56,1536]{1,0:T(8,128)(2,1)S(1)}, bf16[56,1536]{1,0:T(8,128)(2,1)S(1)}, u32[]{:S(2)}, u32[]{:S(2)}) collective-permute-start(bf16[56,1536]{1,0:T(8,128)(2,1)S(1)} %collective-permute-done.11.refs_3_), channel_id=1, source_target_pairs={{2,0},{4,2},{6,4},{7,6},{5,7},{3,5},{1,3},{0,1},{10,8},{12,10},{14... | collective-permute-start | bytes 516104 | tf_op jit(solution)/shard_map/ppermute | solution.py:363
  28.5 8.6 %collective-permute-start.17 = (bf16[168,512]{1,0:T(8,128)(2,1)S(1)}, bf16[168,512]{1,0:T(8,128)(2,1)S(1)}, u32[]{:S(2)}, u32[]{:S(2)}) collective-permute-start(bf16[168,512]{1,0:T(8,128)(2,1)S(1)} %get-tuple-element.71.refs_4_), channel_id=1, source_target_pairs={{0,16},{8,24},{16,0},{24,8},{1,17},{9,25},{17,1},{25,9},{2,18},{10... | collective-permute-start | bytes 516104 | tf_op jit(solution)/shard_map/ppermute | solution.py:44
  30.3 9.5 %collective-permute-start.14 = (bf16[168,512]{1,0:T(8,128)(2,1)S(1)}, bf16[168,512]{1,0:T(8,128)(2,1)S(1)}, u32[]{:S(2)}, u32[]{:S(2)}) collective-permute-start(bf16[168,512]{1,0:T(8,128)(2,1)S(1)} %get-tuple-element.71.refs_4_), channel_id=1, source_target_pairs={{0,8},{8,0},{16,24},{24,16},{1,9},{9,1},{17,25},{25,17},{2,10},{10... | collective-permute-start | bytes 516104 | tf_op jit(solution)/shard_map/ppermute | solution.py:44
  49.7 11.9 %collective-permute-start.26 = (bf16[64,1536]{1,0:T(8,128)(2,1)S(1)}, bf16[64,1536]{1,0:T(8,128)(2,1)S(1)}, u32[]{:S(2)}, u32[]{:S(2)}) collective-permute-start(bf16[64,1536]{1,0:T(8,128)(2,1)S(1)} %get-tuple-element.84), channel_id=1, source_target_pairs={{0,2},{2,4},{4,6},{6,7},{7,5},{5,3},{3,1},{1,0},{8,10},{10,12},{12... | collective-permute-start | bytes 589832 | tf_op jit(solution)/shard_map/ppermute | solution.py:427
  51.3 12.0 %collective-permute-start.30 = (bf16[64,1536]{1,0:T(8,128)(2,1)S(1)}, bf16[64,1536]{1,0:T(8,128)(2,1)S(1)}, u32[]{:S(2)}, u32[]{:S(2)}) collective-permute-start(bf16[64,1536]{1,0:T(8,128)(2,1)S(1)} %get-tuple-element.88), channel_id=1, source_target_pairs={{2,0},{4,2},{6,4},{7,6},{5,7},{3,5},{1,3},{0,1},{10,8},{12,10},{14... | collective-permute-start | bytes 589832 | tf_op jit(solution)/shard_map/ppermute | solution.py:433
  51.7 9.3 %collective-permute-start.36 = (bf16[48,1536]{1,0:T(8,128)(2,1)S(1)}, bf16[48,1536]{1,0:T(8,128)(2,1)S(1)}, u32[]{:S(2)}, u32[]{:S(2)}) collective-permute-start(bf16[48,1536]{1,0:T(8,128)(2,1)S(1)} %get-tuple-element.95), channel_id=1, source_target_pairs={{2,0},{4,2},{6,4},{7,6},{5,7},{3,5},{1,3},{0,1},{10,8},{12,10},{14... | collective-permute-start | bytes 442376 | tf_op jit(solution)/shard_map/ppermute | solution.py:428
  54.8 9.0 %collective-permute-start.34 = (bf16[48,1536]{1,0:T(8,128)(2,1)S(1)}, bf16[48,1536]{1,0:T(8,128)(2,1)S(1)}, u32[]{:S(2)}, u32[]{:S(2)}) collective-permute-start(bf16[48,1536]{1,0:T(8,128)(2,1)S(1)} %add_convert_fusion.9), channel_id=1, source_target_pairs={{0,2},{2,4},{4,6},{6,7},{7,5},{5,3},{3,1},{1,0},{8,10},{10,12},{12... | collective-permute-start | bytes 442376 | tf_op jit(solution)/shard_map/ppermute | solution.py:432
  61.6 7.9 %collective-permute-start.27 = (bf16[64,1536]{1,0:T(8,128)(2,1)S(1)}, bf16[64,1536]{1,0:T(8,128)(2,1)S(1)}, u32[]{:S(2)}, u32[]{:S(2)}) collective-permute-start(bf16[64,1536]{1,0:T(8,128)(2,1)S(1)} %add_convert_fusion.4), channel_id=1, source_target_pairs={{0,2},{2,4},{4,6},{6,7},{7,5},{5,3},{3,1},{1,0},{8,10},{10,12},{12... | collective-permute-start | bytes 589832 | tf_op jit(solution)/shard_map/ppermute | solution.py:427
  63.3 8.7 %collective-permute-start.31 = (bf16[64,1536]{1,0:T(8,128)(2,1)S(1)}, bf16[64,1536]{1,0:T(8,128)(2,1)S(1)}, u32[]{:S(2)}, u32[]{:S(2)}) collective-permute-start(bf16[64,1536]{1,0:T(8,128)(2,1)S(1)} %add_convert_fusion.1), channel_id=1, source_target_pairs={{2,0},{4,2},{6,4},{7,6},{5,7},{3,5},{1,3},{0,1},{10,8},{12,10},{14... | collective-permute-start | bytes 589832 | tf_op jit(solution)/shard_map/ppermute | solution.py:433
  63.8 19.5 %collective-permute-start.35 = (bf16[48,1536]{1,0:T(8,128)(2,1)S(1)}, bf16[48,1536]{1,0:T(8,128)(2,1)S(1)}, u32[]{:S(2)}, u32[]{:S(2)}) collective-permute-start(bf16[48,1536]{1,0:T(8,128)(2,1)S(1)} %add_convert_fusion.8), channel_id=1, source_target_pairs={{0,2},{2,4},{4,6},{6,7},{7,5},{5,3},{3,1},{1,0},{8,10},{10,12},{12... | collective-permute-start | bytes 442376 | tf_op jit(solution)/shard_map/ppermute | solution.py:432
  67.8 9.5 %collective-permute-start.38 = (bf16[48,1536]{1,0:T(8,128)(2,1)S(1)}, bf16[48,1536]{1,0:T(8,128)(2,1)S(1)}, u32[]{:S(2)}, u32[]{:S(2)}) collective-permute-start(bf16[48,1536]{1,0:T(8,128)(2,1)S(1)} %add_convert_fusion.6), channel_id=1, source_target_pairs={{2,0},{4,2},{6,4},{7,6},{5,7},{3,5},{1,3},{0,1},{10,8},{12,10},{14... | collective-permute-start | bytes 442376 | tf_op jit(solution)/shard_map/ppermute | solution.py:428
  72.0 7.2 %collective-permute-start.32 = (bf16[64,1536]{1,0:T(8,128)(2,1)S(1)}, bf16[64,1536]{1,0:T(8,128)(2,1)S(1)}, u32[]{:S(2)}, u32[]{:S(2)}) collective-permute-start(bf16[64,1536]{1,0:T(8,128)(2,1)S(1)} %add_convert_fusion), channel_id=1, source_target_pairs={{2,0},{4,2},{6,4},{7,6},{5,7},{3,5},{1,3},{0,1},{10,8},{12,10},{14... | collective-permute-start | bytes 589832 | tf_op jit(solution)/shard_map/ppermute | solution.py:433
  (21 other events, 169.2 us)

commit v3 on v2

--- a/solution.py
+++ b/solution.py
@@ -213,54 +213,41 @@
         start += size * video_rows
         text.append(rows_out[start : start + size * text_rows])
         start += size * text_rows
-    shards = [jnp.concatenate(rows, axis=0).astype(BF16) for rows in (video, text)]
-    put_partials([0] * sum(sizes), outs, shards, weights)
-
-
-def rest_kernel(sides, video_ref, text_ref, wv_ref, wt_ref, *outs):
-    put_partials(sides, outs, [video_ref[...], text_ref[...]], [wv_ref, wt_ref])
-
-
-def put_partials(sides, outs, heads, weights):
-    outs = list(outs)
-    half = outs[0].shape[1]
-    counts = [h.shape[0] // len(sides) for h in heads]
-    mixed = [
-        [jnp.dot(h, w[:, s * half : (s + 1) * half], preferred_element_type=F32) for s in range(2)]
-        for h, w in zip(heads, weights)
+    video, text = [jnp.concatenate(rows, axis=0).astype(BF16) for rows in (video, text)]
+    put_partials(outs, video, text, weights, sum(sizes))
+
+
+def put_partials(outs, video, text, weights, shards):
+    lead = outs[0].shape[1]
+    cuts = [slice(0, lead), slice(lead, weights[0].shape[1])]
+    vn, tn = video.shape[0] // shards, text.shape[0] // shards
+    left, right = [jnp.dot(video, weights[0][:, c], preferred_element_type=F32) for c in cuts]
+    bands = [
+        jnp.dot(text, weights[1][:, c : c + lead], preferred_element_type=F32)
+        for c in range(0, weights[1].shape[1], lead)
     ]
-    for i, side in enumerate(sides):
-        parts = [[y[i * n : (i + 1) * n] for y in ys] for n, ys in zip(counts, mixed)]
-        rows = [[y] for y in parts[0]]
-        if side is None:
-            rows.append(parts[1])
-        else:
-            rows[side] += parts[1]
-        for row in rows:
-            outs.pop(0)[...] = jnp.concatenate(row, axis=0).astype(BF16)
-
-
-def text_side(r, n):
-    return 0
+    for i in range(shards):
+        rows = [left[i * vn : (i + 1) * vn]] + [y[i * tn : (i + 1) * tn] for y in bands]
+        outs[2 * i][...] = jnp.concatenate(rows, axis=0).astype(BF16)
+        outs[2 * i + 1][...] = right[i * vn : (i + 1) * vn].astype(BF16)
 
 
 def close_text_kernel(fa_ref, ba_ref, own_ref, tmod_ref, text_ref):
-    text_rows = text_ref.shape[0]
-    half = own_ref.shape[1]
-    video_rows = own_ref.shape[0] - 2 * text_rows
-    total = sum(r[...].astype(F32)[video_rows:] for r in (fa_ref, ba_ref, own_ref))
-    for side in range(2):
-        columns = slice(side * half, (side + 1) * half)
+    text_rows, width = text_ref.shape
+    lead = own_ref.shape[1]
+    start = own_ref.shape[0] - text_rows * (width // lead)
+    total = sum(r[...].astype(F32)[start:] for r in (fa_ref, ba_ref, own_ref))
+    for band in range(width // lead):
+        columns = slice(band * lead, (band + 1) * lead)
         gate = tmod_ref[2:3, columns].astype(F32)
-        text_ref[:, columns] = (total[side * text_rows : (side + 1) * text_rows] * gate).astype(BF16)
+        text_ref[:, columns] = (total[band * text_rows : (band + 1) * text_rows] * gate).astype(BF16)
 
 
 def close_kernel(part_ref, fa, ba, own_a, fb, bb, own_b, vmod_ref, *refs):
     pieces, (video_ref, text_ref, wide) = refs[:-3], refs[-3:]
-    video_rows = video_ref.shape[0]
-    half = own_a.shape[1]
-    for side, arrivals in enumerate(((fa, ba, own_a), (fb, bb, own_b))):
-        columns = slice(side * half, (side + 1) * half)
+    video_rows, width = video_ref.shape
+    lead = own_a.shape[1]
+    for columns, arrivals in ((slice(0, lead), (fa, ba, own_a)), (slice(lead, width), (fb, bb, own_b))):
         total = sum(r[...].astype(F32)[:video_rows] for r in arrivals)
         video_ref[:, columns] = (total * vmod_ref[2:3, columns].astype(F32)).astype(BF16)
     rows = pieces[0].shape[0]
@@ -399,23 +386,20 @@
         16,
         flops=4 * total_rows * (total_rows - shard_rows) * (n_blk - 2) * cols,
     )
-    sides = [text_side(r, n_uly) for r in slots]
-    shapes = []
-    for side in sides:
-        rows = [video_rows, video_rows] + ([2 * text_rows] if side is None else [])
-        if side is not None:
-            rows[side] += 2 * text_rows
-        shapes.append([jax.ShapeDtypeStruct((n, half), BF16) for n in rows])
+    lead = width // 3
+    left_rows = video_rows + text_rows * (width // lead)
+    shapes = [
+        jax.ShapeDtypeStruct((left_rows, lead), BF16),
+        jax.ShapeDtypeStruct((video_rows, width - lead), BF16),
+    ]
     partial = call(
         functools.partial(finish_kernel, sizes, video_rows, with_text),
-        [shape for group in shapes for shape in group],
+        shapes * n_uly,
         [query, *carried] + pieces[-1] + ends[:2],
         16,
         flops=2 * total_rows * cols * width,
     )
-    mine = {}
-    for r, group in zip(slots, shapes):
-        mine[r], partial = partial[: len(group)], partial[len(group) :]
+    mine = {r: (partial[2 * i], partial[2 * i + 1]) for i, r in enumerate(slots)}
     mine[-reach] = mine[reach]
 
     def joined(arriving, own_part):

time: 87.6 us -> 82.5 us (0.942)
  waiting for transfers between devices: 27.1 us -> 22.1 us
    ppermute x8, waiting for transfers between devices: 6.86 us -> 2.73 us  [local(): bb = lax.ppermute(bb, 'uly', back)]
    ppermute x6, waiting for transfers between devices: 4.12 us -> 1.95 us  [local(): ba = lax.ppermute(ba, 'uly', back)]
    ppermute x3, waiting for transfers between devices: 2.62 us -> 4.56 us  [local(): fb = lax.ppermute(fb, 'uly', ahead)]
  transfers between devices with their start and end apart: 43 -> 43, of which waited for: 16 -> 15; matrix products, arithmetic and copies ran while one was open for 0% -> 1% of each run, Pallas kernels for 18% -> 19%
where the time goes in v3:
time: 82.5 us; the launch traced here: 82.4 us
  starting transfers between devices  39.2 us (48%)
  waiting for transfers between devices  22.1 us (27%)
  Pallas kernels  19.8 us (24%)
  between operations  0.89 us (1%)
    pallas_call x12, Pallas kernels, call(): pl.pallas_call(kernel, out_shape=outs, in_specs=[SMEM if i in smem else H...  19.8 us
    ppermute x4, starting transfers between devices, local(): fa = lax.ppermute(tied(fa, *due) if due else fa, 'uly', ahead)  8.91 us
    ppermute x15, starting transfers between devices, across(): return lax.ppermute(block, 'blk', [(i, i ^ distance) for i in range(n)])  8.82 us
    ppermute x4, starting transfers between devices, local(): fa = lax.ppermute(fa, 'uly', ahead)  6.51 us
    ppermute x3, starting transfers between devices, local(): fb = lax.ppermute(tied(fb, *due) if due else fb, 'uly', ahead)  6.22 us
    ppermute x4, waiting for transfers between devices, local(): fa = lax.ppermute(fa, 'uly', ahead)  5.76 us
    ppermute x15, waiting for transfers between devices, across(): return lax.ppermute(block, 'blk', [(i, i ^ distance) for i in range(n)])  5.08 us
    ppermute x3, starting transfers between devices, local(): fb = lax.ppermute(fb, 'uly', ahead)  4.84 us
  transfers between devices with their start and end apart: 43, of which 15 were waited for; matrix products, arithmetic and copies ran while one was open for 1% of the time, Pallas kernels for 19%

profile of v3, /device:TPU:0, one launch (start us, length us, event | category | flops | bytes accessed | tf_op | source)
XLA Modules:
  0.0 82.4 jit_solution(10928482074265356766)
XLA Ops:
  2.1 3.1 %collective-permute-start.1 = (bf16[56,1536]{1,0:T(8,128)(2,1)S(1)}, bf16[56,1536]{1,0:T(8,128)(2,1)S(1)}, u32[]{:S(2)}, u32[]{:S(2)}) collective-permute-start(bf16[56,1536]{1,0:T(8,128)(2,1)S(1)} %get-tuple-element.53.refs_0_), channel_id=1, source_target_pairs={{0,2},{2,4},{4,6},{6,7},{7,5},{5,3},{3,1},{1,0},{8,10},{10,12},{12... | collective-permute-start | bytes 516104 | tf_op jit(solution)/shard_map/ppermute | solution.py:349
  5.2 2.0 %collective-permute-start = (bf16[56,1536]{1,0:T(8,128)(2,1)S(1)}, bf16[56,1536]{1,0:T(8,128)(2,1)S(1)}, u32[]{:S(2)}, u32[]{:S(2)}) collective-permute-start(bf16[56,1536]{1,0:T(8,128)(2,1)S(1)} %get-tuple-element.52.refs_1_), channel_id=1, source_target_pairs={{0,2},{2,4},{4,6},{6,7},{7,5},{5,3},{3,1},{1,0},{8,10},{10,12},{12... | collective-permute-start | bytes 516104 | tf_op jit(solution)/shard_map/ppermute | solution.py:354
  7.2 3.8 %shard_map.114 = (bf16[3,3072,256]{2,1,0:T(8,128)(2,1)S(1)}, bf16[3,3072,256]{2,1,0:T(8,128)(2,1)S(1)}) custom-call(bf16[3,3072,256]{2,1,0:T(8,128)(2,1)} %bitcast.3, bf16[3,3072,256]{2,1,0:T(8,128)(2,1)} %bitcast.4), custom_call_target="tpu_custom_call" | custom-call | bytes 9437184 | tf_op jit(solution)/shard_map/pallas_call | solution.py:23
  11.0 2.1 %collective-permute-start.4 = (bf16[56,1536]{1,0:T(8,128)(2,1)S(1)}, bf16[56,1536]{1,0:T(8,128)(2,1)S(1)}, u32[]{:S(2)}, u32[]{:S(2)}) collective-permute-start(bf16[56,1536]{1,0:T(8,128)(2,1)S(1)} %collective-permute-done.1.refs_2_), channel_id=1, source_target_pairs={{0,2},{2,4},{4,6},{6,7},{7,5},{5,3},{3,1},{1,0},{8,10},{10,12},{12... | collective-permute-start | bytes 516104 | tf_op jit(solution)/shard_map/ppermute | solution.py:349
  13.6 1.9 %shard_map.115 = (bf16[256,3072]{1,0:T(8,128)(2,1)S(1)}, bf16[256,3072]{1,0:T(8,128)(2,1)S(1)}, f32[2,128]{1,0:T(2,128)S(1)}, f32[2,128]{1,0:T(2,128)S(1)}) custom-call(bf16[256,3072]{1,0:T(8,128)(2,1)} %refs_0_.2, bf16[256,3072]{1,0:T(8,128)(2,1)} %refs_1_.3, f32[2,128]{1,0:T(2,128)} %refs_2_.3, f32[2,128]{1,0:T(2,128)} %refs_3_.3), custom_call_target="tpu_custom_call" | custom-call | bytes 3147776 | tf_op jit(solution)/shard_map/pallas_call | solution.py:23
  15.6 1.9 %collective-permute-start.5 = (bf16[56,1536]{1,0:T(8,128)(2,1)S(1)}, bf16[56,1536]{1,0:T(8,128)(2,1)S(1)}, u32[]{:S(2)}, u32[]{:S(2)}) collective-permute-start(bf16[56,1536]{1,0:T(8,128)(2,1)S(1)} %collective-permute-done.refs_3_), channel_id=1, source_target_pairs={{0,2},{2,4},{4,6},{6,7},{7,5},{5,3},{3,1},{1,0},{8,10},{10,12},{12... | collective-permute-start | bytes 516104 | tf_op jit(solution)/shard_map/ppermute | solution.py:354
  19.1 1.9 %collective-permute-start.8 = (bf16[56,1536]{1,0:T(8,128)(2,1)S(1)}, bf16[56,1536]{1,0:T(8,128)(2,1)S(1)}, u32[]{:S(2)}, u32[]{:S(2)}) collective-permute-start(bf16[56,1536]{1,0:T(8,128)(2,1)S(1)} %collective-permute-done.4.refs_0_), channel_id=1, source_target_pairs={{0,2},{2,4},{4,6},{6,7},{7,5},{5,3},{3,1},{1,0},{8,10},{10,12},{12... | collective-permute-start | bytes 516104 | tf_op jit(solution)/shard_map/ppermute | solution.py:349
  22.0 2.3 %collective-permute-start.9 = (bf16[56,1536]{1,0:T(8,128)(2,1)S(1)}, bf16[56,1536]{1,0:T(8,128)(2,1)S(1)}, u32[]{:S(2)}, u32[]{:S(2)}) collective-permute-start(bf16[56,1536]{1,0:T(8,128)(2,1)S(1)} %collective-permute-done.5.refs_1_), channel_id=1, source_target_pairs={{0,2},{2,4},{4,6},{6,7},{7,5},{5,3},{3,1},{1,0},{8,10},{10,12},{12... | collective-permute-start | bytes 516104 | tf_op jit(solution)/shard_map/ppermute | solution.py:354
  26.5 1.9 %collective-permute-start.12 = (bf16[56,1536]{1,0:T(8,128)(2,1)S(1)}, bf16[56,1536]{1,0:T(8,128)(2,1)S(1)}, u32[]{:S(2)}, u32[]{:S(2)}) collective-permute-start(bf16[56,1536]{1,0:T(8,128)(2,1)S(1)} %collective-permute-done.8.refs_0_), channel_id=1, source_target_pairs={{0,2},{2,4},{4,6},{6,7},{7,5},{5,3},{3,1},{1,0},{8,10},{10,12},{12... | collective-permute-start | bytes 516104 | tf_op jit(solution)/shard_map/ppermute | solution.py:349
  28.5 1.8 %collective-permute-start.17 = (bf16[168,512]{1,0:T(8,128)(2,1)S(1)}, bf16[168,512]{1,0:T(8,128)(2,1)S(1)}, u32[]{:S(2)}, u32[]{:S(2)}) collective-permute-start(bf16[168,512]{1,0:T(8,128)(2,1)S(1)} %get-tuple-element.71.refs_4_), channel_id=1, source_target_pairs={{0,16},{8,24},{16,0},{24,8},{1,17},{9,25},{17,1},{25,9},{2,18},{10... | collective-permute-start | bytes 516104 | tf_op jit(solution)/shard_map/ppermute | solution.py:44
  30.3 1.7 %collective-permute-done.10.refs_2_ = bf16[56,1536]{1,0:T(8,128)(2,1)S(1)} collective-permute-done((bf16[56,1536]{1,0:T(8,128)(2,1)S(1)}, bf16[56,1536]{1,0:T(8,128)(2,1)S(1)}, u32[]{:S(2)}, u32[]{:S(2)}) %collective-permute-start.10) | collective-permute-done | bytes 172064 | tf_op jit(solution)/shard_map/ppermute | solution.py:355
  37.8 2.0 %collective-permute-done.19.refs_5_ = bf16[112,512]{1,0:T(8,128)(2,1)S(1)} collective-permute-done((bf16[112,512]{1,0:T(8,128)(2,1)S(1)}, bf16[112,512]{1,0:T(8,128)(2,1)S(1)}, u32[]{:S(2)}, u32[]{:S(2)}) %collective-permute-start.19) | collective-permute-done | bytes 114720 | tf_op jit(solution)/shard_map/ppermute | solution.py:44
  42.1 1.9 %shard_map.120 = (bf16[448,256]{1,0:T(8,128)(2,1)S(1)}, f32[4,448]{1,0:T(4,128)S(1)}, f32[256,448]{1,0:T(8,128)S(1)}) custom-call(bf16[168,256]{1,0:T(8,128)(2,1)S(1)} %get-tuple-element.60.refs_0_, bf16[112,256]{1,0:T(8,128)(2,1)S(1)} %get-tuple-element.65.refs_1_, bf16[112,256]{1,0:T(8,128)(2,1)S(1)} %get-tuple-element.68.refs_2_, ...), custom_call_target="tpu_custom_call" | custom-call | flops 359661568 | bytes 1032192 | tf_op jit(solution)/shard_map/pallas_call | solution.py:23
  44.0 2.1 %shard_map.121 = (f32[4,448]{1,0:T(4,128)S(1)}, f32[256,448]{1,0:T(8,128)S(1)}) custom-call(bf16[448,256]{1,0:T(8,128)(2,1)S(1)} %get-tuple-element.74.refs_0_.query_ref, f32[4,448]{1,0:T(4,128)S(1)} %get-tuple-element.75.refs_1_, f32[256,448]{1,0:T(8,128)S(1)} %get-tuple-element.76.refs_2_, bf16[168,512]{1,0:T(8,128)(2,1)S(1)} %collective-permute-done.17.refs_3_, ...), custom_call_target="tpu_custom_call" | custom-call | flops 359661568 | bytes 1498112 | tf_op jit(solution)/shard_map/pallas_call | solution.py:23
  46.2 1.8 %shard_map.122 = (bf16[72,1024]{1,0:T(8,128)(2,1)S(1)}, bf16[48,2048]{1,0:T(8,128)(2,1)S(1)}, bf16[72,1024]{1,0:T(8,128)(2,1)S(1)}, bf16[48,2048]{1,0:T(8,128)(2...) custom-call(bf16[448,256]{1,0:T(8,128)(2,1)S(1)} %get-tuple-element., ...), custom_call_target="tpu_custom_call" | custom-call | flops 704643072 | bytes 4070400 | tf_op jit(solution)/shard_map/pallas_call | solution.py:23
  52.2 2.6 %collective-permute-done.26 = bf16[72,1024]{1,0:T(8,128)(2,1)S(1)} collective-permute-done((bf16[72,1024]{1,0:T(8,128)(2,1)S(1)}, bf16[72,1024]{1,0:T(8,128)(2,1)S(1)}, u32[]{:S(2)}, u32[]{:S(2)}) %collective-permute-start.26) | collective-permute-done | bytes 147488 | tf_op jit(solution)/shard_map/ppermute | solution.py:411
  54.8 1.6 %collective-permute-start.27 = (bf16[72,1024]{1,0:T(8,128)(2,1)S(1)}, bf16[72,1024]{1,0:T(8,128)(2,1)S(1)}, u32[]{:S(2)}, u32[]{:S(2)}) collective-permute-start(bf16[72,1024]{1,0:T(8,128)(2,1)S(1)} %add_convert_fusion.9), channel_id=1, source_target_pairs={{0,2},{2,4},{4,6},{6,7},{7,5},{5,3},{3,1},{1,0},{8,10},{10,12},{12... | collective-permute-start | bytes 442376 | tf_op jit(solution)/shard_map/ppermute | solution.py:411
  57.0 2.0 %collective-permute-done.33 = bf16[48,2048]{1,0:T(8,128)(2,1)S(1)} collective-permute-done((bf16[48,2048]{1,0:T(8,128)(2,1)S(1)}, bf16[48,2048]{1,0:T(8,128)(2,1)S(1)}, u32[]{:S(2)}, u32[]{:S(2)}) %collective-permute-start.33) | collective-permute-done | bytes 196640 | tf_op jit(solution)/shard_map/ppermute | solution.py:416
  59.1 1.6 %collective-permute-start.34 = (bf16[48,2048]{1,0:T(8,128)(2,1)S(1)}, bf16[48,2048]{1,0:T(8,128)(2,1)S(1)}, u32[]{:S(2)}, u32[]{:S(2)}) collective-permute-start(bf16[48,2048]{1,0:T(8,128)(2,1)S(1)} %add_convert_fusion.4), channel_id=1, source_target_pairs={{0,2},{2,4},{4,6},{6,7},{7,5},{5,3},{3,1},{1,0},{8,10},{10,12},{12... | collective-permute-start | bytes 589832 | tf_op jit(solution)/shard_map/ppermute | solution.py:416
  62.2 1.6 %collective-permute-start.28 = (bf16[72,1024]{1,0:T(8,128)(2,1)S(1)}, bf16[72,1024]{1,0:T(8,128)(2,1)S(1)}, u32[]{:S(2)}, u32[]{:S(2)}) collective-permute-start(bf16[72,1024]{1,0:T(8,128)(2,1)S(1)} %add_convert_fusion.8), channel_id=1, source_target_pairs={{0,2},{2,4},{4,6},{6,7},{7,5},{5,3},{3,1},{1,0},{8,10},{10,12},{12... | collective-permute-start | bytes 442376 | tf_op jit(solution)/shard_map/ppermute | solution.py:411
  64.4 2.6 %collective-permute-done.34 = bf16[48,2048]{1,0:T(8,128)(2,1)S(1)} collective-permute-done((bf16[48,2048]{1,0:T(8,128)(2,1)S(1)}, bf16[48,2048]{1,0:T(8,128)(2,1)S(1)}, u32[]{:S(2)}, u32[]{:S(2)}) %collective-permute-start.34) | collective-permute-done | bytes 196640 | tf_op jit(solution)/shard_map/ppermute | solution.py:416
  67.0 1.6 %collective-permute-start.35 = (bf16[48,2048]{1,0:T(8,128)(2,1)S(1)}, bf16[48,2048]{1,0:T(8,128)(2,1)S(1)}, u32[]{:S(2)}, u32[]{:S(2)}) collective-permute-start(bf16[48,2048]{1,0:T(8,128)(2,1)S(1)} %add_convert_fusion.3), channel_id=1, source_target_pairs={{0,2},{2,4},{4,6},{6,7},{7,5},{5,3},{3,1},{1,0},{8,10},{10,12},{12... | collective-permute-start | bytes 589832 | tf_op jit(solution)/shard_map/ppermute | solution.py:416
  71.8 2.7 %collective-permute-done.38 = bf16[48,2048]{1,0:T(8,128)(2,1)S(1)} collective-permute-done((bf16[48,2048]{1,0:T(8,128)(2,1)S(1)}, bf16[48,2048]{1,0:T(8,128)(2,1)S(1)}, u32[]{:S(2)}, u32[]{:S(2)}) %collective-permute-start.38) | collective-permute-done | bytes 196640 | tf_op jit(solution)/shard_map/ppermute | solution.py:412
  78.3 2.5 %collective-permute-done.41.refs_2_ = bf16[8,3072]{1,0:T(8,128)(2,1)S(1)} collective-permute-done((bf16[8,3072]{1,0:T(8,128)(2,1)S(1)}, bf16[8,3072]{1,0:T(8,128)(2,1)S(1)}, u32[]{:S(2)}, u32[]{:S(2)}) %collective-permute-start.41) | collective-permute-done | bytes 49184 | tf_op jit(solution)/shard_map/ppermute | solution.py:44
  (88 shorter events, 30.4 us)
Async XLA Ops:
  2.1 8.9 %collective-permute-start.1 = (bf16[56,1536]{1,0:T(8,128)(2,1)S(1)}, bf16[56,1536]{1,0:T(8,128)(2,1)S(1)}, u32[]{:S(2)}, u32[]{:S(2)}) collective-permute-start(bf16[56,1536]{1,0:T(8,128)(2,1)S(1)} %get-tuple-element.53.refs_0_), channel_id=1, source_target_pairs={{0,2},{2,4},{4,6},{6,7},{7,5},{5,3},{3,1},{1,0},{8,10},{10,12},{12... | collective-permute-start | bytes 516104 | tf_op jit(solution)/shard_map/ppermute | solution.py:349
  5.2 7.9 %collective-permute-start.3 = (bf16[56,1536]{1,0:T(8,128)(2,1)S(1)}, bf16[56,1536]{1,0:T(8,128)(2,1)S(1)}, u32[]{:S(2)}, u32[]{:S(2)}) collective-permute-start(bf16[56,1536]{1,0:T(8,128)(2,1)S(1)} %get-tuple-element.52.refs_1_), channel_id=1, source_target_pairs={{2,0},{4,2},{6,4},{7,6},{5,7},{3,5},{1,3},{0,1},{10,8},{12,10},{14... | collective-permute-start | bytes 516104 | tf_op jit(solution)/shard_map/ppermute | solution.py:350
  5.2 8.5 %collective-permute-start = (bf16[56,1536]{1,0:T(8,128)(2,1)S(1)}, bf16[56,1536]{1,0:T(8,128)(2,1)S(1)}, u32[]{:S(2)}, u32[]{:S(2)}) collective-permute-start(bf16[56,1536]{1,0:T(8,128)(2,1)S(1)} %get-tuple-element.52.refs_1_), channel_id=1, source_target_pairs={{0,2},{2,4},{4,6},{6,7},{7,5},{5,3},{3,1},{1,0},{8,10},{10,12},{12... | collective-permute-start | bytes 516104 | tf_op jit(solution)/shard_map/ppermute | solution.py:354
  7.2 10.3 %collective-permute-start.2 = (bf16[56,1536]{1,0:T(8,128)(2,1)S(1)}, bf16[56,1536]{1,0:T(8,128)(2,1)S(1)}, u32[]{:S(2)}, u32[]{:S(2)}) collective-permute-start(bf16[56,1536]{1,0:T(8,128)(2,1)S(1)} %get-tuple-element.53.refs_0_), channel_id=1, source_target_pairs={{2,0},{4,2},{6,4},{7,6},{5,7},{3,5},{1,3},{0,1},{10,8},{12,10},{14... | collective-permute-start | bytes 516104 | tf_op jit(solution)/shard_map/ppermute | solution.py:355
  11.0 8.1 %collective-permute-start.4 = (bf16[56,1536]{1,0:T(8,128)(2,1)S(1)}, bf16[56,1536]{1,0:T(8,128)(2,1)S(1)}, u32[]{:S(2)}, u32[]{:S(2)}) collective-permute-start(bf16[56,1536]{1,0:T(8,128)(2,1)S(1)} %collective-permute-done.1.refs_2_), channel_id=1, source_target_pairs={{0,2},{2,4},{4,6},{6,7},{7,5},{5,3},{3,1},{1,0},{8,10},{10,12},{12... | collective-permute-start | bytes 516104 | tf_op jit(solution)/shard_map/ppermute | solution.py:349
  13.1 8.0 %collective-permute-start.7 = (bf16[56,1536]{1,0:T(8,128)(2,1)S(1)}, bf16[56,1536]{1,0:T(8,128)(2,1)S(1)}, u32[]{:S(2)}, u32[]{:S(2)}) collective-permute-start(bf16[56,1536]{1,0:T(8,128)(2,1)S(1)} %collective-permute-done.3.refs_5_), channel_id=1, source_target_pairs={{2,0},{4,2},{6,4},{7,6},{5,7},{3,5},{1,3},{0,1},{10,8},{12,10},{14... | collective-permute-start | bytes 516104 | tf_op jit(solution)/shard_map/ppermute | solution.py:350
  17.5 7.1 %collective-permute-start.6 = (bf16[56,1536]{1,0:T(8,128)(2,1)S(1)}, bf16[56,1536]{1,0:T(8,128)(2,1)S(1)}, u32[]{:S(2)}, u32[]{:S(2)}) collective-permute-start(bf16[56,1536]{1,0:T(8,128)(2,1)S(1)} %collective-permute-done.2.refs_4_), channel_id=1, source_target_pairs={{2,0},{4,2},{6,4},{7,6},{5,7},{3,5},{1,3},{0,1},{10,8},{12,10},{14... | collective-permute-start | bytes 516104 | tf_op jit(solution)/shard_map/ppermute | solution.py:355
  19.1 7.4 %collective-permute-start.8 = (bf16[56,1536]{1,0:T(8,128)(2,1)S(1)}, bf16[56,1536]{1,0:T(8,128)(2,1)S(1)}, u32[]{:S(2)}, u32[]{:S(2)}) collective-permute-start(bf16[56,1536]{1,0:T(8,128)(2,1)S(1)} %collective-permute-done.4.refs_0_), channel_id=1, source_target_pairs={{0,2},{2,4},{4,6},{6,7},{7,5},{5,3},{3,1},{1,0},{8,10},{10,12},{12... | collective-permute-start | bytes 516104 | tf_op jit(solution)/shard_map/ppermute | solution.py:349
  21.0 7.3 %collective-permute-start.11 = (bf16[56,1536]{1,0:T(8,128)(2,1)S(1)}, bf16[56,1536]{1,0:T(8,128)(2,1)S(1)}, u32[]{:S(2)}, u32[]{:S(2)}) collective-permute-start(bf16[56,1536]{1,0:T(8,128)(2,1)S(1)} %collective-permute-done.7.refs_3_), channel_id=1, source_target_pairs={{2,0},{4,2},{6,4},{7,6},{5,7},{3,5},{1,3},{0,1},{10,8},{12,10},{14... | collective-permute-start | bytes 516104 | tf_op jit(solution)/shard_map/ppermute | solution.py:350
  22.0 8.3 %collective-permute-start.9 = (bf16[56,1536]{1,0:T(8,128)(2,1)S(1)}, bf16[56,1536]{1,0:T(8,128)(2,1)S(1)}, u32[]{:S(2)}, u32[]{:S(2)}) collective-permute-start(bf16[56,1536]{1,0:T(8,128)(2,1)S(1)} %collective-permute-done.5.refs_1_), channel_id=1, source_target_pairs={{0,2},{2,4},{4,6},{6,7},{7,5},{5,3},{3,1},{1,0},{8,10},{10,12},{12... | collective-permute-start | bytes 516104 | tf_op jit(solution)/shard_map/ppermute | solution.py:354
  24.5 7.5 %collective-permute-start.10 = (bf16[56,1536]{1,0:T(8,128)(2,1)S(1)}, bf16[56,1536]{1,0:T(8,128)(2,1)S(1)}, u32[]{:S(2)}, u32[]{:S(2)}) collective-permute-start(bf16[56,1536]{1,0:T(8,128)(2,1)S(1)} %collective-permute-done.6.refs_2_), channel_id=1, source_target_pairs={{2,0},{4,2},{6,4},{7,6},{5,7},{3,5},{1,3},{0,1},{10,8},{12,10},{14... | collective-permute-start | bytes 516104 | tf_op jit(solution)/shard_map/ppermute | solution.py:355
  26.5 8.4 %collective-permute-start.12 = (bf16[56,1536]{1,0:T(8,128)(2,1)S(1)}, bf16[56,1536]{1,0:T(8,128)(2,1)S(1)}, u32[]{:S(2)}, u32[]{:S(2)}) collective-permute-start(bf16[56,1536]{1,0:T(8,128)(2,1)S(1)} %collective-permute-done.8.refs_0_), channel_id=1, source_target_pairs={{0,2},{2,4},{4,6},{6,7},{7,5},{5,3},{3,1},{1,0},{8,10},{10,12},{12... | collective-permute-start | bytes 516104 | tf_op jit(solution)/shard_map/ppermute | solution.py:349
  28.3 7.2 %collective-permute-start.13 = (bf16[56,1536]{1,0:T(8,128)(2,1)S(1)}, bf16[56,1536]{1,0:T(8,128)(2,1)S(1)}, u32[]{:S(2)}, u32[]{:S(2)}) collective-permute-start(bf16[56,1536]{1,0:T(8,128)(2,1)S(1)} %collective-permute-done.11.refs_3_), channel_id=1, source_target_pairs={{2,0},{4,2},{6,4},{7,6},{5,7},{3,5},{1,3},{0,1},{10,8},{12,10},{14... | collective-permute-start | bytes 516104 | tf_op jit(solution)/shard_map/ppermute | solution.py:350
  28.5 8.6 %collective-permute-start.17 = (bf16[168,512]{1,0:T(8,128)(2,1)S(1)}, bf16[168,512]{1,0:T(8,128)(2,1)S(1)}, u32[]{:S(2)}, u32[]{:S(2)}) collective-permute-start(bf16[168,512]{1,0:T(8,128)(2,1)S(1)} %get-tuple-element.71.refs_4_), channel_id=1, source_target_pairs={{0,16},{8,24},{16,0},{24,8},{1,17},{9,25},{17,1},{25,9},{2,18},{10... | collective-permute-start | bytes 516104 | tf_op jit(solution)/shard_map/ppermute | solution.py:44
  30.3 9.5 %collective-permute-start.14 = (bf16[168,512]{1,0:T(8,128)(2,1)S(1)}, bf16[168,512]{1,0:T(8,128)(2,1)S(1)}, u32[]{:S(2)}, u32[]{:S(2)}) collective-permute-start(bf16[168,512]{1,0:T(8,128)(2,1)S(1)} %get-tuple-element.71.refs_4_), channel_id=1, source_target_pairs={{0,8},{8,0},{16,24},{24,16},{1,9},{9,1},{17,25},{25,17},{2,10},{10... | collective-permute-start | bytes 516104 | tf_op jit(solution)/shard_map/ppermute | solution.py:44
  50.1 8.9 %collective-permute-start.33 = (bf16[48,2048]{1,0:T(8,128)(2,1)S(1)}, bf16[48,2048]{1,0:T(8,128)(2,1)S(1)}, u32[]{:S(2)}, u32[]{:S(2)}) collective-permute-start(bf16[48,2048]{1,0:T(8,128)(2,1)S(1)} %get-tuple-element.92), channel_id=1, source_target_pairs={{0,2},{2,4},{4,6},{6,7},{7,5},{5,3},{3,1},{1,0},{8,10},{10,12},{12... | collective-permute-start | bytes 589832 | tf_op jit(solution)/shard_map/ppermute | solution.py:416
  51.7 9.0 %collective-permute-start.36 = (bf16[48,2048]{1,0:T(8,128)(2,1)S(1)}, bf16[48,2048]{1,0:T(8,128)(2,1)S(1)}, u32[]{:S(2)}, u32[]{:S(2)}) collective-permute-start(bf16[48,2048]{1,0:T(8,128)(2,1)S(1)} %get-tuple-element.95), channel_id=1, source_target_pairs={{2,0},{4,2},{6,4},{7,6},{5,7},{3,5},{1,3},{0,1},{10,8},{12,10},{14... | collective-permute-start | bytes 589832 | tf_op jit(solution)/shard_map/ppermute | solution.py:412
  54.8 7.3 %collective-permute-start.27 = (bf16[72,1024]{1,0:T(8,128)(2,1)S(1)}, bf16[72,1024]{1,0:T(8,128)(2,1)S(1)}, u32[]{:S(2)}, u32[]{:S(2)}) collective-permute-start(bf16[72,1024]{1,0:T(8,128)(2,1)S(1)} %add_convert_fusion.9), channel_id=1, source_target_pairs={{0,2},{2,4},{4,6},{6,7},{7,5},{5,3},{3,1},{1,0},{8,10},{10,12},{12... | collective-permute-start | bytes 442376 | tf_op jit(solution)/shard_map/ppermute | solution.py:411
  56.5 7.3 %collective-permute-start.31 = (bf16[72,1024]{1,0:T(8,128)(2,1)S(1)}, bf16[72,1024]{1,0:T(8,128)(2,1)S(1)}, u32[]{:S(2)}, u32[]{:S(2)}) collective-permute-start(bf16[72,1024]{1,0:T(8,128)(2,1)S(1)} %add_convert_fusion.6), channel_id=1, source_target_pairs={{2,0},{4,2},{6,4},{7,6},{5,7},{3,5},{1,3},{0,1},{10,8},{12,10},{14... | collective-permute-start | bytes 442376 | tf_op jit(solution)/shard_map/ppermute | solution.py:417
  59.1 7.9 %collective-permute-start.34 = (bf16[48,2048]{1,0:T(8,128)(2,1)S(1)}, bf16[48,2048]{1,0:T(8,128)(2,1)S(1)}, u32[]{:S(2)}, u32[]{:S(2)}) collective-permute-start(bf16[48,2048]{1,0:T(8,128)(2,1)S(1)} %add_convert_fusion.4), channel_id=1, source_target_pairs={{0,2},{2,4},{4,6},{6,7},{7,5},{5,3},{3,1},{1,0},{8,10},{10,12},{12... | collective-permute-start | bytes 589832 | tf_op jit(solution)/shard_map/ppermute | solution.py:416
  60.7 7.9 %collective-permute-start.37 = (bf16[48,2048]{1,0:T(8,128)(2,1)S(1)}, bf16[48,2048]{1,0:T(8,128)(2,1)S(1)}, u32[]{:S(2)}, u32[]{:S(2)}) collective-permute-start(bf16[48,2048]{1,0:T(8,128)(2,1)S(1)} %add_convert_fusion.2), channel_id=1, source_target_pairs={{2,0},{4,2},{6,4},{7,6},{5,7},{3,5},{1,3},{0,1},{10,8},{12,10},{14... | collective-permute-start | bytes 589832 | tf_op jit(solution)/shard_map/ppermute | solution.py:412
  62.2 7.9 %collective-permute-start.28 = (bf16[72,1024]{1,0:T(8,128)(2,1)S(1)}, bf16[72,1024]{1,0:T(8,128)(2,1)S(1)}, u32[]{:S(2)}, u32[]{:S(2)}) collective-permute-start(bf16[72,1024]{1,0:T(8,128)(2,1)S(1)} %add_convert_fusion.8), channel_id=1, source_target_pairs={{0,2},{2,4},{4,6},{6,7},{7,5},{5,3},{3,1},{1,0},{8,10},{10,12},{12... | collective-permute-start | bytes 442376 | tf_op jit(solution)/shard_map/ppermute | solution.py:411
  63.9 11.2 %collective-permute-start.32 = (bf16[72,1024]{1,0:T(8,128)(2,1)S(1)}, bf16[72,1024]{1,0:T(8,128)(2,1)S(1)}, u32[]{:S(2)}, u32[]{:S(2)}) collective-permute-start(bf16[72,1024]{1,0:T(8,128)(2,1)S(1)} %add_convert_fusion.5), channel_id=1, source_target_pairs={{2,0},{4,2},{6,4},{7,6},{5,7},{3,5},{1,3},{0,1},{10,8},{12,10},{14... | collective-permute-start | bytes 442376 | tf_op jit(solution)/shard_map/ppermute | solution.py:417
  67.0 11.3 %collective-permute-start.35 = (bf16[48,2048]{1,0:T(8,128)(2,1)S(1)}, bf16[48,2048]{1,0:T(8,128)(2,1)S(1)}, u32[]{:S(2)}, u32[]{:S(2)}) collective-permute-start(bf16[48,2048]{1,0:T(8,128)(2,1)S(1)} %add_convert_fusion.3), channel_id=1, source_target_pairs={{0,2},{2,4},{4,6},{6,7},{7,5},{5,3},{3,1},{1,0},{8,10},{10,12},{12... | collective-permute-start | bytes 589832 | tf_op jit(solution)/shard_map/ppermute | solution.py:416
  (21 other events, 160.3 us)

commit v4 on v3

--- a/solution.py
+++ b/solution.py
@@ -35,8 +35,7 @@
     n = lax.axis_size(axis)
     order = list(range(0, n, 2)) + list(range(1, n, 2))[::-1]
     ahead = [(order[i], order[(i + 1) % n]) for i in range(n)]
-    across_ring = [(order[i], order[(i + n // 2) % n]) for i in range(n)]
-    return ahead, [(b, a) for a, b in ahead], across_ring
+    return ahead, [(b, a) for a, b in ahead]
 
 
 def across(block, distance):
@@ -78,14 +77,17 @@
     right_ref[...] = both[:, half:]
 
 
-def fetch_kernel(count, *refs):
-    many = (len(refs) - 1) // 2
-    sources, landed, sems = refs[:many], refs[many : 2 * many], refs[-1]
-    if count:
-        step = sources[0].shape[1] // count
-        sources = [s.at[:, i * step : (i + 1) * step, :] for s in sources for i in range(count)]
-        landed = [s.at[:, i * step : (i + 1) * step, :] for s in landed for i in range(count)]
-    copies = [pltpu.make_async_copy(s, d, sems.at[i]) for i, (s, d) in enumerate(zip(sources, landed))]
+def bands(array, count):
+    step = array.shape[-2] // count
+    return [array.at[..., i * step : (i + 1) * step, :] for i in range(count)]
+
+
+def fetch_kernel(counts, *refs):
+    many = len(counts)
+    copies = []
+    for source, landed, count in zip(refs[:many], refs[many : 2 * many], counts):
+        for pair in zip(bands(source, count), bands(landed, count)):
+            copies.append(pltpu.make_async_copy(*pair, refs[-1].at[len(copies)]))
     for copy in copies:
         copy.start()
     for copy in copies:
@@ -174,22 +176,25 @@
     ]
 
 
-def attend_kernel(sizes, video_rows, with_text, fresh, queries, *refs):
-    groups, sources = len(sizes), len(with_text)
-    query = wide_rows(refs[:queries], [r.shape[0] for r in refs[:queries]])
-    refs = refs[queries:]
-    state = []
-    if not fresh:
-        state = load_state(*refs[:2])
-        refs = refs[2:]
-    pieces, outs = refs[: groups * sources], refs[groups * sources :]
-    if fresh:
-        outs[0][...] = query
-    stats_ref, sums_ref = outs[-2:]
-    for s in range(sources):
-        held = pieces[s * groups : (s + 1) * groups]
-        counts = [p.shape[0] if with_text[s] else n * video_rows for p, n in zip(held, sizes)]
+def absorb_blocks(state, query, blocks, pieces):
+    start = 0
+    for counts in blocks:
+        held = pieces[start : start + len(counts)]
         state = absorbed(state, query, wide_rows(held, counts))
+        start += len(counts)
+    return state
+
+
+def attend_kernel(blocks, queries, *refs):
+    if queries:
+        query = wide_rows(refs[:queries], [r.shape[0] for r in refs[:queries]])
+        pieces, (query_ref, stats_ref, sums_ref) = refs[queries:-3], refs[-3:]
+        query_ref[...] = query
+        state = absorb_blocks([], query, blocks, pieces)
+    else:
+        query, state = refs[0][...], load_state(*refs[1:3])
+        pieces, (stats_ref, sums_ref) = refs[3:-2], refs[-2:]
+        state = absorb_blocks(state, query, blocks, pieces)
     heads = len(state)
     for h, (highest, totals, sums) in enumerate(state):
         stats_ref[h : h + 1, :] = highest
@@ -197,12 +202,10 @@
         sums_ref[h * HD : (h + 1) * HD, :] = sums
 
 
-def finish_kernel(sizes, video_rows, with_text, query_ref, stats_ref, sums_ref, *refs):
-    sources = len(with_text)
-    pieces, weights = refs[:sources], refs[sources : sources + 2]
-    outs = refs[sources + 2 :]
-    counts = [p.shape[0] if w else sizes[-1] * video_rows for p, w in zip(pieces, with_text)]
-    state = absorbed(load_state(stats_ref, sums_ref), query_ref[...], wide_rows(pieces, counts))
+def finish_kernel(blocks, sizes, video_rows, query_ref, stats_ref, sums_ref, *refs):
+    held = sum(len(counts) for counts in blocks)
+    pieces, weights, outs = refs[:held], refs[held : held + 2], refs[held + 2 :]
+    state = absorb_blocks(load_state(stats_ref, sums_ref), query_ref[...], blocks, pieces)
     flat = jnp.concatenate([sums / totals for _, totals, sums in state], axis=0)
     rows_out = jnp.transpose(flat)
     text_rows = rows_out.shape[0] // sum(sizes) - video_rows
@@ -271,7 +274,7 @@
 ):
     n_blk, n_uly = lax.axis_size("blk"), lax.axis_size("uly")
     reach = n_uly // 2
-    ahead, back, opposite = ring_routes("uly")
+    ahead, back = ring_routes("uly")
     video_rows, width = video_tokens.shape
     half = width // 2
     parts = math.gcd(n_blk, text_tokens.shape[0] // 8)
@@ -292,27 +295,30 @@
         hbm=(1, 2, 3, 4),
     )
 
-    def fetched(arrays, after, count=0):
+    def fetched(arrays, counts, after):
         arrays = [tied(arrays[0], after), *arrays[1:]]
         return call(
-            functools.partial(fetch_kernel, count),
+            functools.partial(fetch_kernel, counts),
             [jax.ShapeDtypeStruct(a.shape, a.dtype) for a in arrays],
             arrays,
             1,
-            [pltpu.SemaphoreType.DMA((len(arrays) * max(count, 1),))],
+            [pltpu.SemaphoreType.DMA((sum(counts),))],
             hbm=range(len(arrays)),
         )
 
-    weights = [jnp.transpose(p, (1, 0, 2)) for p in (video_projection, text_projection)]
-    held, ends, waiting = [], [], []
+    weights, gains, ends = [], [], []
+    waiting = []
     queries, pieces, groups = [], [], []
 
-    def fetch_all(after):
-        held.extend(fetched(weights, after, 4))
-        return held[-1]
-
-    def fetch_rest(after):
-        ends.extend(fetched([video_output, text_output, video_gains, text_gains], after))
+    def fetch_first(after):
+        held = [jnp.transpose(p, (1, 0, 2)) for p in (video_projection, text_projection)]
+        *held, vgains, tgains = fetched([*held, video_gains, text_gains], [4, 4, 1, 1], after)
+        weights.extend(held)
+        gains.extend((vgains, tgains))
+        return held[0]
+
+    def fetch_last(after):
+        ends.extend(fetched([video_output, text_output], [2, 2], after))
         return ends[0]
 
     def project(after, direct=False):
@@ -326,7 +332,7 @@
                 jax.ShapeDtypeStruct((rows, cols), BF16),
                 jax.ShapeDtypeStruct((rows, 2 * cols), BF16),
             ],
-            [tied(chunks[0], after), *chunks[1:], *held, *ends[2:]],
+            [tied(chunks[0], after), *chunks[1:], *weights, *gains],
             12,
             flops=2 * rows * width * 3 * cols,
         )
@@ -339,7 +345,7 @@
         groups.append(group)
         return q
 
-    beside = {(1, 1): [fetch_all], (2, 0): [fetch_rest], (2, 1): [project], (3, 1): [project], (4, 1): [project]}
+    beside = {(1, 1): [fetch_first], (2, 1): [project], (3, 1): [project], (4, 1): [project]}
     fa, fb = own
     ba, bb = own
     waiting.append((0, *own))
@@ -360,44 +366,63 @@
             waiting += [(reach, fa, bb)]
             project(fa, True)
 
+    def second_leg(spread, after):
+        for d in range(3, n_blk, 2):
+            if isinstance(spread, dict):
+                spread[d] = across(tied(spread[d - 1], after), 1)
+
     for spread in pieces[:-1]:
-        for d in range(3, n_blk, 2):
-            spread[d] = across(tied(spread[d - 1], queries[-1]), 1)
-
+        second_leg(spread, queries[-1])
     sizes = [len(g) for g in groups]
     slots = [r for group in groups for r, *_ in group]
     total_rows = shard_rows * n_uly
-    with_text = [d < parts for d in range(n_blk)]
+
+    def some(sources, chosen):
+        return [
+            [(pieces[g][d], sizes[g] * (shard_rows if d < parts else video_rows)) for g in chosen]
+            for d in sources
+        ]
+
+    def attended(blocks, given, queries, kernel, outs, extra=(), more=0):
+        counts = [[n for _, n in block] for block in blocks]
+        keys = [piece for block in blocks for piece, _ in block]
+        return call(
+            functools.partial(kernel, counts, *queries),
+            outs,
+            [*given, *keys, *extra],
+            16,
+            flops=4 * total_rows * sum(map(sum, counts)) * cols + more,
+        )
+
     state = [
         jax.ShapeDtypeStruct((2 * cols // HD, total_rows), F32),
         jax.ShapeDtypeStruct((cols, total_rows), F32),
     ]
-    query, *carried = call(
-        functools.partial(attend_kernel, sizes[:-1], video_rows, with_text[:2], True, len(queries)),
+    first = range(len(groups) - 1)
+    outer = range(2, n_blk)
+    query, *carried = attended(
+        some((0, 1), first),
+        queries,
+        (len(queries),),
+        attend_kernel,
         [jax.ShapeDtypeStruct((total_rows, cols), BF16), *state],
-        queries + [spread[d] for d in range(2) for spread in pieces[:-1]],
-        16,
-        flops=8 * total_rows * (total_rows - shard_rows) * cols,
-    )
-    carried = call(
-        functools.partial(attend_kernel, sizes[:-1], video_rows, with_text[2:], False, 1),
-        state,
-        [query, *carried] + [spread[d] for d in range(2, n_blk) for spread in pieces[:-1]],
-        16,
-        flops=4 * total_rows * (total_rows - shard_rows) * (n_blk - 2) * cols,
-    )
+    )
+    carried = attended(some(outer, first[:-1]), [query, *carried], (0,), attend_kernel, state)
     lead = width // 3
     left_rows = video_rows + text_rows * (width // lead)
     shapes = [
         jax.ShapeDtypeStruct((left_rows, lead), BF16),
         jax.ShapeDtypeStruct((video_rows, width - lead), BF16),
     ]
-    partial = call(
-        functools.partial(finish_kernel, sizes, video_rows, with_text),
+    last = [piece for block in some(outer, first[-1:]) + some(range(n_blk), (len(groups) - 1,)) for piece in block]
+    partial = attended(
+        [last],
+        [query, *carried],
+        (sizes, video_rows),
+        finish_kernel,
         shapes * n_uly,
-        [query, *carried] + pieces[-1] + ends[:2],
-        16,
-        flops=2 * total_rows * cols * width,
+        (video_output, text_output),
+        2 * total_rows * cols * width,
     )
     mine = {r: (partial[2 * i], partial[2 * i + 1]) for i, r in enumerate(slots)}
     mine[-reach] = mine[reach]

time: 82.5 us -> 80.8 us (0.979)
  Pallas kernels: 19.8 us -> 18.1 us
  waiting for transfers between devices: 22.1 us -> 20.7 us
  starting transfers between devices: 39.2 us -> 40.6 us
    ppermute x6, waiting for transfers between devices: 1.95 us -> 0.02 us  [local(): ba = lax.ppermute(ba, 'uly', back)]
    pallas_call x12 -> x11, Pallas kernels: 19.8 us -> 18.1 us  [call(): pl.pallas_call(kernel, out_shape=outs, in_specs=[SMEM if i in smem else H...]
    ppermute x15, starting transfers between devices: 8.82 us -> 10.4 us  [across(): return lax.ppermute(block, 'blk', [(i, i ^ distance) for i in range(n)])]
    ppermute x15, waiting for transfers between devices: 5.08 us -> 3.9 us  [across(): return lax.ppermute(block, 'blk', [(i, i ^ distance) for i in range(n)])]
    ppermute x4, waiting for transfers between devices: 0.59 us -> 1.57 us  [local(): fa = lax.ppermute(tied(fa, *due) if due else fa, 'uly', ahead)]
  transfers between devices with their start and end apart: 43 -> 43, of which waited for: 15 -> 14; matrix products, arithmetic and copies ran while one was open for 1% -> 1% of each run, Pallas kernels for 19% -> 17%
where the time goes in v4:
time: 80.8 us; the launch traced here: 80.6 us
  starting transfers between devices  40.6 us (50%)
  waiting for transfers between devices  20.7 us (26%)
  Pallas kernels  18.1 us (22%)
  between operations  0.89 us (1%)
    pallas_call x11, Pallas kernels, call(): pl.pallas_call(kernel, out_shape=outs, in_specs=[SMEM if i in smem else H...  18.1 us
    ppermute x15, starting transfers between devices, across(): return lax.ppermute(block, 'blk', [(i, i ^ distance) for i in range(n)])  10.4 us
    ppermute x4, starting transfers between devices, local(): fa = lax.ppermute(tied(fa, *due) if due else fa, 'uly', ahead)  9.18 us
    ppermute x4, starting transfers between devices, local(): fa = lax.ppermute(fa, 'uly', ahead)  6.52 us
    ppermute x3, starting transfers between devices, local(): fb = lax.ppermute(tied(fb, *due) if due else fb, 'uly', ahead)  5.89 us
    ppermute x4, waiting for transfers between devices, local(): fa = lax.ppermute(fa, 'uly', ahead)  5.76 us
    ppermute x3, starting transfers between devices, local(): fb = lax.ppermute(fb, 'uly', ahead)  4.84 us
    ppermute x3, waiting for transfers between devices, local(): fb = lax.ppermute(fb, 'uly', ahead)  4.56 us
  transfers between devices with their start and end apart: 43, of which 14 were waited for; matrix products, arithmetic and copies ran while one was open for 1% of the time, Pallas kernels for 17%

profile of v4, /device:TPU:0, one launch (start us, length us, event | category | flops | bytes accessed | tf_op | source)
XLA Modules:
  0.0 80.6 jit_solution(6153926176106373631)
XLA Ops:
  2.1 3.1 %collective-permute-start.1 = (bf16[56,1536]{1,0:T(8,128)(2,1)S(1)}, bf16[56,1536]{1,0:T(8,128)(2,1)S(1)}, u32[]{:S(2)}, u32[]{:S(2)}) collective-permute-start(bf16[56,1536]{1,0:T(8,128)(2,1)S(1)} %get-tuple-element.49.refs_0_), channel_id=1, source_target_pairs={{0,2},{2,4},{4,6},{6,7},{7,5},{5,3},{3,1},{1,0},{8,10},{10,12},{12... | collective-permute-start | bytes 516104 | tf_op jit(solution)/shard_map/ppermute | solution.py:355
  5.2 2.0 %collective-permute-start = (bf16[56,1536]{1,0:T(8,128)(2,1)S(1)}, bf16[56,1536]{1,0:T(8,128)(2,1)S(1)}, u32[]{:S(2)}, u32[]{:S(2)}) collective-permute-start(bf16[56,1536]{1,0:T(8,128)(2,1)S(1)} %get-tuple-element.48.refs_1_), channel_id=1, source_target_pairs={{0,2},{2,4},{4,6},{6,7},{7,5},{5,3},{3,1},{1,0},{8,10},{10,12},{12... | collective-permute-start | bytes 516104 | tf_op jit(solution)/shard_map/ppermute | solution.py:360
  7.2 3.8 %shard_map.114 = (bf16[3,3072,256]{2,1,0:T(8,128)(2,1)S(1)}, bf16[3,3072,256]{2,1,0:T(8,128)(2,1)S(1)}, f32[2,128]{1,0:T(2,128)S(1)}, f32[2,128]{1,0:T(2,128)S(1)}) custom-call(bf16[3,3072,256]{2,1,0:T(8,128)(2,1)} %bitcast.3, bf16[3,3072,256]{2,1,0:T(8,128)(2,1)} %bitcast.4, f32[2,128]{1,0:T(2,128)} %refs_2_.3, f32[2,128]{1,0:T(2,128)} %refs_3_.3), custom_call_target="tpu_custom_call" | custom-call | bytes 9439232 | tf_op jit(solution)/shard_map/pallas_call | solution.py:23
  11.0 2.1 %collective-permute-start.4 = (bf16[56,1536]{1,0:T(8,128)(2,1)S(1)}, bf16[56,1536]{1,0:T(8,128)(2,1)S(1)}, u32[]{:S(2)}, u32[]{:S(2)}) collective-permute-start(bf16[56,1536]{1,0:T(8,128)(2,1)S(1)} %collective-permute-done.1.refs_2_), channel_id=1, source_target_pairs={{0,2},{2,4},{4,6},{6,7},{7,5},{5,3},{3,1},{1,0},{8,10},{10,12},{12... | collective-permute-start | bytes 516104 | tf_op jit(solution)/shard_map/ppermute | solution.py:355
  13.6 1.9 %collective-permute-start.5 = (bf16[56,1536]{1,0:T(8,128)(2,1)S(1)}, bf16[56,1536]{1,0:T(8,128)(2,1)S(1)}, u32[]{:S(2)}, u32[]{:S(2)}) collective-permute-start(bf16[56,1536]{1,0:T(8,128)(2,1)S(1)} %collective-permute-done.refs_3_), channel_id=1, source_target_pairs={{0,2},{2,4},{4,6},{6,7},{7,5},{5,3},{3,1},{1,0},{8,10},{10,12},{12... | collective-permute-start | bytes 516104 | tf_op jit(solution)/shard_map/ppermute | solution.py:360
  18.4 2.0 %collective-permute-start.8 = (bf16[56,1536]{1,0:T(8,128)(2,1)S(1)}, bf16[56,1536]{1,0:T(8,128)(2,1)S(1)}, u32[]{:S(2)}, u32[]{:S(2)}) collective-permute-start(bf16[56,1536]{1,0:T(8,128)(2,1)S(1)} %collective-permute-done.4.refs_0_), channel_id=1, source_target_pairs={{0,2},{2,4},{4,6},{6,7},{7,5},{5,3},{3,1},{1,0},{8,10},{10,12},{12... | collective-permute-start | bytes 516104 | tf_op jit(solution)/shard_map/ppermute | solution.py:355
  20.4 1.6 %collective-permute-done.5.refs_1_ = bf16[56,1536]{1,0:T(8,128)(2,1)S(1)} collective-permute-done((bf16[56,1536]{1,0:T(8,128)(2,1)S(1)}, bf16[56,1536]{1,0:T(8,128)(2,1)S(1)}, u32[]{:S(2)}, u32[]{:S(2)}) %collective-permute-start.5) | collective-permute-done | bytes 172064 | tf_op jit(solution)/shard_map/ppermute | solution.py:360
  22.1 2.0 %collective-permute-start.9 = (bf16[56,1536]{1,0:T(8,128)(2,1)S(1)}, bf16[56,1536]{1,0:T(8,128)(2,1)S(1)}, u32[]{:S(2)}, u32[]{:S(2)}) collective-permute-start(bf16[56,1536]{1,0:T(8,128)(2,1)S(1)} %collective-permute-done.5.refs_1_), channel_id=1, source_target_pairs={{0,2},{2,4},{4,6},{6,7},{7,5},{5,3},{3,1},{1,0},{8,10},{10,12},{12... | collective-permute-start | bytes 516104 | tf_op jit(solution)/shard_map/ppermute | solution.py:360
  25.8 2.0 %collective-permute-start.12 = (bf16[56,1536]{1,0:T(8,128)(2,1)S(1)}, bf16[56,1536]{1,0:T(8,128)(2,1)S(1)}, u32[]{:S(2)}, u32[]{:S(2)}) collective-permute-start(bf16[56,1536]{1,0:T(8,128)(2,1)S(1)} %collective-permute-done.8.refs_0_), channel_id=1, source_target_pairs={{0,2},{2,4},{4,6},{6,7},{7,5},{5,3},{3,1},{1,0},{8,10},{10,12},{12... | collective-permute-start | bytes 516104 | tf_op jit(solution)/shard_map/ppermute | solution.py:355
  27.8 1.9 %collective-permute-start.17 = (bf16[168,512]{1,0:T(8,128)(2,1)S(1)}, bf16[168,512]{1,0:T(8,128)(2,1)S(1)}, u32[]{:S(2)}, u32[]{:S(2)}) collective-permute-start(bf16[168,512]{1,0:T(8,128)(2,1)S(1)} %get-tuple-element.64.refs_4_), channel_id=1, source_target_pairs={{0,16},{8,24},{16,0},{24,8},{1,17},{9,25},{17,1},{25,9},{2,18},{10... | collective-permute-start | bytes 516104 | tf_op jit(solution)/shard_map/ppermute | solution.py:43
  29.7 1.7 %collective-permute-start.18 = (bf16[112,512]{1,0:T(8,128)(2,1)S(1)}, bf16[112,512]{1,0:T(8,128)(2,1)S(1)}, u32[]{:S(2)}, u32[]{:S(2)}) collective-permute-start(bf16[112,512]{1,0:T(8,128)(2,1)S(1)} %get-tuple-element.65.refs_5_), channel_id=1, source_target_pairs={{0,16},{8,24},{16,0},{24,8},{1,17},{9,25},{17,1},{25,9},{2,18},{10... | collective-permute-start | bytes 344072 | tf_op jit(solution)/shard_map/ppermute | solution.py:43
  40.1 1.9 %shard_map.119 = (bf16[448,256]{1,0:T(8,128)(2,1)S(1)}, f32[4,448]{1,0:T(4,128)S(1)}, f32[256,448]{1,0:T(8,128)S(1)}) custom-call(bf16[168,256]{1,0:T(8,128)(2,1)S(1)} %get-tuple-element.55.refs_0_, bf16[112,256]{1,0:T(8,128)(2,1)S(1)} %get-tuple-element.58.refs_1_, bf16[112,256]{1,0:T(8,128)(2,1)S(1)} %get-tuple-element.61.refs_2_, ...), custom_call_target="tpu_custom_call" | custom-call | flops 359661568 | bytes 1032192 | tf_op jit(solution)/shard_map/pallas_call | solution.py:23
  42.0 1.9 %shard_map.120 = (f32[4,448]{1,0:T(4,128)S(1)}, f32[256,448]{1,0:T(8,128)S(1)}) custom-call(bf16[448,256]{1,0:T(8,128)(2,1)S(1)} %get-tuple-element.67.refs_0_.query_ref, f32[4,448]{1,0:T(4,128)S(1)} %get-tuple-element.68.refs_1_, f32[256,448]{1,0:T(8,128)S(1)} %get-tuple-element.69.refs_2_, bf16[168,512]{1,0:T(8,128)(2,1)S(1)} %collective-permute-done.17.refs_3_, ...), custom_call_target="tpu_custom_call" | custom-call | flops 256901120 | bytes 1268736 | tf_op jit(solution)/shard_map/pallas_call | solution.py:23
  43.9 2.3 %shard_map.121 = (bf16[72,1024]{1,0:T(8,128)(2,1)S(1)}, bf16[48,2048]{1,0:T(8,128)(2,1)S(1)}, bf16[72,1024]{1,0:T(8,128)(2,1)S(1)}, bf16[48,2048]{1,0:T(8,128)(2...) custom-call(bf16[448,256]{1,0:T(8,128)(2,1)S(1)} %get-tuple-element., ...), custom_call_target="tpu_custom_call" | custom-call | flops 910163968 | bytes 4299776 | tf_op jit(solution)/shard_map/pallas_call | solution.py:23
  50.3 2.6 %collective-permute-done.26 = bf16[72,1024]{1,0:T(8,128)(2,1)S(1)} collective-permute-done((bf16[72,1024]{1,0:T(8,128)(2,1)S(1)}, bf16[72,1024]{1,0:T(8,128)(2,1)S(1)}, u32[]{:S(2)}, u32[]{:S(2)}) %collective-permute-start.26) | collective-permute-done | bytes 147488 | tf_op jit(solution)/shard_map/ppermute | solution.py:436
  53.0 1.6 %collective-permute-start.27 = (bf16[72,1024]{1,0:T(8,128)(2,1)S(1)}, bf16[72,1024]{1,0:T(8,128)(2,1)S(1)}, u32[]{:S(2)}, u32[]{:S(2)}) collective-permute-start(bf16[72,1024]{1,0:T(8,128)(2,1)S(1)} %add_convert_fusion.9), channel_id=1, source_target_pairs={{0,2},{2,4},{4,6},{6,7},{7,5},{5,3},{3,1},{1,0},{8,10},{10,12},{12... | collective-permute-start | bytes 442376 | tf_op jit(solution)/shard_map/ppermute | solution.py:436
  55.2 2.0 %collective-permute-done.33 = bf16[48,2048]{1,0:T(8,128)(2,1)S(1)} collective-permute-done((bf16[48,2048]{1,0:T(8,128)(2,1)S(1)}, bf16[48,2048]{1,0:T(8,128)(2,1)S(1)}, u32[]{:S(2)}, u32[]{:S(2)}) %collective-permute-start.33) | collective-permute-done | bytes 196640 | tf_op jit(solution)/shard_map/ppermute | solution.py:441
  57.2 1.6 %collective-permute-start.34 = (bf16[48,2048]{1,0:T(8,128)(2,1)S(1)}, bf16[48,2048]{1,0:T(8,128)(2,1)S(1)}, u32[]{:S(2)}, u32[]{:S(2)}) collective-permute-start(bf16[48,2048]{1,0:T(8,128)(2,1)S(1)} %add_convert_fusion.4), channel_id=1, source_target_pairs={{0,2},{2,4},{4,6},{6,7},{7,5},{5,3},{3,1},{1,0},{8,10},{10,12},{12... | collective-permute-start | bytes 589832 | tf_op jit(solution)/shard_map/ppermute | solution.py:441
  60.3 1.6 %collective-permute-start.28 = (bf16[72,1024]{1,0:T(8,128)(2,1)S(1)}, bf16[72,1024]{1,0:T(8,128)(2,1)S(1)}, u32[]{:S(2)}, u32[]{:S(2)}) collective-permute-start(bf16[72,1024]{1,0:T(8,128)(2,1)S(1)} %add_convert_fusion.8), channel_id=1, source_target_pairs={{0,2},{2,4},{4,6},{6,7},{7,5},{5,3},{3,1},{1,0},{8,10},{10,12},{12... | collective-permute-start | bytes 442376 | tf_op jit(solution)/shard_map/ppermute | solution.py:436
  62.5 2.6 %collective-permute-done.34 = bf16[48,2048]{1,0:T(8,128)(2,1)S(1)} collective-permute-done((bf16[48,2048]{1,0:T(8,128)(2,1)S(1)}, bf16[48,2048]{1,0:T(8,128)(2,1)S(1)}, u32[]{:S(2)}, u32[]{:S(2)}) %collective-permute-start.34) | collective-permute-done | bytes 196640 | tf_op jit(solution)/shard_map/ppermute | solution.py:441
  65.1 1.6 %collective-permute-start.35 = (bf16[48,2048]{1,0:T(8,128)(2,1)S(1)}, bf16[48,2048]{1,0:T(8,128)(2,1)S(1)}, u32[]{:S(2)}, u32[]{:S(2)}) collective-permute-start(bf16[48,2048]{1,0:T(8,128)(2,1)S(1)} %add_convert_fusion.3), channel_id=1, source_target_pairs={{0,2},{2,4},{4,6},{6,7},{7,5},{5,3},{3,1},{1,0},{8,10},{10,12},{12... | collective-permute-start | bytes 589832 | tf_op jit(solution)/shard_map/ppermute | solution.py:441
  68.3 1.6 %collective-permute-start.29 = (bf16[72,1024]{1,0:T(8,128)(2,1)S(1)}, bf16[72,1024]{1,0:T(8,128)(2,1)S(1)}, u32[]{:S(2)}, u32[]{:S(2)}) collective-permute-start(bf16[72,1024]{1,0:T(8,128)(2,1)S(1)} %add_convert_fusion.7), channel_id=1, source_target_pairs={{0,2},{2,4},{4,6},{6,7},{7,5},{5,3},{3,1},{1,0},{8,10},{10,12},{12... | collective-permute-start | bytes 442376 | tf_op jit(solution)/shard_map/ppermute | solution.py:436
  69.9 2.7 %collective-permute-done.38 = bf16[48,2048]{1,0:T(8,128)(2,1)S(1)} collective-permute-done((bf16[48,2048]{1,0:T(8,128)(2,1)S(1)}, bf16[48,2048]{1,0:T(8,128)(2,1)S(1)}, u32[]{:S(2)}, u32[]{:S(2)}) %collective-permute-start.38) | collective-permute-done | bytes 196640 | tf_op jit(solution)/shard_map/ppermute | solution.py:437
  76.5 2.3 %collective-permute-done.41.refs_2_ = bf16[8,3072]{1,0:T(8,128)(2,1)S(1)} collective-permute-done((bf16[8,3072]{1,0:T(8,128)(2,1)S(1)}, bf16[8,3072]{1,0:T(8,128)(2,1)S(1)}, u32[]{:S(2)}, u32[]{:S(2)}) %collective-permute-start.41) | collective-permute-done | bytes 49184 | tf_op jit(solution)/shard_map/ppermute | solution.py:43
  (91 shorter events, 29.4 us)
Async XLA Ops:
  2.1 8.9 %collective-permute-start.1 = (bf16[56,1536]{1,0:T(8,128)(2,1)S(1)}, bf16[56,1536]{1,0:T(8,128)(2,1)S(1)}, u32[]{:S(2)}, u32[]{:S(2)}) collective-permute-start(bf16[56,1536]{1,0:T(8,128)(2,1)S(1)} %get-tuple-element.49.refs_0_), channel_id=1, source_target_pairs={{0,2},{2,4},{4,6},{6,7},{7,5},{5,3},{3,1},{1,0},{8,10},{10,12},{12... | collective-permute-start | bytes 516104 | tf_op jit(solution)/shard_map/ppermute | solution.py:355
  5.2 7.9 %collective-permute-start.3 = (bf16[56,1536]{1,0:T(8,128)(2,1)S(1)}, bf16[56,1536]{1,0:T(8,128)(2,1)S(1)}, u32[]{:S(2)}, u32[]{:S(2)}) collective-permute-start(bf16[56,1536]{1,0:T(8,128)(2,1)S(1)} %get-tuple-element.48.refs_1_), channel_id=1, source_target_pairs={{2,0},{4,2},{6,4},{7,6},{5,7},{3,5},{1,3},{0,1},{10,8},{12,10},{14... | collective-permute-start | bytes 516104 | tf_op jit(solution)/shard_map/ppermute | solution.py:356
  5.2 8.4 %collective-permute-start = (bf16[56,1536]{1,0:T(8,128)(2,1)S(1)}, bf16[56,1536]{1,0:T(8,128)(2,1)S(1)}, u32[]{:S(2)}, u32[]{:S(2)}) collective-permute-start(bf16[56,1536]{1,0:T(8,128)(2,1)S(1)} %get-tuple-element.48.refs_1_), channel_id=1, source_target_pairs={{0,2},{2,4},{4,6},{6,7},{7,5},{5,3},{3,1},{1,0},{8,10},{10,12},{12... | collective-permute-start | bytes 516104 | tf_op jit(solution)/shard_map/ppermute | solution.py:360
  7.2 8.3 %collective-permute-start.2 = (bf16[56,1536]{1,0:T(8,128)(2,1)S(1)}, bf16[56,1536]{1,0:T(8,128)(2,1)S(1)}, u32[]{:S(2)}, u32[]{:S(2)}) collective-permute-start(bf16[56,1536]{1,0:T(8,128)(2,1)S(1)} %get-tuple-element.49.refs_0_), channel_id=1, source_target_pairs={{2,0},{4,2},{6,4},{7,6},{5,7},{3,5},{1,3},{0,1},{10,8},{12,10},{14... | collective-permute-start | bytes 516104 | tf_op jit(solution)/shard_map/ppermute | solution.py:361
  11.0 7.4 %collective-permute-start.4 = (bf16[56,1536]{1,0:T(8,128)(2,1)S(1)}, bf16[56,1536]{1,0:T(8,128)(2,1)S(1)}, u32[]{:S(2)}, u32[]{:S(2)}) collective-permute-start(bf16[56,1536]{1,0:T(8,128)(2,1)S(1)} %collective-permute-done.1.refs_2_), channel_id=1, source_target_pairs={{0,2},{2,4},{4,6},{6,7},{7,5},{5,3},{3,1},{1,0},{8,10},{10,12},{12... | collective-permute-start | bytes 516104 | tf_op jit(solution)/shard_map/ppermute | solution.py:355
  13.1 7.3 %collective-permute-start.7 = (bf16[56,1536]{1,0:T(8,128)(2,1)S(1)}, bf16[56,1536]{1,0:T(8,128)(2,1)S(1)}, u32[]{:S(2)}, u32[]{:S(2)}) collective-permute-start(bf16[56,1536]{1,0:T(8,128)(2,1)S(1)} %collective-permute-done.3.refs_5_), channel_id=1, source_target_pairs={{2,0},{4,2},{6,4},{7,6},{5,7},{3,5},{1,3},{0,1},{10,8},{12,10},{14... | collective-permute-start | bytes 516104 | tf_op jit(solution)/shard_map/ppermute | solution.py:356
  13.6 8.5 %collective-permute-start.5 = (bf16[56,1536]{1,0:T(8,128)(2,1)S(1)}, bf16[56,1536]{1,0:T(8,128)(2,1)S(1)}, u32[]{:S(2)}, u32[]{:S(2)}) collective-permute-start(bf16[56,1536]{1,0:T(8,128)(2,1)S(1)} %collective-permute-done.refs_3_), channel_id=1, source_target_pairs={{0,2},{2,4},{4,6},{6,7},{7,5},{5,3},{3,1},{1,0},{8,10},{10,12},{12... | collective-permute-start | bytes 516104 | tf_op jit(solution)/shard_map/ppermute | solution.py:360
  15.5 8.6 %collective-permute-start.6 = (bf16[56,1536]{1,0:T(8,128)(2,1)S(1)}, bf16[56,1536]{1,0:T(8,128)(2,1)S(1)}, u32[]{:S(2)}, u32[]{:S(2)}) collective-permute-start(bf16[56,1536]{1,0:T(8,128)(2,1)S(1)} %collective-permute-done.2.refs_4_), channel_id=1, source_target_pairs={{2,0},{4,2},{6,4},{7,6},{5,7},{3,5},{1,3},{0,1},{10,8},{12,10},{14... | collective-permute-start | bytes 516104 | tf_op jit(solution)/shard_map/ppermute | solution.py:361
  18.4 7.4 %collective-permute-start.8 = (bf16[56,1536]{1,0:T(8,128)(2,1)S(1)}, bf16[56,1536]{1,0:T(8,128)(2,1)S(1)}, u32[]{:S(2)}, u32[]{:S(2)}) collective-permute-start(bf16[56,1536]{1,0:T(8,128)(2,1)S(1)} %collective-permute-done.4.refs_0_), channel_id=1, source_target_pairs={{0,2},{2,4},{4,6},{6,7},{7,5},{5,3},{3,1},{1,0},{8,10},{10,12},{12... | collective-permute-start | bytes 516104 | tf_op jit(solution)/shard_map/ppermute | solution.py:355
  20.4 7.4 %collective-permute-start.11 = (bf16[56,1536]{1,0:T(8,128)(2,1)S(1)}, bf16[56,1536]{1,0:T(8,128)(2,1)S(1)}, u32[]{:S(2)}, u32[]{:S(2)}) collective-permute-start(bf16[56,1536]{1,0:T(8,128)(2,1)S(1)} %collective-permute-done.7.refs_3_), channel_id=1, source_target_pairs={{2,0},{4,2},{6,4},{7,6},{5,7},{3,5},{1,3},{0,1},{10,8},{12,10},{14... | collective-permute-start | bytes 516104 | tf_op jit(solution)/shard_map/ppermute | solution.py:356
  22.1 7.7 %collective-permute-start.9 = (bf16[56,1536]{1,0:T(8,128)(2,1)S(1)}, bf16[56,1536]{1,0:T(8,128)(2,1)S(1)}, u32[]{:S(2)}, u32[]{:S(2)}) collective-permute-start(bf16[56,1536]{1,0:T(8,128)(2,1)S(1)} %collective-permute-done.5.refs_1_), channel_id=1, source_target_pairs={{0,2},{2,4},{4,6},{6,7},{7,5},{5,3},{3,1},{1,0},{8,10},{10,12},{12... | collective-permute-start | bytes 516104 | tf_op jit(solution)/shard_map/ppermute | solution.py:360
  24.1 7.3 %collective-permute-start.10 = (bf16[56,1536]{1,0:T(8,128)(2,1)S(1)}, bf16[56,1536]{1,0:T(8,128)(2,1)S(1)}, u32[]{:S(2)}, u32[]{:S(2)}) collective-permute-start(bf16[56,1536]{1,0:T(8,128)(2,1)S(1)} %collective-permute-done.6.refs_2_), channel_id=1, source_target_pairs={{2,0},{4,2},{6,4},{7,6},{5,7},{3,5},{1,3},{0,1},{10,8},{12,10},{14... | collective-permute-start | bytes 516104 | tf_op jit(solution)/shard_map/ppermute | solution.py:361
  25.8 8.5 %collective-permute-start.12 = (bf16[56,1536]{1,0:T(8,128)(2,1)S(1)}, bf16[56,1536]{1,0:T(8,128)(2,1)S(1)}, u32[]{:S(2)}, u32[]{:S(2)}) collective-permute-start(bf16[56,1536]{1,0:T(8,128)(2,1)S(1)} %collective-permute-done.8.refs_0_), channel_id=1, source_target_pairs={{0,2},{2,4},{4,6},{6,7},{7,5},{5,3},{3,1},{1,0},{8,10},{10,12},{12... | collective-permute-start | bytes 516104 | tf_op jit(solution)/shard_map/ppermute | solution.py:355
  27.8 8.0 %collective-permute-start.17 = (bf16[168,512]{1,0:T(8,128)(2,1)S(1)}, bf16[168,512]{1,0:T(8,128)(2,1)S(1)}, u32[]{:S(2)}, u32[]{:S(2)}) collective-permute-start(bf16[168,512]{1,0:T(8,128)(2,1)S(1)} %get-tuple-element.64.refs_4_), channel_id=1, source_target_pairs={{0,16},{8,24},{16,0},{24,8},{1,17},{9,25},{17,1},{25,9},{2,18},{10... | collective-permute-start | bytes 516104 | tf_op jit(solution)/shard_map/ppermute | solution.py:43
  48.3 8.9 %collective-permute-start.33 = (bf16[48,2048]{1,0:T(8,128)(2,1)S(1)}, bf16[48,2048]{1,0:T(8,128)(2,1)S(1)}, u32[]{:S(2)}, u32[]{:S(2)}) collective-permute-start(bf16[48,2048]{1,0:T(8,128)(2,1)S(1)} %get-tuple-element.84), channel_id=1, source_target_pairs={{0,2},{2,4},{4,6},{6,7},{7,5},{5,3},{3,1},{1,0},{8,10},{10,12},{12... | collective-permute-start | bytes 589832 | tf_op jit(solution)/shard_map/ppermute | solution.py:441
  49.9 9.0 %collective-permute-start.36 = (bf16[48,2048]{1,0:T(8,128)(2,1)S(1)}, bf16[48,2048]{1,0:T(8,128)(2,1)S(1)}, u32[]{:S(2)}, u32[]{:S(2)}) collective-permute-start(bf16[48,2048]{1,0:T(8,128)(2,1)S(1)} %get-tuple-element.87), channel_id=1, source_target_pairs={{2,0},{4,2},{6,4},{7,6},{5,7},{3,5},{1,3},{0,1},{10,8},{12,10},{14... | collective-permute-start | bytes 589832 | tf_op jit(solution)/shard_map/ppermute | solution.py:437
  53.0 7.3 %collective-permute-start.27 = (bf16[72,1024]{1,0:T(8,128)(2,1)S(1)}, bf16[72,1024]{1,0:T(8,128)(2,1)S(1)}, u32[]{:S(2)}, u32[]{:S(2)}) collective-permute-start(bf16[72,1024]{1,0:T(8,128)(2,1)S(1)} %add_convert_fusion.9), channel_id=1, source_target_pairs={{0,2},{2,4},{4,6},{6,7},{7,5},{5,3},{3,1},{1,0},{8,10},{10,12},{12... | collective-permute-start | bytes 442376 | tf_op jit(solution)/shard_map/ppermute | solution.py:436
  54.7 7.3 %collective-permute-start.31 = (bf16[72,1024]{1,0:T(8,128)(2,1)S(1)}, bf16[72,1024]{1,0:T(8,128)(2,1)S(1)}, u32[]{:S(2)}, u32[]{:S(2)}) collective-permute-start(bf16[72,1024]{1,0:T(8,128)(2,1)S(1)} %add_convert_fusion.6), channel_id=1, source_target_pairs={{2,0},{4,2},{6,4},{7,6},{5,7},{3,5},{1,3},{0,1},{10,8},{12,10},{14... | collective-permute-start | bytes 442376 | tf_op jit(solution)/shard_map/ppermute | solution.py:442
  57.2 7.9 %collective-permute-start.34 = (bf16[48,2048]{1,0:T(8,128)(2,1)S(1)}, bf16[48,2048]{1,0:T(8,128)(2,1)S(1)}, u32[]{:S(2)}, u32[]{:S(2)}) collective-permute-start(bf16[48,2048]{1,0:T(8,128)(2,1)S(1)} %add_convert_fusion.4), channel_id=1, source_target_pairs={{0,2},{2,4},{4,6},{6,7},{7,5},{5,3},{3,1},{1,0},{8,10},{10,12},{12... | collective-permute-start | bytes 589832 | tf_op jit(solution)/shard_map/ppermute | solution.py:441
  58.9 7.9 %collective-permute-start.37 = (bf16[48,2048]{1,0:T(8,128)(2,1)S(1)}, bf16[48,2048]{1,0:T(8,128)(2,1)S(1)}, u32[]{:S(2)}, u32[]{:S(2)}) collective-permute-start(bf16[48,2048]{1,0:T(8,128)(2,1)S(1)} %add_convert_fusion.2), channel_id=1, source_target_pairs={{2,0},{4,2},{6,4},{7,6},{5,7},{3,5},{1,3},{0,1},{10,8},{12,10},{14... | collective-permute-start | bytes 589832 | tf_op jit(solution)/shard_map/ppermute | solution.py:437
  60.3 7.9 %collective-permute-start.28 = (bf16[72,1024]{1,0:T(8,128)(2,1)S(1)}, bf16[72,1024]{1,0:T(8,128)(2,1)S(1)}, u32[]{:S(2)}, u32[]{:S(2)}) collective-permute-start(bf16[72,1024]{1,0:T(8,128)(2,1)S(1)} %add_convert_fusion.8), channel_id=1, source_target_pairs={{0,2},{2,4},{4,6},{6,7},{7,5},{5,3},{3,1},{1,0},{8,10},{10,12},{12... | collective-permute-start | bytes 442376 | tf_op jit(solution)/shard_map/ppermute | solution.py:436
  62.0 11.2 %collective-permute-start.32 = (bf16[72,1024]{1,0:T(8,128)(2,1)S(1)}, bf16[72,1024]{1,0:T(8,128)(2,1)S(1)}, u32[]{:S(2)}, u32[]{:S(2)}) collective-permute-start(bf16[72,1024]{1,0:T(8,128)(2,1)S(1)} %add_convert_fusion.5), channel_id=1, source_target_pairs={{2,0},{4,2},{6,4},{7,6},{5,7},{3,5},{1,3},{0,1},{10,8},{12,10},{14... | collective-permute-start | bytes 442376 | tf_op jit(solution)/shard_map/ppermute | solution.py:442
  65.1 11.3 %collective-permute-start.35 = (bf16[48,2048]{1,0:T(8,128)(2,1)S(1)}, bf16[48,2048]{1,0:T(8,128)(2,1)S(1)}, u32[]{:S(2)}, u32[]{:S(2)}) collective-permute-start(bf16[48,2048]{1,0:T(8,128)(2,1)S(1)} %add_convert_fusion.3), channel_id=1, source_target_pairs={{0,2},{2,4},{4,6},{6,7},{7,5},{5,3},{3,1},{1,0},{8,10},{10,12},{12... | collective-permute-start | bytes 589832 | tf_op jit(solution)/shard_map/ppermute | solution.py:441
  72.7 7.0 %collective-permute-start.39 = (bf16[48,2048]{1,0:T(8,128)(2,1)S(1)}, bf16[48,2048]{1,0:T(8,128)(2,1)S(1)}, u32[]{:S(2)}, u32[]{:S(2)}) collective-permute-start(bf16[48,2048]{1,0:T(8,128)(2,1)S(1)} %add_convert_fusion), channel_id=1, source_target_pairs={{2,0},{4,2},{6,4},{7,6},{5,7},{3,5},{1,3},{0,1},{10,8},{12,10},{14... | collective-permute-start | bytes 589832 | tf_op jit(solution)/shard_map/ppermute | solution.py:437
  (23 other events, 178.8 us)

commit v5 on v4

--- a/solution.py
+++ b/solution.py
@@ -217,22 +217,26 @@
         text.append(rows_out[start : start + size * text_rows])
         start += size * text_rows
     video, text = [jnp.concatenate(rows, axis=0).astype(BF16) for rows in (video, text)]
-    put_partials(outs, video, text, weights, sum(sizes))
-
-
-def put_partials(outs, video, text, weights, shards):
+    video_ref, *outs = outs
+    video_ref[...] = video
     lead = outs[0].shape[1]
-    cuts = [slice(0, lead), slice(lead, weights[0].shape[1])]
-    vn, tn = video.shape[0] // shards, text.shape[0] // shards
-    left, right = [jnp.dot(video, weights[0][:, c], preferred_element_type=F32) for c in cuts]
+    left = jnp.dot(video, weights[0][:, :lead], preferred_element_type=F32)
     bands = [
         jnp.dot(text, weights[1][:, c : c + lead], preferred_element_type=F32)
         for c in range(0, weights[1].shape[1], lead)
     ]
-    for i in range(shards):
-        rows = [left[i * vn : (i + 1) * vn]] + [y[i * tn : (i + 1) * tn] for y in bands]
-        outs[2 * i][...] = jnp.concatenate(rows, axis=0).astype(BF16)
-        outs[2 * i + 1][...] = right[i * vn : (i + 1) * vn].astype(BF16)
+    for i, out in enumerate(outs):
+        rows = [left[i * video_rows : (i + 1) * video_rows]]
+        rows += [y[i * text_rows : (i + 1) * text_rows] for y in bands]
+        out[...] = jnp.concatenate(rows, axis=0).astype(BF16)
+
+
+def right_kernel(video_ref, wv_ref, *outs):
+    video_rows, columns = outs[0].shape
+    lead = wv_ref.shape[1] - columns
+    right = jnp.dot(video_ref[...], wv_ref[:, lead:], preferred_element_type=F32)
+    for i, out in enumerate(outs):
+        out[...] = right[i * video_rows : (i + 1) * video_rows].astype(BF16)
 
 
 def close_text_kernel(fa_ref, ba_ref, own_ref, tmod_ref, text_ref):
@@ -379,8 +383,12 @@
 
     def some(sources, chosen):
         return [
-            [(pieces[g][d], sizes[g] * (shard_rows if d < parts else video_rows)) for g in chosen]
-            for d in sources
+            [
+                (pieces[g][d], sizes[g] * (shard_rows if d < parts else video_rows))
+                for d in sources[i : i + 2]
+                for g in chosen
+            ]
+            for i in range(0, len(sources), 2)
         ]
 
     def attended(blocks, given, queries, kernel, outs, extra=(), more=0):
@@ -415,16 +423,23 @@
         jax.ShapeDtypeStruct((video_rows, width - lead), BF16),
     ]
     last = [piece for block in some(outer, first[-1:]) + some(range(n_blk), (len(groups) - 1,)) for piece in block]
-    partial = attended(
+    video_heads, *lefts = attended(
         [last],
         [query, *carried],
         (sizes, video_rows),
         finish_kernel,
-        shapes * n_uly,
+        [jax.ShapeDtypeStruct((video_rows * n_uly, cols), BF16)] + [shapes[0]] * n_uly,
         (video_output, text_output),
         2 * total_rows * cols * width,
     )
-    mine = {r: (partial[2 * i], partial[2 * i + 1]) for i, r in enumerate(slots)}
+    rights = call(
+        right_kernel,
+        [shapes[1]] * n_uly,
+        [video_heads, video_output],
+        16,
+        flops=2 * video_rows * n_uly * cols * (width - lead),
+    )
+    mine = {r: pair for r, *pair in zip(slots, lefts, rights)}
     mine[-reach] = mine[reach]
 
     def joined(arriving, own_part):

time: 80.8 us -> 79.8 us (0.988)
    pallas_call x11 -> x12, Pallas kernels: 18.1 us -> 17.6 us  [call(): pl.pallas_call(kernel, out_shape=outs, in_specs=[SMEM if i in smem else H...]
  transfers between devices with their start and end apart: 43 -> 43, of which waited for: 14 -> 15; matrix products, arithmetic and copies ran while one was open for 1% -> 1% of each run, Pallas kernels for 17% -> 17%
where the time goes in v5:
time: 79.8 us; the launch traced here: 79.6 us
  starting transfers between devices  40.6 us (51%)
  waiting for transfers between devices  20.1 us (25%)
  Pallas kernels  17.6 us (22%)
  between operations  0.87 us (1%)
    pallas_call x12, Pallas kernels, call(): pl.pallas_call(kernel, out_shape=outs, in_specs=[SMEM if i in smem else H...  17.6 us
    ppermute x15, starting transfers between devices, across(): return lax.ppermute(block, 'blk', [(i, i ^ distance) for i in range(n)])  10.5 us
    ppermute x4, starting transfers between devices, local(): fa = lax.ppermute(tied(fa, *due) if due else fa, 'uly', ahead)  9.18 us
    ppermute x4, starting transfers between devices, local(): fa = lax.ppermute(fa, 'uly', ahead)  6.51 us
    ppermute x3, starting transfers between devices, local(): fb = lax.ppermute(tied(fb, *due) if due else fb, 'uly', ahead)  5.89 us
    ppermute x4, waiting for transfers between devices, local(): fa = lax.ppermute(fa, 'uly', ahead)  5.06 us
    ppermute x3, starting transfers between devices, local(): fb = lax.ppermute(fb, 'uly', ahead)  4.89 us
    ppermute x3, waiting for transfers between devices, local(): fb = lax.ppermute(fb, 'uly', ahead)  4.56 us
  transfers between devices with their start and end apart: 43, of which 15 were waited for; matrix products, arithmetic and copies ran while one was open for 1% of the time, Pallas kernels for 17%

profile of v5, /device:TPU:0, one launch (start us, length us, event | category | flops | bytes accessed | tf_op | source)
XLA Modules:
  0.0 79.6 jit_solution(6800848238758300630)
XLA Ops:
  2.1 3.1 %collective-permute-start.1 = (bf16[56,1536]{1,0:T(8,128)(2,1)S(1)}, bf16[56,1536]{1,0:T(8,128)(2,1)S(1)}, u32[]{:S(2)}, u32[]{:S(2)}) collective-permute-start(bf16[56,1536]{1,0:T(8,128)(2,1)S(1)} %get-tuple-element.50.refs_0_), channel_id=1, source_target_pairs={{0,2},{2,4},{4,6},{6,7},{7,5},{5,3},{3,1},{1,0},{8,10},{10,12},{12... | collective-permute-start | bytes 516104 | tf_op jit(solution)/shard_map/ppermute | solution.py:359
  5.2 2.0 %collective-permute-start = (bf16[56,1536]{1,0:T(8,128)(2,1)S(1)}, bf16[56,1536]{1,0:T(8,128)(2,1)S(1)}, u32[]{:S(2)}, u32[]{:S(2)}) collective-permute-start(bf16[56,1536]{1,0:T(8,128)(2,1)S(1)} %get-tuple-element.49.refs_1_), channel_id=1, source_target_pairs={{0,2},{2,4},{4,6},{6,7},{7,5},{5,3},{3,1},{1,0},{8,10},{10,12},{12... | collective-permute-start | bytes 516104 | tf_op jit(solution)/shard_map/ppermute | solution.py:364
  7.2 3.8 %shard_map.114 = (bf16[3,3072,256]{2,1,0:T(8,128)(2,1)S(1)}, bf16[3,3072,256]{2,1,0:T(8,128)(2,1)S(1)}, f32[2,128]{1,0:T(2,128)S(1)}, f32[2,128]{1,0:T(2,128)S(1)}) custom-call(bf16[3,3072,256]{2,1,0:T(8,128)(2,1)} %bitcast.3, bf16[3,3072,256]{2,1,0:T(8,128)(2,1)} %bitcast.4, f32[2,128]{1,0:T(2,128)} %refs_2_.3, f32[2,128]{1,0:T(2,128)} %refs_3_.3), custom_call_target="tpu_custom_call" | custom-call | bytes 9439232 | tf_op jit(solution)/shard_map/pallas_call | solution.py:23
  11.0 2.1 %collective-permute-start.4 = (bf16[56,1536]{1,0:T(8,128)(2,1)S(1)}, bf16[56,1536]{1,0:T(8,128)(2,1)S(1)}, u32[]{:S(2)}, u32[]{:S(2)}) collective-permute-start(bf16[56,1536]{1,0:T(8,128)(2,1)S(1)} %collective-permute-done.1.refs_2_), channel_id=1, source_target_pairs={{0,2},{2,4},{4,6},{6,7},{7,5},{5,3},{3,1},{1,0},{8,10},{10,12},{12... | collective-permute-start | bytes 516104 | tf_op jit(solution)/shard_map/ppermute | solution.py:359
  13.6 1.9 %collective-permute-start.5 = (bf16[56,1536]{1,0:T(8,128)(2,1)S(1)}, bf16[56,1536]{1,0:T(8,128)(2,1)S(1)}, u32[]{:S(2)}, u32[]{:S(2)}) collective-permute-start(bf16[56,1536]{1,0:T(8,128)(2,1)S(1)} %collective-permute-done.refs_3_), channel_id=1, source_target_pairs={{0,2},{2,4},{4,6},{6,7},{7,5},{5,3},{3,1},{1,0},{8,10},{10,12},{12... | collective-permute-start | bytes 516104 | tf_op jit(solution)/shard_map/ppermute | solution.py:364
  18.4 2.0 %collective-permute-start.8 = (bf16[56,1536]{1,0:T(8,128)(2,1)S(1)}, bf16[56,1536]{1,0:T(8,128)(2,1)S(1)}, u32[]{:S(2)}, u32[]{:S(2)}) collective-permute-start(bf16[56,1536]{1,0:T(8,128)(2,1)S(1)} %collective-permute-done.4.refs_0_), channel_id=1, source_target_pairs={{0,2},{2,4},{4,6},{6,7},{7,5},{5,3},{3,1},{1,0},{8,10},{10,12},{12... | collective-permute-start | bytes 516104 | tf_op jit(solution)/shard_map/ppermute | solution.py:359
  20.4 1.6 %collective-permute-done.5.refs_1_ = bf16[56,1536]{1,0:T(8,128)(2,1)S(1)} collective-permute-done((bf16[56,1536]{1,0:T(8,128)(2,1)S(1)}, bf16[56,1536]{1,0:T(8,128)(2,1)S(1)}, u32[]{:S(2)}, u32[]{:S(2)}) %collective-permute-start.5) | collective-permute-done | bytes 172064 | tf_op jit(solution)/shard_map/ppermute | solution.py:364
  22.1 2.0 %collective-permute-start.9 = (bf16[56,1536]{1,0:T(8,128)(2,1)S(1)}, bf16[56,1536]{1,0:T(8,128)(2,1)S(1)}, u32[]{:S(2)}, u32[]{:S(2)}) collective-permute-start(bf16[56,1536]{1,0:T(8,128)(2,1)S(1)} %collective-permute-done.5.refs_1_), channel_id=1, source_target_pairs={{0,2},{2,4},{4,6},{6,7},{7,5},{5,3},{3,1},{1,0},{8,10},{10,12},{12... | collective-permute-start | bytes 516104 | tf_op jit(solution)/shard_map/ppermute | solution.py:364
  25.8 2.0 %collective-permute-start.12 = (bf16[56,1536]{1,0:T(8,128)(2,1)S(1)}, bf16[56,1536]{1,0:T(8,128)(2,1)S(1)}, u32[]{:S(2)}, u32[]{:S(2)}) collective-permute-start(bf16[56,1536]{1,0:T(8,128)(2,1)S(1)} %collective-permute-done.8.refs_0_), channel_id=1, source_target_pairs={{0,2},{2,4},{4,6},{6,7},{7,5},{5,3},{3,1},{1,0},{8,10},{10,12},{12... | collective-permute-start | bytes 516104 | tf_op jit(solution)/shard_map/ppermute | solution.py:359
  27.8 1.9 %collective-permute-start.17 = (bf16[168,512]{1,0:T(8,128)(2,1)S(1)}, bf16[168,512]{1,0:T(8,128)(2,1)S(1)}, u32[]{:S(2)}, u32[]{:S(2)}) collective-permute-start(bf16[168,512]{1,0:T(8,128)(2,1)S(1)} %get-tuple-element.65.refs_4_), channel_id=1, source_target_pairs={{0,16},{8,24},{16,0},{24,8},{1,17},{9,25},{17,1},{25,9},{2,18},{10... | collective-permute-start | bytes 516104 | tf_op jit(solution)/shard_map/ppermute | solution.py:43
  29.7 1.7 %collective-permute-start.18 = (bf16[112,512]{1,0:T(8,128)(2,1)S(1)}, bf16[112,512]{1,0:T(8,128)(2,1)S(1)}, u32[]{:S(2)}, u32[]{:S(2)}) collective-permute-start(bf16[112,512]{1,0:T(8,128)(2,1)S(1)} %get-tuple-element.66.refs_5_), channel_id=1, source_target_pairs={{0,16},{8,24},{16,0},{24,8},{1,17},{9,25},{17,1},{25,9},{2,18},{10... | collective-permute-start | bytes 344072 | tf_op jit(solution)/shard_map/ppermute | solution.py:43
  40.1 1.7 %shard_map.119 = (bf16[448,256]{1,0:T(8,128)(2,1)S(1)}, f32[4,448]{1,0:T(4,128)S(1)}, f32[256,448]{1,0:T(8,128)S(1)}) custom-call(bf16[168,256]{1,0:T(8,128)(2,1)S(1)} %get-tuple-element.56.refs_0_, bf16[112,256]{1,0:T(8,128)(2,1)S(1)} %get-tuple-element.59.refs_1_, bf16[112,256]{1,0:T(8,128)(2,1)S(1)} %get-tuple-element.62.refs_2_, ...), custom_call_target="tpu_custom_call" | custom-call | flops 359661568 | bytes 1032192 | tf_op jit(solution)/shard_map/pallas_call | solution.py:23
  43.5 1.9 %shard_map.121 = (bf16[384,256]{1,0:T(8,128)(2,1)S(1)}, bf16[72,1024]{1,0:T(8,128)(2,1)S(1)}, bf16[72,1024]{1,0:T(8,128)(2,1)S(1)}, bf16[72,1024]{1,0:T(8,128)(2...) custom-call(bf16[448,256]{1,0:T(8,128)(2,1)S(1)} %get-tuple-element., ...), custom_call_target="tpu_custom_call" | custom-call | flops 910163968 | bytes 4299776 | tf_op jit(solution)/shard_map/pallas_call | solution.py:23
  48.0 1.6 %collective-permute-start.33 = (bf16[48,2048]{1,0:T(8,128)(2,1)S(1)}, bf16[48,2048]{1,0:T(8,128)(2,1)S(1)}, u32[]{:S(2)}, u32[]{:S(2)}) collective-permute-start(bf16[48,2048]{1,0:T(8,128)(2,1)S(1)} %get-tuple-element.86), channel_id=1, source_target_pairs={{0,2},{2,4},{4,6},{6,7},{7,5},{5,3},{3,1},{1,0},{8,10},{10,12},{12... | collective-permute-start | bytes 589832 | tf_op jit(solution)/shard_map/ppermute | solution.py:456
  50.1 2.0 %collective-permute-done.26 = bf16[72,1024]{1,0:T(8,128)(2,1)S(1)} collective-permute-done((bf16[72,1024]{1,0:T(8,128)(2,1)S(1)}, bf16[72,1024]{1,0:T(8,128)(2,1)S(1)}, u32[]{:S(2)}, u32[]{:S(2)}) %collective-permute-start.26) | collective-permute-done | bytes 147488 | tf_op jit(solution)/shard_map/ppermute | solution.py:451
  52.1 1.6 %collective-permute-start.27 = (bf16[72,1024]{1,0:T(8,128)(2,1)S(1)}, bf16[72,1024]{1,0:T(8,128)(2,1)S(1)}, u32[]{:S(2)}, u32[]{:S(2)}) collective-permute-start(bf16[72,1024]{1,0:T(8,128)(2,1)S(1)} %add_convert_fusion.9), channel_id=1, source_target_pairs={{0,2},{2,4},{4,6},{6,7},{7,5},{5,3},{3,1},{1,0},{8,10},{10,12},{12... | collective-permute-start | bytes 442376 | tf_op jit(solution)/shard_map/ppermute | solution.py:451
  54.3 2.0 %collective-permute-done.33 = bf16[48,2048]{1,0:T(8,128)(2,1)S(1)} collective-permute-done((bf16[48,2048]{1,0:T(8,128)(2,1)S(1)}, bf16[48,2048]{1,0:T(8,128)(2,1)S(1)}, u32[]{:S(2)}, u32[]{:S(2)}) %collective-permute-start.33) | collective-permute-done | bytes 196640 | tf_op jit(solution)/shard_map/ppermute | solution.py:456
  56.4 1.6 %collective-permute-start.34 = (bf16[48,2048]{1,0:T(8,128)(2,1)S(1)}, bf16[48,2048]{1,0:T(8,128)(2,1)S(1)}, u32[]{:S(2)}, u32[]{:S(2)}) collective-permute-start(bf16[48,2048]{1,0:T(8,128)(2,1)S(1)} %add_convert_fusion.4), channel_id=1, source_target_pairs={{0,2},{2,4},{4,6},{6,7},{7,5},{5,3},{3,1},{1,0},{8,10},{10,12},{12... | collective-permute-start | bytes 589832 | tf_op jit(solution)/shard_map/ppermute | solution.py:456
  59.5 1.6 %collective-permute-start.28 = (bf16[72,1024]{1,0:T(8,128)(2,1)S(1)}, bf16[72,1024]{1,0:T(8,128)(2,1)S(1)}, u32[]{:S(2)}, u32[]{:S(2)}) collective-permute-start(bf16[72,1024]{1,0:T(8,128)(2,1)S(1)} %add_convert_fusion.8), channel_id=1, source_target_pairs={{0,2},{2,4},{4,6},{6,7},{7,5},{5,3},{3,1},{1,0},{8,10},{10,12},{12... | collective-permute-start | bytes 442376 | tf_op jit(solution)/shard_map/ppermute | solution.py:451
  61.7 2.6 %collective-permute-done.34 = bf16[48,2048]{1,0:T(8,128)(2,1)S(1)} collective-permute-done((bf16[48,2048]{1,0:T(8,128)(2,1)S(1)}, bf16[48,2048]{1,0:T(8,128)(2,1)S(1)}, u32[]{:S(2)}, u32[]{:S(2)}) %collective-permute-start.34) | collective-permute-done | bytes 196640 | tf_op jit(solution)/shard_map/ppermute | solution.py:456
  64.3 1.6 %collective-permute-start.35 = (bf16[48,2048]{1,0:T(8,128)(2,1)S(1)}, bf16[48,2048]{1,0:T(8,128)(2,1)S(1)}, u32[]{:S(2)}, u32[]{:S(2)}) collective-permute-start(bf16[48,2048]{1,0:T(8,128)(2,1)S(1)} %add_convert_fusion.3), channel_id=1, source_target_pairs={{0,2},{2,4},{4,6},{6,7},{7,5},{5,3},{3,1},{1,0},{8,10},{10,12},{12... | collective-permute-start | bytes 589832 | tf_op jit(solution)/shard_map/ppermute | solution.py:456
  67.5 1.6 %collective-permute-start.29 = (bf16[72,1024]{1,0:T(8,128)(2,1)S(1)}, bf16[72,1024]{1,0:T(8,128)(2,1)S(1)}, u32[]{:S(2)}, u32[]{:S(2)}) collective-permute-start(bf16[72,1024]{1,0:T(8,128)(2,1)S(1)} %add_convert_fusion.7), channel_id=1, source_target_pairs={{0,2},{2,4},{4,6},{6,7},{7,5},{5,3},{3,1},{1,0},{8,10},{10,12},{12... | collective-permute-start | bytes 442376 | tf_op jit(solution)/shard_map/ppermute | solution.py:451
  69.1 2.6 %collective-permute-done.38 = bf16[48,2048]{1,0:T(8,128)(2,1)S(1)} collective-permute-done((bf16[48,2048]{1,0:T(8,128)(2,1)S(1)}, bf16[48,2048]{1,0:T(8,128)(2,1)S(1)}, u32[]{:S(2)}, u32[]{:S(2)}) %collective-permute-start.38) | collective-permute-done | bytes 196640 | tf_op jit(solution)/shard_map/ppermute | solution.py:452
  75.5 2.3 %collective-permute-done.41.refs_2_ = bf16[8,3072]{1,0:T(8,128)(2,1)S(1)} collective-permute-done((bf16[8,3072]{1,0:T(8,128)(2,1)S(1)}, bf16[8,3072]{1,0:T(8,128)(2,1)S(1)}, u32[]{:S(2)}, u32[]{:S(2)}) %collective-permute-start.41) | collective-permute-done | bytes 49184 | tf_op jit(solution)/shard_map/ppermute | solution.py:43
  (92 shorter events, 29.9 us)
Async XLA Ops:
  2.1 8.9 %collective-permute-start.1 = (bf16[56,1536]{1,0:T(8,128)(2,1)S(1)}, bf16[56,1536]{1,0:T(8,128)(2,1)S(1)}, u32[]{:S(2)}, u32[]{:S(2)}) collective-permute-start(bf16[56,1536]{1,0:T(8,128)(2,1)S(1)} %get-tuple-element.50.refs_0_), channel_id=1, source_target_pairs={{0,2},{2,4},{4,6},{6,7},{7,5},{5,3},{3,1},{1,0},{8,10},{10,12},{12... | collective-permute-start | bytes 516104 | tf_op jit(solution)/shard_map/ppermute | solution.py:359
  5.2 7.9 %collective-permute-start.3 = (bf16[56,1536]{1,0:T(8,128)(2,1)S(1)}, bf16[56,1536]{1,0:T(8,128)(2,1)S(1)}, u32[]{:S(2)}, u32[]{:S(2)}) collective-permute-start(bf16[56,1536]{1,0:T(8,128)(2,1)S(1)} %get-tuple-element.49.refs_1_), channel_id=1, source_target_pairs={{2,0},{4,2},{6,4},{7,6},{5,7},{3,5},{1,3},{0,1},{10,8},{12,10},{14... | collective-permute-start | bytes 516104 | tf_op jit(solution)/shard_map/ppermute | solution.py:360
  5.2 8.4 %collective-permute-start = (bf16[56,1536]{1,0:T(8,128)(2,1)S(1)}, bf16[56,1536]{1,0:T(8,128)(2,1)S(1)}, u32[]{:S(2)}, u32[]{:S(2)}) collective-permute-start(bf16[56,1536]{1,0:T(8,128)(2,1)S(1)} %get-tuple-element.49.refs_1_), channel_id=1, source_target_pairs={{0,2},{2,4},{4,6},{6,7},{7,5},{5,3},{3,1},{1,0},{8,10},{10,12},{12... | collective-permute-start | bytes 516104 | tf_op jit(solution)/shard_map/ppermute | solution.py:364
  7.2 8.3 %collective-permute-start.2 = (bf16[56,1536]{1,0:T(8,128)(2,1)S(1)}, bf16[56,1536]{1,0:T(8,128)(2,1)S(1)}, u32[]{:S(2)}, u32[]{:S(2)}) collective-permute-start(bf16[56,1536]{1,0:T(8,128)(2,1)S(1)} %get-tuple-element.50.refs_0_), channel_id=1, source_target_pairs={{2,0},{4,2},{6,4},{7,6},{5,7},{3,5},{1,3},{0,1},{10,8},{12,10},{14... | collective-permute-start | bytes 516104 | tf_op jit(solution)/shard_map/ppermute | solution.py:365
  11.0 7.4 %collective-permute-start.4 = (bf16[56,1536]{1,0:T(8,128)(2,1)S(1)}, bf16[56,1536]{1,0:T(8,128)(2,1)S(1)}, u32[]{:S(2)}, u32[]{:S(2)}) collective-permute-start(bf16[56,1536]{1,0:T(8,128)(2,1)S(1)} %collective-permute-done.1.refs_2_), channel_id=1, source_target_pairs={{0,2},{2,4},{4,6},{6,7},{7,5},{5,3},{3,1},{1,0},{8,10},{10,12},{12... | collective-permute-start | bytes 516104 | tf_op jit(solution)/shard_map/ppermute | solution.py:359
  13.1 7.3 %collective-permute-start.7 = (bf16[56,1536]{1,0:T(8,128)(2,1)S(1)}, bf16[56,1536]{1,0:T(8,128)(2,1)S(1)}, u32[]{:S(2)}, u32[]{:S(2)}) collective-permute-start(bf16[56,1536]{1,0:T(8,128)(2,1)S(1)} %collective-permute-done.3.refs_5_), channel_id=1, source_target_pairs={{2,0},{4,2},{6,4},{7,6},{5,7},{3,5},{1,3},{0,1},{10,8},{12,10},{14... | collective-permute-start | bytes 516104 | tf_op jit(solution)/shard_map/ppermute | solution.py:360
  13.6 8.5 %collective-permute-start.5 = (bf16[56,1536]{1,0:T(8,128)(2,1)S(1)}, bf16[56,1536]{1,0:T(8,128)(2,1)S(1)}, u32[]{:S(2)}, u32[]{:S(2)}) collective-permute-start(bf16[56,1536]{1,0:T(8,128)(2,1)S(1)} %collective-permute-done.refs_3_), channel_id=1, source_target_pairs={{0,2},{2,4},{4,6},{6,7},{7,5},{5,3},{3,1},{1,0},{8,10},{10,12},{12... | collective-permute-start | bytes 516104 | tf_op jit(solution)/shard_map/ppermute | solution.py:364
  15.5 8.6 %collective-permute-start.6 = (bf16[56,1536]{1,0:T(8,128)(2,1)S(1)}, bf16[56,1536]{1,0:T(8,128)(2,1)S(1)}, u32[]{:S(2)}, u32[]{:S(2)}) collective-permute-start(bf16[56,1536]{1,0:T(8,128)(2,1)S(1)} %collective-permute-done.2.refs_4_), channel_id=1, source_target_pairs={{2,0},{4,2},{6,4},{7,6},{5,7},{3,5},{1,3},{0,1},{10,8},{12,10},{14... | collective-permute-start | bytes 516104 | tf_op jit(solution)/shard_map/ppermute | solution.py:365
  18.4 7.4 %collective-permute-start.8 = (bf16[56,1536]{1,0:T(8,128)(2,1)S(1)}, bf16[56,1536]{1,0:T(8,128)(2,1)S(1)}, u32[]{:S(2)}, u32[]{:S(2)}) collective-permute-start(bf16[56,1536]{1,0:T(8,128)(2,1)S(1)} %collective-permute-done.4.refs_0_), channel_id=1, source_target_pairs={{0,2},{2,4},{4,6},{6,7},{7,5},{5,3},{3,1},{1,0},{8,10},{10,12},{12... | collective-permute-start | bytes 516104 | tf_op jit(solution)/shard_map/ppermute | solution.py:359
  20.4 7.4 %collective-permute-start.11 = (bf16[56,1536]{1,0:T(8,128)(2,1)S(1)}, bf16[56,1536]{1,0:T(8,128)(2,1)S(1)}, u32[]{:S(2)}, u32[]{:S(2)}) collective-permute-start(bf16[56,1536]{1,0:T(8,128)(2,1)S(1)} %collective-permute-done.7.refs_3_), channel_id=1, source_target_pairs={{2,0},{4,2},{6,4},{7,6},{5,7},{3,5},{1,3},{0,1},{10,8},{12,10},{14... | collective-permute-start | bytes 516104 | tf_op jit(solution)/shard_map/ppermute | solution.py:360
  22.1 7.7 %collective-permute-start.9 = (bf16[56,1536]{1,0:T(8,128)(2,1)S(1)}, bf16[56,1536]{1,0:T(8,128)(2,1)S(1)}, u32[]{:S(2)}, u32[]{:S(2)}) collective-permute-start(bf16[56,1536]{1,0:T(8,128)(2,1)S(1)} %collective-permute-done.5.refs_1_), channel_id=1, source_target_pairs={{0,2},{2,4},{4,6},{6,7},{7,5},{5,3},{3,1},{1,0},{8,10},{10,12},{12... | collective-permute-start | bytes 516104 | tf_op jit(solution)/shard_map/ppermute | solution.py:364
  24.1 7.3 %collective-permute-start.10 = (bf16[56,1536]{1,0:T(8,128)(2,1)S(1)}, bf16[56,1536]{1,0:T(8,128)(2,1)S(1)}, u32[]{:S(2)}, u32[]{:S(2)}) collective-permute-start(bf16[56,1536]{1,0:T(8,128)(2,1)S(1)} %collective-permute-done.6.refs_2_), channel_id=1, source_target_pairs={{2,0},{4,2},{6,4},{7,6},{5,7},{3,5},{1,3},{0,1},{10,8},{12,10},{14... | collective-permute-start | bytes 516104 | tf_op jit(solution)/shard_map/ppermute | solution.py:365
  25.8 8.5 %collective-permute-start.12 = (bf16[56,1536]{1,0:T(8,128)(2,1)S(1)}, bf16[56,1536]{1,0:T(8,128)(2,1)S(1)}, u32[]{:S(2)}, u32[]{:S(2)}) collective-permute-start(bf16[56,1536]{1,0:T(8,128)(2,1)S(1)} %collective-permute-done.8.refs_0_), channel_id=1, source_target_pairs={{0,2},{2,4},{4,6},{6,7},{7,5},{5,3},{3,1},{1,0},{8,10},{10,12},{12... | collective-permute-start | bytes 516104 | tf_op jit(solution)/shard_map/ppermute | solution.py:359
  27.8 8.1 %collective-permute-start.17 = (bf16[168,512]{1,0:T(8,128)(2,1)S(1)}, bf16[168,512]{1,0:T(8,128)(2,1)S(1)}, u32[]{:S(2)}, u32[]{:S(2)}) collective-permute-start(bf16[168,512]{1,0:T(8,128)(2,1)S(1)} %get-tuple-element.65.refs_4_), channel_id=1, source_target_pairs={{0,16},{8,24},{16,0},{24,8},{1,17},{9,25},{17,1},{25,9},{2,18},{10... | collective-permute-start | bytes 516104 | tf_op jit(solution)/shard_map/ppermute | solution.py:43
  48.0 8.3 %collective-permute-start.33 = (bf16[48,2048]{1,0:T(8,128)(2,1)S(1)}, bf16[48,2048]{1,0:T(8,128)(2,1)S(1)}, u32[]{:S(2)}, u32[]{:S(2)}) collective-permute-start(bf16[48,2048]{1,0:T(8,128)(2,1)S(1)} %get-tuple-element.86), channel_id=1, source_target_pairs={{0,2},{2,4},{4,6},{6,7},{7,5},{5,3},{3,1},{1,0},{8,10},{10,12},{12... | collective-permute-start | bytes 589832 | tf_op jit(solution)/shard_map/ppermute | solution.py:456
  49.6 8.4 %collective-permute-start.36 = (bf16[48,2048]{1,0:T(8,128)(2,1)S(1)}, bf16[48,2048]{1,0:T(8,128)(2,1)S(1)}, u32[]{:S(2)}, u32[]{:S(2)}) collective-permute-start(bf16[48,2048]{1,0:T(8,128)(2,1)S(1)} %get-tuple-element.89), channel_id=1, source_target_pairs={{2,0},{4,2},{6,4},{7,6},{5,7},{3,5},{1,3},{0,1},{10,8},{12,10},{14... | collective-permute-start | bytes 589832 | tf_op jit(solution)/shard_map/ppermute | solution.py:452
  52.1 7.3 %collective-permute-start.27 = (bf16[72,1024]{1,0:T(8,128)(2,1)S(1)}, bf16[72,1024]{1,0:T(8,128)(2,1)S(1)}, u32[]{:S(2)}, u32[]{:S(2)}) collective-permute-start(bf16[72,1024]{1,0:T(8,128)(2,1)S(1)} %add_convert_fusion.9), channel_id=1, source_target_pairs={{0,2},{2,4},{4,6},{6,7},{7,5},{5,3},{3,1},{1,0},{8,10},{10,12},{12... | collective-permute-start | bytes 442376 | tf_op jit(solution)/shard_map/ppermute | solution.py:451
  53.8 7.3 %collective-permute-start.31 = (bf16[72,1024]{1,0:T(8,128)(2,1)S(1)}, bf16[72,1024]{1,0:T(8,128)(2,1)S(1)}, u32[]{:S(2)}, u32[]{:S(2)}) collective-permute-start(bf16[72,1024]{1,0:T(8,128)(2,1)S(1)} %add_convert_fusion.6), channel_id=1, source_target_pairs={{2,0},{4,2},{6,4},{7,6},{5,7},{3,5},{1,3},{0,1},{10,8},{12,10},{14... | collective-permute-start | bytes 442376 | tf_op jit(solution)/shard_map/ppermute | solution.py:457
  56.4 7.9 %collective-permute-start.34 = (bf16[48,2048]{1,0:T(8,128)(2,1)S(1)}, bf16[48,2048]{1,0:T(8,128)(2,1)S(1)}, u32[]{:S(2)}, u32[]{:S(2)}) collective-permute-start(bf16[48,2048]{1,0:T(8,128)(2,1)S(1)} %add_convert_fusion.4), channel_id=1, source_target_pairs={{0,2},{2,4},{4,6},{6,7},{7,5},{5,3},{3,1},{1,0},{8,10},{10,12},{12... | collective-permute-start | bytes 589832 | tf_op jit(solution)/shard_map/ppermute | solution.py:456
  58.1 7.9 %collective-permute-start.37 = (bf16[48,2048]{1,0:T(8,128)(2,1)S(1)}, bf16[48,2048]{1,0:T(8,128)(2,1)S(1)}, u32[]{:S(2)}, u32[]{:S(2)}) collective-permute-start(bf16[48,2048]{1,0:T(8,128)(2,1)S(1)} %add_convert_fusion.2), channel_id=1, source_target_pairs={{2,0},{4,2},{6,4},{7,6},{5,7},{3,5},{1,3},{0,1},{10,8},{12,10},{14... | collective-permute-start | bytes 589832 | tf_op jit(solution)/shard_map/ppermute | solution.py:452
  59.5 7.9 %collective-permute-start.28 = (bf16[72,1024]{1,0:T(8,128)(2,1)S(1)}, bf16[72,1024]{1,0:T(8,128)(2,1)S(1)}, u32[]{:S(2)}, u32[]{:S(2)}) collective-permute-start(bf16[72,1024]{1,0:T(8,128)(2,1)S(1)} %add_convert_fusion.8), channel_id=1, source_target_pairs={{0,2},{2,4},{4,6},{6,7},{7,5},{5,3},{3,1},{1,0},{8,10},{10,12},{12... | collective-permute-start | bytes 442376 | tf_op jit(solution)/shard_map/ppermute | solution.py:451
  61.2 11.1 %collective-permute-start.32 = (bf16[72,1024]{1,0:T(8,128)(2,1)S(1)}, bf16[72,1024]{1,0:T(8,128)(2,1)S(1)}, u32[]{:S(2)}, u32[]{:S(2)}) collective-permute-start(bf16[72,1024]{1,0:T(8,128)(2,1)S(1)} %add_convert_fusion.5), channel_id=1, source_target_pairs={{2,0},{4,2},{6,4},{7,6},{5,7},{3,5},{1,3},{0,1},{10,8},{12,10},{14... | collective-permute-start | bytes 442376 | tf_op jit(solution)/shard_map/ppermute | solution.py:457
  64.3 11.2 %collective-permute-start.35 = (bf16[48,2048]{1,0:T(8,128)(2,1)S(1)}, bf16[48,2048]{1,0:T(8,128)(2,1)S(1)}, u32[]{:S(2)}, u32[]{:S(2)}) collective-permute-start(bf16[48,2048]{1,0:T(8,128)(2,1)S(1)} %add_convert_fusion.3), channel_id=1, source_target_pairs={{0,2},{2,4},{4,6},{6,7},{7,5},{5,3},{3,1},{1,0},{8,10},{10,12},{12... | collective-permute-start | bytes 589832 | tf_op jit(solution)/shard_map/ppermute | solution.py:456
  71.8 6.9 %collective-permute-start.39 = (bf16[48,2048]{1,0:T(8,128)(2,1)S(1)}, bf16[48,2048]{1,0:T(8,128)(2,1)S(1)}, u32[]{:S(2)}, u32[]{:S(2)}) collective-permute-start(bf16[48,2048]{1,0:T(8,128)(2,1)S(1)} %add_convert_fusion), channel_id=1, source_target_pairs={{2,0},{4,2},{6,4},{7,6},{5,7},{3,5},{1,3},{0,1},{10,8},{12,10},{14... | collective-permute-start | bytes 589832 | tf_op jit(solution)/shard_map/ppermute | solution.py:452
  (23 other events, 172.6 us)

commit v6 on v5

--- a/solution.py
+++ b/solution.py
@@ -310,7 +310,7 @@
             hbm=range(len(arrays)),
         )
 
-    weights, gains, ends = [], [], []
+    weights, gains = [], []
     waiting = []
     queries, pieces, groups = [], [], []
 
@@ -320,10 +320,6 @@
         weights.extend(held)
         gains.extend((vgains, tgains))
         return held[0]
-
-    def fetch_last(after):
-        ends.extend(fetched([video_output, text_output], [2, 2], after))
-        return ends[0]
 
     def project(after, direct=False):
         group = list(waiting)
@@ -409,13 +405,12 @@
     first = range(len(groups) - 1)
     outer = range(2, n_blk)
     query, *carried = attended(
-        some((0, 1), first),
+        some((0, 1), first) + some(outer, first[:-1]),
         queries,
         (len(queries),),
         attend_kernel,
         [jax.ShapeDtypeStruct((total_rows, cols), BF16), *state],
     )
-    carried = attended(some(outer, first[:-1]), [query, *carried], (0,), attend_kernel, state)
     lead = width // 3
     left_rows = video_rows + text_rows * (width // lead)
     shapes = [

time: 79.8 us -> 79.7 us (level)
    pallas_call x12 -> x11, Pallas kernels: 17.6 us -> 17.2 us  [call(): pl.pallas_call(kernel, out_shape=outs, in_specs=[SMEM if i in smem else H...]
  transfers between devices with their start and end apart: 43 -> 43, of which waited for: 15 -> 15; matrix products, arithmetic and copies ran while one was open for 1% -> 1% of each run, Pallas kernels for 17% -> 16%
where the time goes in v6:
time: 79.7 us; the launch traced here: 79.6 us
  starting transfers between devices  40.6 us (51%)
  waiting for transfers between devices  20.5 us (26%)
  Pallas kernels  17.2 us (22%)
  between operations  0.85 us (1%)
    pallas_call x11, Pallas kernels, call(): pl.pallas_call(kernel, out_shape=outs, in_specs=[SMEM if i in smem else H...  17.2 us
    ppermute x15, starting transfers between devices, across(): return lax.ppermute(block, 'blk', [(i, i ^ distance) for i in range(n)])  10.5 us
    ppermute x4, starting transfers between devices, local(): fa = lax.ppermute(tied(fa, *due) if due else fa, 'uly', ahead)  9.18 us
    ppermute x4, starting transfers between devices, local(): fa = lax.ppermute(fa, 'uly', ahead)  6.51 us
    ppermute x3, starting transfers between devices, local(): fb = lax.ppermute(tied(fb, *due) if due else fb, 'uly', ahead)  5.89 us
    ppermute x4, waiting for transfers between devices, local(): fa = lax.ppermute(fa, 'uly', ahead)  5.02 us
    ppermute x3, starting transfers between devices, local(): fb = lax.ppermute(fb, 'uly', ahead)  4.89 us
    ppermute x3, waiting for transfers between devices, local(): fb = lax.ppermute(fb, 'uly', ahead)  4.56 us
  transfers between devices with their start and end apart: 43, of which 15 were waited for; matrix products, arithmetic and copies ran while one was open for 1% of the time, Pallas kernels for 16%

profile of v6, /device:TPU:0, one launch (start us, length us, event | category | flops | bytes accessed | tf_op | source)
XLA Modules:
  0.0 79.6 jit_solution(9226307448696653535)
XLA Ops:
  2.1 3.1 %collective-permute-start.1 = (bf16[56,1536]{1,0:T(8,128)(2,1)S(1)}, bf16[56,1536]{1,0:T(8,128)(2,1)S(1)}, u32[]{:S(2)}, u32[]{:S(2)}) collective-permute-start(bf16[56,1536]{1,0:T(8,128)(2,1)S(1)} %get-tuple-element.48.refs_0_), channel_id=1, source_target_pairs={{0,2},{2,4},{4,6},{6,7},{7,5},{5,3},{3,1},{1,0},{8,10},{10,12},{12... | collective-permute-start | bytes 516104 | tf_op jit(solution)/shard_map/ppermute | solution.py:355
  5.2 2.0 %collective-permute-start = (bf16[56,1536]{1,0:T(8,128)(2,1)S(1)}, bf16[56,1536]{1,0:T(8,128)(2,1)S(1)}, u32[]{:S(2)}, u32[]{:S(2)}) collective-permute-start(bf16[56,1536]{1,0:T(8,128)(2,1)S(1)} %get-tuple-element.47.refs_1_), channel_id=1, source_target_pairs={{0,2},{2,4},{4,6},{6,7},{7,5},{5,3},{3,1},{1,0},{8,10},{10,12},{12... | collective-permute-start | bytes 516104 | tf_op jit(solution)/shard_map/ppermute | solution.py:360
  7.2 3.8 %shard_map.114 = (bf16[3,3072,256]{2,1,0:T(8,128)(2,1)S(1)}, bf16[3,3072,256]{2,1,0:T(8,128)(2,1)S(1)}, f32[2,128]{1,0:T(2,128)S(1)}, f32[2,128]{1,0:T(2,128)S(1)}) custom-call(bf16[3,3072,256]{2,1,0:T(8,128)(2,1)} %bitcast.3, bf16[3,3072,256]{2,1,0:T(8,128)(2,1)} %bitcast.4, f32[2,128]{1,0:T(2,128)} %refs_2_.3, f32[2,128]{1,0:T(2,128)} %refs_3_.3), custom_call_target="tpu_custom_call" | custom-call | bytes 9439232 | tf_op jit(solution)/shard_map/pallas_call | solution.py:23
  11.0 2.1 %collective-permute-start.4 = (bf16[56,1536]{1,0:T(8,128)(2,1)S(1)}, bf16[56,1536]{1,0:T(8,128)(2,1)S(1)}, u32[]{:S(2)}, u32[]{:S(2)}) collective-permute-start(bf16[56,1536]{1,0:T(8,128)(2,1)S(1)} %collective-permute-done.1.refs_2_), channel_id=1, source_target_pairs={{0,2},{2,4},{4,6},{6,7},{7,5},{5,3},{3,1},{1,0},{8,10},{10,12},{12... | collective-permute-start | bytes 516104 | tf_op jit(solution)/shard_map/ppermute | solution.py:355
  13.6 1.9 %collective-permute-start.5 = (bf16[56,1536]{1,0:T(8,128)(2,1)S(1)}, bf16[56,1536]{1,0:T(8,128)(2,1)S(1)}, u32[]{:S(2)}, u32[]{:S(2)}) collective-permute-start(bf16[56,1536]{1,0:T(8,128)(2,1)S(1)} %collective-permute-done.refs_3_), channel_id=1, source_target_pairs={{0,2},{2,4},{4,6},{6,7},{7,5},{5,3},{3,1},{1,0},{8,10},{10,12},{12... | collective-permute-start | bytes 516104 | tf_op jit(solution)/shard_map/ppermute | solution.py:360
  18.4 2.0 %collective-permute-start.8 = (bf16[56,1536]{1,0:T(8,128)(2,1)S(1)}, bf16[56,1536]{1,0:T(8,128)(2,1)S(1)}, u32[]{:S(2)}, u32[]{:S(2)}) collective-permute-start(bf16[56,1536]{1,0:T(8,128)(2,1)S(1)} %collective-permute-done.4.refs_0_), channel_id=1, source_target_pairs={{0,2},{2,4},{4,6},{6,7},{7,5},{5,3},{3,1},{1,0},{8,10},{10,12},{12... | collective-permute-start | bytes 516104 | tf_op jit(solution)/shard_map/ppermute | solution.py:355
  20.4 1.6 %collective-permute-done.5.refs_1_ = bf16[56,1536]{1,0:T(8,128)(2,1)S(1)} collective-permute-done((bf16[56,1536]{1,0:T(8,128)(2,1)S(1)}, bf16[56,1536]{1,0:T(8,128)(2,1)S(1)}, u32[]{:S(2)}, u32[]{:S(2)}) %collective-permute-start.5) | collective-permute-done | bytes 172064 | tf_op jit(solution)/shard_map/ppermute | solution.py:360
  22.1 2.0 %collective-permute-start.9 = (bf16[56,1536]{1,0:T(8,128)(2,1)S(1)}, bf16[56,1536]{1,0:T(8,128)(2,1)S(1)}, u32[]{:S(2)}, u32[]{:S(2)}) collective-permute-start(bf16[56,1536]{1,0:T(8,128)(2,1)S(1)} %collective-permute-done.5.refs_1_), channel_id=1, source_target_pairs={{0,2},{2,4},{4,6},{6,7},{7,5},{5,3},{3,1},{1,0},{8,10},{10,12},{12... | collective-permute-start | bytes 516104 | tf_op jit(solution)/shard_map/ppermute | solution.py:360
  25.8 2.0 %collective-permute-start.12 = (bf16[56,1536]{1,0:T(8,128)(2,1)S(1)}, bf16[56,1536]{1,0:T(8,128)(2,1)S(1)}, u32[]{:S(2)}, u32[]{:S(2)}) collective-permute-start(bf16[56,1536]{1,0:T(8,128)(2,1)S(1)} %collective-permute-done.8.refs_0_), channel_id=1, source_target_pairs={{0,2},{2,4},{4,6},{6,7},{7,5},{5,3},{3,1},{1,0},{8,10},{10,12},{12... | collective-permute-start | bytes 516104 | tf_op jit(solution)/shard_map/ppermute | solution.py:355
  27.8 1.9 %collective-permute-start.17 = (bf16[168,512]{1,0:T(8,128)(2,1)S(1)}, bf16[168,512]{1,0:T(8,128)(2,1)S(1)}, u32[]{:S(2)}, u32[]{:S(2)}) collective-permute-start(bf16[168,512]{1,0:T(8,128)(2,1)S(1)} %get-tuple-element.63.refs_4_), channel_id=1, source_target_pairs={{0,16},{8,24},{16,0},{24,8},{1,17},{9,25},{17,1},{25,9},{2,18},{10... | collective-permute-start | bytes 516104 | tf_op jit(solution)/shard_map/ppermute | solution.py:43
  29.7 1.7 %collective-permute-start.18 = (bf16[112,512]{1,0:T(8,128)(2,1)S(1)}, bf16[112,512]{1,0:T(8,128)(2,1)S(1)}, u32[]{:S(2)}, u32[]{:S(2)}) collective-permute-start(bf16[112,512]{1,0:T(8,128)(2,1)S(1)} %get-tuple-element.64.refs_5_), channel_id=1, source_target_pairs={{0,16},{8,24},{16,0},{24,8},{1,17},{9,25},{17,1},{25,9},{2,18},{10... | collective-permute-start | bytes 344072 | tf_op jit(solution)/shard_map/ppermute | solution.py:43
  40.1 2.7 %shard_map.119 = (bf16[448,256]{1,0:T(8,128)(2,1)S(1)}, f32[4,448]{1,0:T(4,128)S(1)}, f32[256,448]{1,0:T(8,128)S(1)}) custom-call(bf16[168,256]{1,0:T(8,128)(2,1)S(1)} %get-tuple-element.54.refs_0_, bf16[112,256]{1,0:T(8,128)(2,1)S(1)} %get-tuple-element.57.refs_1_, bf16[112,256]{1,0:T(8,128)(2,1)S(1)} %get-tuple-element.60.refs_2_, ...), custom_call_target="tpu_custom_call" | custom-call | flops 616562688 | bytes 1605632 | tf_op jit(solution)/shard_map/pallas_call | solution.py:23
  43.5 1.9 %shard_map.120 = (bf16[384,256]{1,0:T(8,128)(2,1)S(1)}, bf16[72,1024]{1,0:T(8,128)(2,1)S(1)}, bf16[72,1024]{1,0:T(8,128)(2,1)S(1)}, bf16[72,1024]{1,0:T(8,128)(2...) custom-call(bf16[448,256]{1,0:T(8,128)(2,1)S(1)} %get-tuple-element., ...), custom_call_target="tpu_custom_call" | custom-call | flops 910163968 | bytes 4299776 | tf_op jit(solution)/shard_map/pallas_call | solution.py:23
  48.0 1.6 %collective-permute-start.33 = (bf16[48,2048]{1,0:T(8,128)(2,1)S(1)}, bf16[48,2048]{1,0:T(8,128)(2,1)S(1)}, u32[]{:S(2)}, u32[]{:S(2)}) collective-permute-start(bf16[48,2048]{1,0:T(8,128)(2,1)S(1)} %get-tuple-element.82), channel_id=1, source_target_pairs={{0,2},{2,4},{4,6},{6,7},{7,5},{5,3},{3,1},{1,0},{8,10},{10,12},{12... | collective-permute-start | bytes 589832 | tf_op jit(solution)/shard_map/ppermute | solution.py:451
  50.1 2.0 %collective-permute-done.26 = bf16[72,1024]{1,0:T(8,128)(2,1)S(1)} collective-permute-done((bf16[72,1024]{1,0:T(8,128)(2,1)S(1)}, bf16[72,1024]{1,0:T(8,128)(2,1)S(1)}, u32[]{:S(2)}, u32[]{:S(2)}) %collective-permute-start.26) | collective-permute-done | bytes 147488 | tf_op jit(solution)/shard_map/ppermute | solution.py:446
  52.2 1.6 %collective-permute-start.27 = (bf16[72,1024]{1,0:T(8,128)(2,1)S(1)}, bf16[72,1024]{1,0:T(8,128)(2,1)S(1)}, u32[]{:S(2)}, u32[]{:S(2)}) collective-permute-start(bf16[72,1024]{1,0:T(8,128)(2,1)S(1)} %add_convert_fusion.9), channel_id=1, source_target_pairs={{0,2},{2,4},{4,6},{6,7},{7,5},{5,3},{3,1},{1,0},{8,10},{10,12},{12... | collective-permute-start | bytes 442376 | tf_op jit(solution)/shard_map/ppermute | solution.py:446
  54.3 2.0 %collective-permute-done.33 = bf16[48,2048]{1,0:T(8,128)(2,1)S(1)} collective-permute-done((bf16[48,2048]{1,0:T(8,128)(2,1)S(1)}, bf16[48,2048]{1,0:T(8,128)(2,1)S(1)}, u32[]{:S(2)}, u32[]{:S(2)}) %collective-permute-start.33) | collective-permute-done | bytes 196640 | tf_op jit(solution)/shard_map/ppermute | solution.py:451
  56.4 1.6 %collective-permute-start.34 = (bf16[48,2048]{1,0:T(8,128)(2,1)S(1)}, bf16[48,2048]{1,0:T(8,128)(2,1)S(1)}, u32[]{:S(2)}, u32[]{:S(2)}) collective-permute-start(bf16[48,2048]{1,0:T(8,128)(2,1)S(1)} %add_convert_fusion.4), channel_id=1, source_target_pairs={{0,2},{2,4},{4,6},{6,7},{7,5},{5,3},{3,1},{1,0},{8,10},{10,12},{12... | collective-permute-start | bytes 589832 | tf_op jit(solution)/shard_map/ppermute | solution.py:451
  59.5 1.6 %collective-permute-start.28 = (bf16[72,1024]{1,0:T(8,128)(2,1)S(1)}, bf16[72,1024]{1,0:T(8,128)(2,1)S(1)}, u32[]{:S(2)}, u32[]{:S(2)}) collective-permute-start(bf16[72,1024]{1,0:T(8,128)(2,1)S(1)} %add_convert_fusion.8), channel_id=1, source_target_pairs={{0,2},{2,4},{4,6},{6,7},{7,5},{5,3},{3,1},{1,0},{8,10},{10,12},{12... | collective-permute-start | bytes 442376 | tf_op jit(solution)/shard_map/ppermute | solution.py:446
  61.7 2.6 %collective-permute-done.34 = bf16[48,2048]{1,0:T(8,128)(2,1)S(1)} collective-permute-done((bf16[48,2048]{1,0:T(8,128)(2,1)S(1)}, bf16[48,2048]{1,0:T(8,128)(2,1)S(1)}, u32[]{:S(2)}, u32[]{:S(2)}) %collective-permute-start.34) | collective-permute-done | bytes 196640 | tf_op jit(solution)/shard_map/ppermute | solution.py:451
  64.3 1.6 %collective-permute-start.35 = (bf16[48,2048]{1,0:T(8,128)(2,1)S(1)}, bf16[48,2048]{1,0:T(8,128)(2,1)S(1)}, u32[]{:S(2)}, u32[]{:S(2)}) collective-permute-start(bf16[48,2048]{1,0:T(8,128)(2,1)S(1)} %add_convert_fusion.3), channel_id=1, source_target_pairs={{0,2},{2,4},{4,6},{6,7},{7,5},{5,3},{3,1},{1,0},{8,10},{10,12},{12... | collective-permute-start | bytes 589832 | tf_op jit(solution)/shard_map/ppermute | solution.py:451
  67.5 1.6 %collective-permute-start.29 = (bf16[72,1024]{1,0:T(8,128)(2,1)S(1)}, bf16[72,1024]{1,0:T(8,128)(2,1)S(1)}, u32[]{:S(2)}, u32[]{:S(2)}) collective-permute-start(bf16[72,1024]{1,0:T(8,128)(2,1)S(1)} %add_convert_fusion.7), channel_id=1, source_target_pairs={{0,2},{2,4},{4,6},{6,7},{7,5},{5,3},{3,1},{1,0},{8,10},{10,12},{12... | collective-permute-start | bytes 442376 | tf_op jit(solution)/shard_map/ppermute | solution.py:446
  69.1 2.6 %collective-permute-done.38 = bf16[48,2048]{1,0:T(8,128)(2,1)S(1)} collective-permute-done((bf16[48,2048]{1,0:T(8,128)(2,1)S(1)}, bf16[48,2048]{1,0:T(8,128)(2,1)S(1)}, u32[]{:S(2)}, u32[]{:S(2)}) %collective-permute-start.38) | collective-permute-done | bytes 196640 | tf_op jit(solution)/shard_map/ppermute | solution.py:447
  75.4 2.3 %collective-permute-done.41.refs_2_ = bf16[8,3072]{1,0:T(8,128)(2,1)S(1)} collective-permute-done((bf16[8,3072]{1,0:T(8,128)(2,1)S(1)}, bf16[8,3072]{1,0:T(8,128)(2,1)S(1)}, u32[]{:S(2)}, u32[]{:S(2)}) %collective-permute-start.41) | collective-permute-done | bytes 49184 | tf_op jit(solution)/shard_map/ppermute | solution.py:43
  (91 shorter events, 28.8 us)
Async XLA Ops:
  2.1 8.9 %collective-permute-start.1 = (bf16[56,1536]{1,0:T(8,128)(2,1)S(1)}, bf16[56,1536]{1,0:T(8,128)(2,1)S(1)}, u32[]{:S(2)}, u32[]{:S(2)}) collective-permute-start(bf16[56,1536]{1,0:T(8,128)(2,1)S(1)} %get-tuple-element.48.refs_0_), channel_id=1, source_target_pairs={{0,2},{2,4},{4,6},{6,7},{7,5},{5,3},{3,1},{1,0},{8,10},{10,12},{12... | collective-permute-start | bytes 516104 | tf_op jit(solution)/shard_map/ppermute | solution.py:355
  5.2 7.9 %collective-permute-start.3 = (bf16[56,1536]{1,0:T(8,128)(2,1)S(1)}, bf16[56,1536]{1,0:T(8,128)(2,1)S(1)}, u32[]{:S(2)}, u32[]{:S(2)}) collective-permute-start(bf16[56,1536]{1,0:T(8,128)(2,1)S(1)} %get-tuple-element.47.refs_1_), channel_id=1, source_target_pairs={{2,0},{4,2},{6,4},{7,6},{5,7},{3,5},{1,3},{0,1},{10,8},{12,10},{14... | collective-permute-start | bytes 516104 | tf_op jit(solution)/shard_map/ppermute | solution.py:356
  5.2 8.4 %collective-permute-start = (bf16[56,1536]{1,0:T(8,128)(2,1)S(1)}, bf16[56,1536]{1,0:T(8,128)(2,1)S(1)}, u32[]{:S(2)}, u32[]{:S(2)}) collective-permute-start(bf16[56,1536]{1,0:T(8,128)(2,1)S(1)} %get-tuple-element.47.refs_1_), channel_id=1, source_target_pairs={{0,2},{2,4},{4,6},{6,7},{7,5},{5,3},{3,1},{1,0},{8,10},{10,12},{12... | collective-permute-start | bytes 516104 | tf_op jit(solution)/shard_map/ppermute | solution.py:360
  7.2 8.3 %collective-permute-start.2 = (bf16[56,1536]{1,0:T(8,128)(2,1)S(1)}, bf16[56,1536]{1,0:T(8,128)(2,1)S(1)}, u32[]{:S(2)}, u32[]{:S(2)}) collective-permute-start(bf16[56,1536]{1,0:T(8,128)(2,1)S(1)} %get-tuple-element.48.refs_0_), channel_id=1, source_target_pairs={{2,0},{4,2},{6,4},{7,6},{5,7},{3,5},{1,3},{0,1},{10,8},{12,10},{14... | collective-permute-start | bytes 516104 | tf_op jit(solution)/shard_map/ppermute | solution.py:361
  11.0 7.4 %collective-permute-start.4 = (bf16[56,1536]{1,0:T(8,128)(2,1)S(1)}, bf16[56,1536]{1,0:T(8,128)(2,1)S(1)}, u32[]{:S(2)}, u32[]{:S(2)}) collective-permute-start(bf16[56,1536]{1,0:T(8,128)(2,1)S(1)} %collective-permute-done.1.refs_2_), channel_id=1, source_target_pairs={{0,2},{2,4},{4,6},{6,7},{7,5},{5,3},{3,1},{1,0},{8,10},{10,12},{12... | collective-permute-start | bytes 516104 | tf_op jit(solution)/shard_map/ppermute | solution.py:355
  13.1 7.3 %collective-permute-start.7 = (bf16[56,1536]{1,0:T(8,128)(2,1)S(1)}, bf16[56,1536]{1,0:T(8,128)(2,1)S(1)}, u32[]{:S(2)}, u32[]{:S(2)}) collective-permute-start(bf16[56,1536]{1,0:T(8,128)(2,1)S(1)} %collective-permute-done.3.refs_5_), channel_id=1, source_target_pairs={{2,0},{4,2},{6,4},{7,6},{5,7},{3,5},{1,3},{0,1},{10,8},{12,10},{14... | collective-permute-start | bytes 516104 | tf_op jit(solution)/shard_map/ppermute | solution.py:356
  13.6 8.5 %collective-permute-start.5 = (bf16[56,1536]{1,0:T(8,128)(2,1)S(1)}, bf16[56,1536]{1,0:T(8,128)(2,1)S(1)}, u32[]{:S(2)}, u32[]{:S(2)}) collective-permute-start(bf16[56,1536]{1,0:T(8,128)(2,1)S(1)} %collective-permute-done.refs_3_), channel_id=1, source_target_pairs={{0,2},{2,4},{4,6},{6,7},{7,5},{5,3},{3,1},{1,0},{8,10},{10,12},{12... | collective-permute-start | bytes 516104 | tf_op jit(solution)/shard_map/ppermute | solution.py:360
  15.5 8.6 %collective-permute-start.6 = (bf16[56,1536]{1,0:T(8,128)(2,1)S(1)}, bf16[56,1536]{1,0:T(8,128)(2,1)S(1)}, u32[]{:S(2)}, u32[]{:S(2)}) collective-permute-start(bf16[56,1536]{1,0:T(8,128)(2,1)S(1)} %collective-permute-done.2.refs_4_), channel_id=1, source_target_pairs={{2,0},{4,2},{6,4},{7,6},{5,7},{3,5},{1,3},{0,1},{10,8},{12,10},{14... | collective-permute-start | bytes 516104 | tf_op jit(solution)/shard_map/ppermute | solution.py:361
  18.4 7.4 %collective-permute-start.8 = (bf16[56,1536]{1,0:T(8,128)(2,1)S(1)}, bf16[56,1536]{1,0:T(8,128)(2,1)S(1)}, u32[]{:S(2)}, u32[]{:S(2)}) collective-permute-start(bf16[56,1536]{1,0:T(8,128)(2,1)S(1)} %collective-permute-done.4.refs_0_), channel_id=1, source_target_pairs={{0,2},{2,4},{4,6},{6,7},{7,5},{5,3},{3,1},{1,0},{8,10},{10,12},{12... | collective-permute-start | bytes 516104 | tf_op jit(solution)/shard_map/ppermute | solution.py:355
  20.4 7.4 %collective-permute-start.11 = (bf16[56,1536]{1,0:T(8,128)(2,1)S(1)}, bf16[56,1536]{1,0:T(8,128)(2,1)S(1)}, u32[]{:S(2)}, u32[]{:S(2)}) collective-permute-start(bf16[56,1536]{1,0:T(8,128)(2,1)S(1)} %collective-permute-done.7.refs_3_), channel_id=1, source_target_pairs={{2,0},{4,2},{6,4},{7,6},{5,7},{3,5},{1,3},{0,1},{10,8},{12,10},{14... | collective-permute-start | bytes 516104 | tf_op jit(solution)/shard_map/ppermute | solution.py:356
  22.1 7.7 %collective-permute-start.9 = (bf16[56,1536]{1,0:T(8,128)(2,1)S(1)}, bf16[56,1536]{1,0:T(8,128)(2,1)S(1)}, u32[]{:S(2)}, u32[]{:S(2)}) collective-permute-start(bf16[56,1536]{1,0:T(8,128)(2,1)S(1)} %collective-permute-done.5.refs_1_), channel_id=1, source_target_pairs={{0,2},{2,4},{4,6},{6,7},{7,5},{5,3},{3,1},{1,0},{8,10},{10,12},{12... | collective-permute-start | bytes 516104 | tf_op jit(solution)/shard_map/ppermute | solution.py:360
  24.1 7.3 %collective-permute-start.10 = (bf16[56,1536]{1,0:T(8,128)(2,1)S(1)}, bf16[56,1536]{1,0:T(8,128)(2,1)S(1)}, u32[]{:S(2)}, u32[]{:S(2)}) collective-permute-start(bf16[56,1536]{1,0:T(8,128)(2,1)S(1)} %collective-permute-done.6.refs_2_), channel_id=1, source_target_pairs={{2,0},{4,2},{6,4},{7,6},{5,7},{3,5},{1,3},{0,1},{10,8},{12,10},{14... | collective-permute-start | bytes 516104 | tf_op jit(solution)/shard_map/ppermute | solution.py:361
  25.8 8.5 %collective-permute-start.12 = (bf16[56,1536]{1,0:T(8,128)(2,1)S(1)}, bf16[56,1536]{1,0:T(8,128)(2,1)S(1)}, u32[]{:S(2)}, u32[]{:S(2)}) collective-permute-start(bf16[56,1536]{1,0:T(8,128)(2,1)S(1)} %collective-permute-done.8.refs_0_), channel_id=1, source_target_pairs={{0,2},{2,4},{4,6},{6,7},{7,5},{5,3},{3,1},{1,0},{8,10},{10,12},{12... | collective-permute-start | bytes 516104 | tf_op jit(solution)/shard_map/ppermute | solution.py:355
  27.8 8.1 %collective-permute-start.17 = (bf16[168,512]{1,0:T(8,128)(2,1)S(1)}, bf16[168,512]{1,0:T(8,128)(2,1)S(1)}, u32[]{:S(2)}, u32[]{:S(2)}) collective-permute-start(bf16[168,512]{1,0:T(8,128)(2,1)S(1)} %get-tuple-element.63.refs_4_), channel_id=1, source_target_pairs={{0,16},{8,24},{16,0},{24,8},{1,17},{9,25},{17,1},{25,9},{2,18},{10... | collective-permute-start | bytes 516104 | tf_op jit(solution)/shard_map/ppermute | solution.py:43
  48.0 8.3 %collective-permute-start.33 = (bf16[48,2048]{1,0:T(8,128)(2,1)S(1)}, bf16[48,2048]{1,0:T(8,128)(2,1)S(1)}, u32[]{:S(2)}, u32[]{:S(2)}) collective-permute-start(bf16[48,2048]{1,0:T(8,128)(2,1)S(1)} %get-tuple-element.82), channel_id=1, source_target_pairs={{0,2},{2,4},{4,6},{6,7},{7,5},{5,3},{3,1},{1,0},{8,10},{10,12},{12... | collective-permute-start | bytes 589832 | tf_op jit(solution)/shard_map/ppermute | solution.py:451
  49.7 8.4 %collective-permute-start.36 = (bf16[48,2048]{1,0:T(8,128)(2,1)S(1)}, bf16[48,2048]{1,0:T(8,128)(2,1)S(1)}, u32[]{:S(2)}, u32[]{:S(2)}) collective-permute-start(bf16[48,2048]{1,0:T(8,128)(2,1)S(1)} %get-tuple-element.85), channel_id=1, source_target_pairs={{2,0},{4,2},{6,4},{7,6},{5,7},{3,5},{1,3},{0,1},{10,8},{12,10},{14... | collective-permute-start | bytes 589832 | tf_op jit(solution)/shard_map/ppermute | solution.py:447
  52.2 7.3 %collective-permute-start.27 = (bf16[72,1024]{1,0:T(8,128)(2,1)S(1)}, bf16[72,1024]{1,0:T(8,128)(2,1)S(1)}, u32[]{:S(2)}, u32[]{:S(2)}) collective-permute-start(bf16[72,1024]{1,0:T(8,128)(2,1)S(1)} %add_convert_fusion.9), channel_id=1, source_target_pairs={{0,2},{2,4},{4,6},{6,7},{7,5},{5,3},{3,1},{1,0},{8,10},{10,12},{12... | collective-permute-start | bytes 442376 | tf_op jit(solution)/shard_map/ppermute | solution.py:446
  53.8 7.3 %collective-permute-start.31 = (bf16[72,1024]{1,0:T(8,128)(2,1)S(1)}, bf16[72,1024]{1,0:T(8,128)(2,1)S(1)}, u32[]{:S(2)}, u32[]{:S(2)}) collective-permute-start(bf16[72,1024]{1,0:T(8,128)(2,1)S(1)} %add_convert_fusion.6), channel_id=1, source_target_pairs={{2,0},{4,2},{6,4},{7,6},{5,7},{3,5},{1,3},{0,1},{10,8},{12,10},{14... | collective-permute-start | bytes 442376 | tf_op jit(solution)/shard_map/ppermute | solution.py:452
  56.4 7.9 %collective-permute-start.34 = (bf16[48,2048]{1,0:T(8,128)(2,1)S(1)}, bf16[48,2048]{1,0:T(8,128)(2,1)S(1)}, u32[]{:S(2)}, u32[]{:S(2)}) collective-permute-start(bf16[48,2048]{1,0:T(8,128)(2,1)S(1)} %add_convert_fusion.4), channel_id=1, source_target_pairs={{0,2},{2,4},{4,6},{6,7},{7,5},{5,3},{3,1},{1,0},{8,10},{10,12},{12... | collective-permute-start | bytes 589832 | tf_op jit(solution)/shard_map/ppermute | solution.py:451
  58.1 7.9 %collective-permute-start.37 = (bf16[48,2048]{1,0:T(8,128)(2,1)S(1)}, bf16[48,2048]{1,0:T(8,128)(2,1)S(1)}, u32[]{:S(2)}, u32[]{:S(2)}) collective-permute-start(bf16[48,2048]{1,0:T(8,128)(2,1)S(1)} %add_convert_fusion.2), channel_id=1, source_target_pairs={{2,0},{4,2},{6,4},{7,6},{5,7},{3,5},{1,3},{0,1},{10,8},{12,10},{14... | collective-permute-start | bytes 589832 | tf_op jit(solution)/shard_map/ppermute | solution.py:447
  59.5 7.9 %collective-permute-start.28 = (bf16[72,1024]{1,0:T(8,128)(2,1)S(1)}, bf16[72,1024]{1,0:T(8,128)(2,1)S(1)}, u32[]{:S(2)}, u32[]{:S(2)}) collective-permute-start(bf16[72,1024]{1,0:T(8,128)(2,1)S(1)} %add_convert_fusion.8), channel_id=1, source_target_pairs={{0,2},{2,4},{4,6},{6,7},{7,5},{5,3},{3,1},{1,0},{8,10},{10,12},{12... | collective-permute-start | bytes 442376 | tf_op jit(solution)/shard_map/ppermute | solution.py:446
  61.2 11.1 %collective-permute-start.32 = (bf16[72,1024]{1,0:T(8,128)(2,1)S(1)}, bf16[72,1024]{1,0:T(8,128)(2,1)S(1)}, u32[]{:S(2)}, u32[]{:S(2)}) collective-permute-start(bf16[72,1024]{1,0:T(8,128)(2,1)S(1)} %add_convert_fusion.5), channel_id=1, source_target_pairs={{2,0},{4,2},{6,4},{7,6},{5,7},{3,5},{1,3},{0,1},{10,8},{12,10},{14... | collective-permute-start | bytes 442376 | tf_op jit(solution)/shard_map/ppermute | solution.py:452
  64.3 11.1 %collective-permute-start.35 = (bf16[48,2048]{1,0:T(8,128)(2,1)S(1)}, bf16[48,2048]{1,0:T(8,128)(2,1)S(1)}, u32[]{:S(2)}, u32[]{:S(2)}) collective-permute-start(bf16[48,2048]{1,0:T(8,128)(2,1)S(1)} %add_convert_fusion.3), channel_id=1, source_target_pairs={{0,2},{2,4},{4,6},{6,7},{7,5},{5,3},{3,1},{1,0},{8,10},{10,12},{12... | collective-permute-start | bytes 589832 | tf_op jit(solution)/shard_map/ppermute | solution.py:451
  71.8 6.8 %collective-permute-start.39 = (bf16[48,2048]{1,0:T(8,128)(2,1)S(1)}, bf16[48,2048]{1,0:T(8,128)(2,1)S(1)}, u32[]{:S(2)}, u32[]{:S(2)}) collective-permute-start(bf16[48,2048]{1,0:T(8,128)(2,1)S(1)} %add_convert_fusion), channel_id=1, source_target_pairs={{2,0},{4,2},{6,4},{7,6},{5,7},{3,5},{1,3},{0,1},{10,8},{12,10},{14... | collective-permute-start | bytes 589832 | tf_op jit(solution)/shard_map/ppermute | solution.py:447
  (23 other events, 169.9 us)

commit v7 on v5

--- a/solution.py
+++ b/solution.py
@@ -109,9 +109,9 @@
     width = q_ref.shape[1]
     video, text = [], []
     for side in range(2):
-        floats = [chunks[2 * i + side][...].astype(F32) for i in range(shards)]
-        video.append(jnp.concatenate([f[:video_rows] for f in floats], axis=0).astype(BF16))
-        text.append(jnp.concatenate([f[video_rows:] for f in floats], axis=0).astype(BF16))
+        mine = [chunks[2 * i + side] for i in range(shards)]
+        video.append(jnp.concatenate([r[:video_rows, :] for r in mine], axis=0))
+        text.append(jnp.concatenate([r[...].astype(F32)[video_rows:] for r in mine], axis=0).astype(BF16))
     half = video[0].shape[1]
 
     def mixed(sides, w_ref, j):

time: 79.8 us -> 79.8 us (level)
  no operation moved by 1% of the time
where the time goes in v7:
time: 79.8 us; the launch traced here: 79.6 us
  starting transfers between devices  40.6 us (51%)
  waiting for transfers between devices  20.1 us (25%)
  Pallas kernels  17.6 us (22%)
  between operations  0.87 us (1%)
    pallas_call x12, Pallas kernels, call(): pl.pallas_call(kernel, out_shape=outs, in_specs=[SMEM if i in smem else H...  17.6 us
    ppermute x15, starting transfers between devices, across(): return lax.ppermute(block, 'blk', [(i, i ^ distance) for i in range(n)])  10.5 us
    ppermute x4, starting transfers between devices, local(): fa = lax.ppermute(tied(fa, *due) if due else fa, 'uly', ahead)  9.18 us
    ppermute x4, starting transfers between devices, local(): fa = lax.ppermute(fa, 'uly', ahead)  6.51 us
    ppermute x3, starting transfers between devices, local(): fb = lax.ppermute(tied(fb, *due) if due else fb, 'uly', ahead)  5.89 us
    ppermute x4, waiting for transfers between devices, local(): fa = lax.ppermute(fa, 'uly', ahead)  5.06 us
    ppermute x3, starting transfers between devices, local(): fb = lax.ppermute(fb, 'uly', ahead)  4.89 us
    ppermute x3, waiting for transfers between devices, local(): fb = lax.ppermute(fb, 'uly', ahead)  4.56 us
  transfers between devices with their start and end apart: 43, of which 15 were waited for; matrix products, arithmetic and copies ran while one was open for 1% of the time, Pallas kernels for 17%

profile of v7, /device:TPU:0, one launch (start us, length us, event | category | flops | bytes accessed | tf_op | source)
XLA Modules:
  0.0 79.6 jit_solution(6800848238758300630)
XLA Ops:
  2.1 3.1 %collective-permute-start.1 = (bf16[56,1536]{1,0:T(8,128)(2,1)S(1)}, bf16[56,1536]{1,0:T(8,128)(2,1)S(1)}, u32[]{:S(2)}, u32[]{:S(2)}) collective-permute-start(bf16[56,1536]{1,0:T(8,128)(2,1)S(1)} %get-tuple-element.50.refs_0_), channel_id=1, source_target_pairs={{0,2},{2,4},{4,6},{6,7},{7,5},{5,3},{3,1},{1,0},{8,10},{10,12},{12... | collective-permute-start | bytes 516104 | tf_op jit(solution)/shard_map/ppermute | solution.py:359
  5.2 2.0 %collective-permute-start = (bf16[56,1536]{1,0:T(8,128)(2,1)S(1)}, bf16[56,1536]{1,0:T(8,128)(2,1)S(1)}, u32[]{:S(2)}, u32[]{:S(2)}) collective-permute-start(bf16[56,1536]{1,0:T(8,128)(2,1)S(1)} %get-tuple-element.49.refs_1_), channel_id=1, source_target_pairs={{0,2},{2,4},{4,6},{6,7},{7,5},{5,3},{3,1},{1,0},{8,10},{10,12},{12... | collective-permute-start | bytes 516104 | tf_op jit(solution)/shard_map/ppermute | solution.py:364
  7.2 3.8 %shard_map.114 = (bf16[3,3072,256]{2,1,0:T(8,128)(2,1)S(1)}, bf16[3,3072,256]{2,1,0:T(8,128)(2,1)S(1)}, f32[2,128]{1,0:T(2,128)S(1)}, f32[2,128]{1,0:T(2,128)S(1)}) custom-call(bf16[3,3072,256]{2,1,0:T(8,128)(2,1)} %bitcast.3, bf16[3,3072,256]{2,1,0:T(8,128)(2,1)} %bitcast.4, f32[2,128]{1,0:T(2,128)} %refs_2_.3, f32[2,128]{1,0:T(2,128)} %refs_3_.3), custom_call_target="tpu_custom_call" | custom-call | bytes 9439232 | tf_op jit(solution)/shard_map/pallas_call | solution.py:23
  11.0 2.1 %collective-permute-start.4 = (bf16[56,1536]{1,0:T(8,128)(2,1)S(1)}, bf16[56,1536]{1,0:T(8,128)(2,1)S(1)}, u32[]{:S(2)}, u32[]{:S(2)}) collective-permute-start(bf16[56,1536]{1,0:T(8,128)(2,1)S(1)} %collective-permute-done.1.refs_2_), channel_id=1, source_target_pairs={{0,2},{2,4},{4,6},{6,7},{7,5},{5,3},{3,1},{1,0},{8,10},{10,12},{12... | collective-permute-start | bytes 516104 | tf_op jit(solution)/shard_map/ppermute | solution.py:359
  13.6 1.9 %collective-permute-start.5 = (bf16[56,1536]{1,0:T(8,128)(2,1)S(1)}, bf16[56,1536]{1,0:T(8,128)(2,1)S(1)}, u32[]{:S(2)}, u32[]{:S(2)}) collective-permute-start(bf16[56,1536]{1,0:T(8,128)(2,1)S(1)} %collective-permute-done.refs_3_), channel_id=1, source_target_pairs={{0,2},{2,4},{4,6},{6,7},{7,5},{5,3},{3,1},{1,0},{8,10},{10,12},{12... | collective-permute-start | bytes 516104 | tf_op jit(solution)/shard_map/ppermute | solution.py:364
  18.4 2.0 %collective-permute-start.8 = (bf16[56,1536]{1,0:T(8,128)(2,1)S(1)}, bf16[56,1536]{1,0:T(8,128)(2,1)S(1)}, u32[]{:S(2)}, u32[]{:S(2)}) collective-permute-start(bf16[56,1536]{1,0:T(8,128)(2,1)S(1)} %collective-permute-done.4.refs_0_), channel_id=1, source_target_pairs={{0,2},{2,4},{4,6},{6,7},{7,5},{5,3},{3,1},{1,0},{8,10},{10,12},{12... | collective-permute-start | bytes 516104 | tf_op jit(solution)/shard_map/ppermute | solution.py:359
  20.4 1.6 %collective-permute-done.5.refs_1_ = bf16[56,1536]{1,0:T(8,128)(2,1)S(1)} collective-permute-done((bf16[56,1536]{1,0:T(8,128)(2,1)S(1)}, bf16[56,1536]{1,0:T(8,128)(2,1)S(1)}, u32[]{:S(2)}, u32[]{:S(2)}) %collective-permute-start.5) | collective-permute-done | bytes 172064 | tf_op jit(solution)/shard_map/ppermute | solution.py:364
  22.1 2.0 %collective-permute-start.9 = (bf16[56,1536]{1,0:T(8,128)(2,1)S(1)}, bf16[56,1536]{1,0:T(8,128)(2,1)S(1)}, u32[]{:S(2)}, u32[]{:S(2)}) collective-permute-start(bf16[56,1536]{1,0:T(8,128)(2,1)S(1)} %collective-permute-done.5.refs_1_), channel_id=1, source_target_pairs={{0,2},{2,4},{4,6},{6,7},{7,5},{5,3},{3,1},{1,0},{8,10},{10,12},{12... | collective-permute-start | bytes 516104 | tf_op jit(solution)/shard_map/ppermute | solution.py:364
  25.8 2.0 %collective-permute-start.12 = (bf16[56,1536]{1,0:T(8,128)(2,1)S(1)}, bf16[56,1536]{1,0:T(8,128)(2,1)S(1)}, u32[]{:S(2)}, u32[]{:S(2)}) collective-permute-start(bf16[56,1536]{1,0:T(8,128)(2,1)S(1)} %collective-permute-done.8.refs_0_), channel_id=1, source_target_pairs={{0,2},{2,4},{4,6},{6,7},{7,5},{5,3},{3,1},{1,0},{8,10},{10,12},{12... | collective-permute-start | bytes 516104 | tf_op jit(solution)/shard_map/ppermute | solution.py:359
  27.8 1.9 %collective-permute-start.17 = (bf16[168,512]{1,0:T(8,128)(2,1)S(1)}, bf16[168,512]{1,0:T(8,128)(2,1)S(1)}, u32[]{:S(2)}, u32[]{:S(2)}) collective-permute-start(bf16[168,512]{1,0:T(8,128)(2,1)S(1)} %get-tuple-element.65.refs_4_), channel_id=1, source_target_pairs={{0,16},{8,24},{16,0},{24,8},{1,17},{9,25},{17,1},{25,9},{2,18},{10... | collective-permute-start | bytes 516104 | tf_op jit(solution)/shard_map/ppermute | solution.py:43
  29.7 1.7 %collective-permute-start.18 = (bf16[112,512]{1,0:T(8,128)(2,1)S(1)}, bf16[112,512]{1,0:T(8,128)(2,1)S(1)}, u32[]{:S(2)}, u32[]{:S(2)}) collective-permute-start(bf16[112,512]{1,0:T(8,128)(2,1)S(1)} %get-tuple-element.66.refs_5_), channel_id=1, source_target_pairs={{0,16},{8,24},{16,0},{24,8},{1,17},{9,25},{17,1},{25,9},{2,18},{10... | collective-permute-start | bytes 344072 | tf_op jit(solution)/shard_map/ppermute | solution.py:43
  40.1 1.7 %shard_map.119 = (bf16[448,256]{1,0:T(8,128)(2,1)S(1)}, f32[4,448]{1,0:T(4,128)S(1)}, f32[256,448]{1,0:T(8,128)S(1)}) custom-call(bf16[168,256]{1,0:T(8,128)(2,1)S(1)} %get-tuple-element.56.refs_0_, bf16[112,256]{1,0:T(8,128)(2,1)S(1)} %get-tuple-element.59.refs_1_, bf16[112,256]{1,0:T(8,128)(2,1)S(1)} %get-tuple-element.62.refs_2_, ...), custom_call_target="tpu_custom_call" | custom-call | flops 359661568 | bytes 1032192 | tf_op jit(solution)/shard_map/pallas_call | solution.py:23
  43.5 1.9 %shard_map.121 = (bf16[384,256]{1,0:T(8,128)(2,1)S(1)}, bf16[72,1024]{1,0:T(8,128)(2,1)S(1)}, bf16[72,1024]{1,0:T(8,128)(2,1)S(1)}, bf16[72,1024]{1,0:T(8,128)(2...) custom-call(bf16[448,256]{1,0:T(8,128)(2,1)S(1)} %get-tuple-element., ...), custom_call_target="tpu_custom_call" | custom-call | flops 910163968 | bytes 4299776 | tf_op jit(solution)/shard_map/pallas_call | solution.py:23
  48.0 1.6 %collective-permute-start.33 = (bf16[48,2048]{1,0:T(8,128)(2,1)S(1)}, bf16[48,2048]{1,0:T(8,128)(2,1)S(1)}, u32[]{:S(2)}, u32[]{:S(2)}) collective-permute-start(bf16[48,2048]{1,0:T(8,128)(2,1)S(1)} %get-tuple-element.86), channel_id=1, source_target_pairs={{0,2},{2,4},{4,6},{6,7},{7,5},{5,3},{3,1},{1,0},{8,10},{10,12},{12... | collective-permute-start | bytes 589832 | tf_op jit(solution)/shard_map/ppermute | solution.py:456
  50.1 2.0 %collective-permute-done.26 = bf16[72,1024]{1,0:T(8,128)(2,1)S(1)} collective-permute-done((bf16[72,1024]{1,0:T(8,128)(2,1)S(1)}, bf16[72,1024]{1,0:T(8,128)(2,1)S(1)}, u32[]{:S(2)}, u32[]{:S(2)}) %collective-permute-start.26) | collective-permute-done | bytes 147488 | tf_op jit(solution)/shard_map/ppermute | solution.py:451
  52.1 1.6 %collective-permute-start.27 = (bf16[72,1024]{1,0:T(8,128)(2,1)S(1)}, bf16[72,1024]{1,0:T(8,128)(2,1)S(1)}, u32[]{:S(2)}, u32[]{:S(2)}) collective-permute-start(bf16[72,1024]{1,0:T(8,128)(2,1)S(1)} %add_convert_fusion.9), channel_id=1, source_target_pairs={{0,2},{2,4},{4,6},{6,7},{7,5},{5,3},{3,1},{1,0},{8,10},{10,12},{12... | collective-permute-start | bytes 442376 | tf_op jit(solution)/shard_map/ppermute | solution.py:451
  54.3 2.0 %collective-permute-done.33 = bf16[48,2048]{1,0:T(8,128)(2,1)S(1)} collective-permute-done((bf16[48,2048]{1,0:T(8,128)(2,1)S(1)}, bf16[48,2048]{1,0:T(8,128)(2,1)S(1)}, u32[]{:S(2)}, u32[]{:S(2)}) %collective-permute-start.33) | collective-permute-done | bytes 196640 | tf_op jit(solution)/shard_map/ppermute | solution.py:456
  56.4 1.6 %collective-permute-start.34 = (bf16[48,2048]{1,0:T(8,128)(2,1)S(1)}, bf16[48,2048]{1,0:T(8,128)(2,1)S(1)}, u32[]{:S(2)}, u32[]{:S(2)}) collective-permute-start(bf16[48,2048]{1,0:T(8,128)(2,1)S(1)} %add_convert_fusion.4), channel_id=1, source_target_pairs={{0,2},{2,4},{4,6},{6,7},{7,5},{5,3},{3,1},{1,0},{8,10},{10,12},{12... | collective-permute-start | bytes 589832 | tf_op jit(solution)/shard_map/ppermute | solution.py:456
  59.5 1.6 %collective-permute-start.28 = (bf16[72,1024]{1,0:T(8,128)(2,1)S(1)}, bf16[72,1024]{1,0:T(8,128)(2,1)S(1)}, u32[]{:S(2)}, u32[]{:S(2)}) collective-permute-start(bf16[72,1024]{1,0:T(8,128)(2,1)S(1)} %add_convert_fusion.8), channel_id=1, source_target_pairs={{0,2},{2,4},{4,6},{6,7},{7,5},{5,3},{3,1},{1,0},{8,10},{10,12},{12... | collective-permute-start | bytes 442376 | tf_op jit(solution)/shard_map/ppermute | solution.py:451
  61.7 2.6 %collective-permute-done.34 = bf16[48,2048]{1,0:T(8,128)(2,1)S(1)} collective-permute-done((bf16[48,2048]{1,0:T(8,128)(2,1)S(1)}, bf16[48,2048]{1,0:T(8,128)(2,1)S(1)}, u32[]{:S(2)}, u32[]{:S(2)}) %collective-permute-start.34) | collective-permute-done | bytes 196640 | tf_op jit(solution)/shard_map/ppermute | solution.py:456
  64.3 1.6 %collective-permute-start.35 = (bf16[48,2048]{1,0:T(8,128)(2,1)S(1)}, bf16[48,2048]{1,0:T(8,128)(2,1)S(1)}, u32[]{:S(2)}, u32[]{:S(2)}) collective-permute-start(bf16[48,2048]{1,0:T(8,128)(2,1)S(1)} %add_convert_fusion.3), channel_id=1, source_target_pairs={{0,2},{2,4},{4,6},{6,7},{7,5},{5,3},{3,1},{1,0},{8,10},{10,12},{12... | collective-permute-start | bytes 589832 | tf_op jit(solution)/shard_map/ppermute | solution.py:456
  67.5 1.6 %collective-permute-start.29 = (bf16[72,1024]{1,0:T(8,128)(2,1)S(1)}, bf16[72,1024]{1,0:T(8,128)(2,1)S(1)}, u32[]{:S(2)}, u32[]{:S(2)}) collective-permute-start(bf16[72,1024]{1,0:T(8,128)(2,1)S(1)} %add_convert_fusion.7), channel_id=1, source_target_pairs={{0,2},{2,4},{4,6},{6,7},{7,5},{5,3},{3,1},{1,0},{8,10},{10,12},{12... | collective-permute-start | bytes 442376 | tf_op jit(solution)/shard_map/ppermute | solution.py:451
  69.1 2.6 %collective-permute-done.38 = bf16[48,2048]{1,0:T(8,128)(2,1)S(1)} collective-permute-done((bf16[48,2048]{1,0:T(8,128)(2,1)S(1)}, bf16[48,2048]{1,0:T(8,128)(2,1)S(1)}, u32[]{:S(2)}, u32[]{:S(2)}) %collective-permute-start.38) | collective-permute-done | bytes 196640 | tf_op jit(solution)/shard_map/ppermute | solution.py:452
  75.5 2.3 %collective-permute-done.41.refs_2_ = bf16[8,3072]{1,0:T(8,128)(2,1)S(1)} collective-permute-done((bf16[8,3072]{1,0:T(8,128)(2,1)S(1)}, bf16[8,3072]{1,0:T(8,128)(2,1)S(1)}, u32[]{:S(2)}, u32[]{:S(2)}) %collective-permute-start.41) | collective-permute-done | bytes 49184 | tf_op jit(solution)/shard_map/ppermute | solution.py:43
  (92 shorter events, 29.9 us)
Async XLA Ops:
  2.1 8.9 %collective-permute-start.1 = (bf16[56,1536]{1,0:T(8,128)(2,1)S(1)}, bf16[56,1536]{1,0:T(8,128)(2,1)S(1)}, u32[]{:S(2)}, u32[]{:S(2)}) collective-permute-start(bf16[56,1536]{1,0:T(8,128)(2,1)S(1)} %get-tuple-element.50.refs_0_), channel_id=1, source_target_pairs={{0,2},{2,4},{4,6},{6,7},{7,5},{5,3},{3,1},{1,0},{8,10},{10,12},{12... | collective-permute-start | bytes 516104 | tf_op jit(solution)/shard_map/ppermute | solution.py:359
  5.2 7.9 %collective-permute-start.3 = (bf16[56,1536]{1,0:T(8,128)(2,1)S(1)}, bf16[56,1536]{1,0:T(8,128)(2,1)S(1)}, u32[]{:S(2)}, u32[]{:S(2)}) collective-permute-start(bf16[56,1536]{1,0:T(8,128)(2,1)S(1)} %get-tuple-element.49.refs_1_), channel_id=1, source_target_pairs={{2,0},{4,2},{6,4},{7,6},{5,7},{3,5},{1,3},{0,1},{10,8},{12,10},{14... | collective-permute-start | bytes 516104 | tf_op jit(solution)/shard_map/ppermute | solution.py:360
  5.2 8.4 %collective-permute-start = (bf16[56,1536]{1,0:T(8,128)(2,1)S(1)}, bf16[56,1536]{1,0:T(8,128)(2,1)S(1)}, u32[]{:S(2)}, u32[]{:S(2)}) collective-permute-start(bf16[56,1536]{1,0:T(8,128)(2,1)S(1)} %get-tuple-element.49.refs_1_), channel_id=1, source_target_pairs={{0,2},{2,4},{4,6},{6,7},{7,5},{5,3},{3,1},{1,0},{8,10},{10,12},{12... | collective-permute-start | bytes 516104 | tf_op jit(solution)/shard_map/ppermute | solution.py:364
  7.2 8.3 %collective-permute-start.2 = (bf16[56,1536]{1,0:T(8,128)(2,1)S(1)}, bf16[56,1536]{1,0:T(8,128)(2,1)S(1)}, u32[]{:S(2)}, u32[]{:S(2)}) collective-permute-start(bf16[56,1536]{1,0:T(8,128)(2,1)S(1)} %get-tuple-element.50.refs_0_), channel_id=1, source_target_pairs={{2,0},{4,2},{6,4},{7,6},{5,7},{3,5},{1,3},{0,1},{10,8},{12,10},{14... | collective-permute-start | bytes 516104 | tf_op jit(solution)/shard_map/ppermute | solution.py:365
  11.0 7.4 %collective-permute-start.4 = (bf16[56,1536]{1,0:T(8,128)(2,1)S(1)}, bf16[56,1536]{1,0:T(8,128)(2,1)S(1)}, u32[]{:S(2)}, u32[]{:S(2)}) collective-permute-start(bf16[56,1536]{1,0:T(8,128)(2,1)S(1)} %collective-permute-done.1.refs_2_), channel_id=1, source_target_pairs={{0,2},{2,4},{4,6},{6,7},{7,5},{5,3},{3,1},{1,0},{8,10},{10,12},{12... | collective-permute-start | bytes 516104 | tf_op jit(solution)/shard_map/ppermute | solution.py:359
  13.1 7.3 %collective-permute-start.7 = (bf16[56,1536]{1,0:T(8,128)(2,1)S(1)}, bf16[56,1536]{1,0:T(8,128)(2,1)S(1)}, u32[]{:S(2)}, u32[]{:S(2)}) collective-permute-start(bf16[56,1536]{1,0:T(8,128)(2,1)S(1)} %collective-permute-done.3.refs_5_), channel_id=1, source_target_pairs={{2,0},{4,2},{6,4},{7,6},{5,7},{3,5},{1,3},{0,1},{10,8},{12,10},{14... | collective-permute-start | bytes 516104 | tf_op jit(solution)/shard_map/ppermute | solution.py:360
  13.6 8.5 %collective-permute-start.5 = (bf16[56,1536]{1,0:T(8,128)(2,1)S(1)}, bf16[56,1536]{1,0:T(8,128)(2,1)S(1)}, u32[]{:S(2)}, u32[]{:S(2)}) collective-permute-start(bf16[56,1536]{1,0:T(8,128)(2,1)S(1)} %collective-permute-done.refs_3_), channel_id=1, source_target_pairs={{0,2},{2,4},{4,6},{6,7},{7,5},{5,3},{3,1},{1,0},{8,10},{10,12},{12... | collective-permute-start | bytes 516104 | tf_op jit(solution)/shard_map/ppermute | solution.py:364
  15.5 8.6 %collective-permute-start.6 = (bf16[56,1536]{1,0:T(8,128)(2,1)S(1)}, bf16[56,1536]{1,0:T(8,128)(2,1)S(1)}, u32[]{:S(2)}, u32[]{:S(2)}) collective-permute-start(bf16[56,1536]{1,0:T(8,128)(2,1)S(1)} %collective-permute-done.2.refs_4_), channel_id=1, source_target_pairs={{2,0},{4,2},{6,4},{7,6},{5,7},{3,5},{1,3},{0,1},{10,8},{12,10},{14... | collective-permute-start | bytes 516104 | tf_op jit(solution)/shard_map/ppermute | solution.py:365
  18.4 7.4 %collective-permute-start.8 = (bf16[56,1536]{1,0:T(8,128)(2,1)S(1)}, bf16[56,1536]{1,0:T(8,128)(2,1)S(1)}, u32[]{:S(2)}, u32[]{:S(2)}) collective-permute-start(bf16[56,1536]{1,0:T(8,128)(2,1)S(1)} %collective-permute-done.4.refs_0_), channel_id=1, source_target_pairs={{0,2},{2,4},{4,6},{6,7},{7,5},{5,3},{3,1},{1,0},{8,10},{10,12},{12... | collective-permute-start | bytes 516104 | tf_op jit(solution)/shard_map/ppermute | solution.py:359
  20.4 7.4 %collective-permute-start.11 = (bf16[56,1536]{1,0:T(8,128)(2,1)S(1)}, bf16[56,1536]{1,0:T(8,128)(2,1)S(1)}, u32[]{:S(2)}, u32[]{:S(2)}) collective-permute-start(bf16[56,1536]{1,0:T(8,128)(2,1)S(1)} %collective-permute-done.7.refs_3_), channel_id=1, source_target_pairs={{2,0},{4,2},{6,4},{7,6},{5,7},{3,5},{1,3},{0,1},{10,8},{12,10},{14... | collective-permute-start | bytes 516104 | tf_op jit(solution)/shard_map/ppermute | solution.py:360
  22.1 7.7 %collective-permute-start.9 = (bf16[56,1536]{1,0:T(8,128)(2,1)S(1)}, bf16[56,1536]{1,0:T(8,128)(2,1)S(1)}, u32[]{:S(2)}, u32[]{:S(2)}) collective-permute-start(bf16[56,1536]{1,0:T(8,128)(2,1)S(1)} %collective-permute-done.5.refs_1_), channel_id=1, source_target_pairs={{0,2},{2,4},{4,6},{6,7},{7,5},{5,3},{3,1},{1,0},{8,10},{10,12},{12... | collective-permute-start | bytes 516104 | tf_op jit(solution)/shard_map/ppermute | solution.py:364
  24.1 7.3 %collective-permute-start.10 = (bf16[56,1536]{1,0:T(8,128)(2,1)S(1)}, bf16[56,1536]{1,0:T(8,128)(2,1)S(1)}, u32[]{:S(2)}, u32[]{:S(2)}) collective-permute-start(bf16[56,1536]{1,0:T(8,128)(2,1)S(1)} %collective-permute-done.6.refs_2_), channel_id=1, source_target_pairs={{2,0},{4,2},{6,4},{7,6},{5,7},{3,5},{1,3},{0,1},{10,8},{12,10},{14... | collective-permute-start | bytes 516104 | tf_op jit(solution)/shard_map/ppermute | solution.py:365
  25.8 8.5 %collective-permute-start.12 = (bf16[56,1536]{1,0:T(8,128)(2,1)S(1)}, bf16[56,1536]{1,0:T(8,128)(2,1)S(1)}, u32[]{:S(2)}, u32[]{:S(2)}) collective-permute-start(bf16[56,1536]{1,0:T(8,128)(2,1)S(1)} %collective-permute-done.8.refs_0_), channel_id=1, source_target_pairs={{0,2},{2,4},{4,6},{6,7},{7,5},{5,3},{3,1},{1,0},{8,10},{10,12},{12... | collective-permute-start | bytes 516104 | tf_op jit(solution)/shard_map/ppermute | solution.py:359
  27.8 8.1 %collective-permute-start.17 = (bf16[168,512]{1,0:T(8,128)(2,1)S(1)}, bf16[168,512]{1,0:T(8,128)(2,1)S(1)}, u32[]{:S(2)}, u32[]{:S(2)}) collective-permute-start(bf16[168,512]{1,0:T(8,128)(2,1)S(1)} %get-tuple-element.65.refs_4_), channel_id=1, source_target_pairs={{0,16},{8,24},{16,0},{24,8},{1,17},{9,25},{17,1},{25,9},{2,18},{10... | collective-permute-start | bytes 516104 | tf_op jit(solution)/shard_map/ppermute | solution.py:43
  48.0 8.3 %collective-permute-start.33 = (bf16[48,2048]{1,0:T(8,128)(2,1)S(1)}, bf16[48,2048]{1,0:T(8,128)(2,1)S(1)}, u32[]{:S(2)}, u32[]{:S(2)}) collective-permute-start(bf16[48,2048]{1,0:T(8,128)(2,1)S(1)} %get-tuple-element.86), channel_id=1, source_target_pairs={{0,2},{2,4},{4,6},{6,7},{7,5},{5,3},{3,1},{1,0},{8,10},{10,12},{12... | collective-permute-start | bytes 589832 | tf_op jit(solution)/shard_map/ppermute | solution.py:456
  49.6 8.4 %collective-permute-start.36 = (bf16[48,2048]{1,0:T(8,128)(2,1)S(1)}, bf16[48,2048]{1,0:T(8,128)(2,1)S(1)}, u32[]{:S(2)}, u32[]{:S(2)}) collective-permute-start(bf16[48,2048]{1,0:T(8,128)(2,1)S(1)} %get-tuple-element.89), channel_id=1, source_target_pairs={{2,0},{4,2},{6,4},{7,6},{5,7},{3,5},{1,3},{0,1},{10,8},{12,10},{14... | collective-permute-start | bytes 589832 | tf_op jit(solution)/shard_map/ppermute | solution.py:452
  52.1 7.3 %collective-permute-start.27 = (bf16[72,1024]{1,0:T(8,128)(2,1)S(1)}, bf16[72,1024]{1,0:T(8,128)(2,1)S(1)}, u32[]{:S(2)}, u32[]{:S(2)}) collective-permute-start(bf16[72,1024]{1,0:T(8,128)(2,1)S(1)} %add_convert_fusion.9), channel_id=1, source_target_pairs={{0,2},{2,4},{4,6},{6,7},{7,5},{5,3},{3,1},{1,0},{8,10},{10,12},{12... | collective-permute-start | bytes 442376 | tf_op jit(solution)/shard_map/ppermute | solution.py:451
  53.8 7.3 %collective-permute-start.31 = (bf16[72,1024]{1,0:T(8,128)(2,1)S(1)}, bf16[72,1024]{1,0:T(8,128)(2,1)S(1)}, u32[]{:S(2)}, u32[]{:S(2)}) collective-permute-start(bf16[72,1024]{1,0:T(8,128)(2,1)S(1)} %add_convert_fusion.6), channel_id=1, source_target_pairs={{2,0},{4,2},{6,4},{7,6},{5,7},{3,5},{1,3},{0,1},{10,8},{12,10},{14... | collective-permute-start | bytes 442376 | tf_op jit(solution)/shard_map/ppermute | solution.py:457
  56.4 7.9 %collective-permute-start.34 = (bf16[48,2048]{1,0:T(8,128)(2,1)S(1)}, bf16[48,2048]{1,0:T(8,128)(2,1)S(1)}, u32[]{:S(2)}, u32[]{:S(2)}) collective-permute-start(bf16[48,2048]{1,0:T(8,128)(2,1)S(1)} %add_convert_fusion.4), channel_id=1, source_target_pairs={{0,2},{2,4},{4,6},{6,7},{7,5},{5,3},{3,1},{1,0},{8,10},{10,12},{12... | collective-permute-start | bytes 589832 | tf_op jit(solution)/shard_map/ppermute | solution.py:456
  58.1 7.9 %collective-permute-start.37 = (bf16[48,2048]{1,0:T(8,128)(2,1)S(1)}, bf16[48,2048]{1,0:T(8,128)(2,1)S(1)}, u32[]{:S(2)}, u32[]{:S(2)}) collective-permute-start(bf16[48,2048]{1,0:T(8,128)(2,1)S(1)} %add_convert_fusion.2), channel_id=1, source_target_pairs={{2,0},{4,2},{6,4},{7,6},{5,7},{3,5},{1,3},{0,1},{10,8},{12,10},{14... | collective-permute-start | bytes 589832 | tf_op jit(solution)/shard_map/ppermute | solution.py:452
  59.5 7.9 %collective-permute-start.28 = (bf16[72,1024]{1,0:T(8,128)(2,1)S(1)}, bf16[72,1024]{1,0:T(8,128)(2,1)S(1)}, u32[]{:S(2)}, u32[]{:S(2)}) collective-permute-start(bf16[72,1024]{1,0:T(8,128)(2,1)S(1)} %add_convert_fusion.8), channel_id=1, source_target_pairs={{0,2},{2,4},{4,6},{6,7},{7,5},{5,3},{3,1},{1,0},{8,10},{10,12},{12... | collective-permute-start | bytes 442376 | tf_op jit(solution)/shard_map/ppermute | solution.py:451
  61.2 11.1 %collective-permute-start.32 = (bf16[72,1024]{1,0:T(8,128)(2,1)S(1)}, bf16[72,1024]{1,0:T(8,128)(2,1)S(1)}, u32[]{:S(2)}, u32[]{:S(2)}) collective-permute-start(bf16[72,1024]{1,0:T(8,128)(2,1)S(1)} %add_convert_fusion.5), channel_id=1, source_target_pairs={{2,0},{4,2},{6,4},{7,6},{5,7},{3,5},{1,3},{0,1},{10,8},{12,10},{14... | collective-permute-start | bytes 442376 | tf_op jit(solution)/shard_map/ppermute | solution.py:457
  64.3 11.2 %collective-permute-start.35 = (bf16[48,2048]{1,0:T(8,128)(2,1)S(1)}, bf16[48,2048]{1,0:T(8,128)(2,1)S(1)}, u32[]{:S(2)}, u32[]{:S(2)}) collective-permute-start(bf16[48,2048]{1,0:T(8,128)(2,1)S(1)} %add_convert_fusion.3), channel_id=1, source_target_pairs={{0,2},{2,4},{4,6},{6,7},{7,5},{5,3},{3,1},{1,0},{8,10},{10,12},{12... | collective-permute-start | bytes 589832 | tf_op jit(solution)/shard_map/ppermute | solution.py:456
  71.8 6.9 %collective-permute-start.39 = (bf16[48,2048]{1,0:T(8,128)(2,1)S(1)}, bf16[48,2048]{1,0:T(8,128)(2,1)S(1)}, u32[]{:S(2)}, u32[]{:S(2)}) collective-permute-start(bf16[48,2048]{1,0:T(8,128)(2,1)S(1)} %add_convert_fusion), channel_id=1, source_target_pairs={{2,0},{4,2},{6,4},{7,6},{5,7},{3,5},{1,3},{0,1},{10,8},{12,10},{14... | collective-permute-start | bytes 589832 | tf_op jit(solution)/shard_map/ppermute | solution.py:452
  (23 other events, 172.6 us)

commit v8 on v7

--- a/solution.py
+++ b/solution.py
@@ -409,13 +409,12 @@
     first = range(len(groups) - 1)
     outer = range(2, n_blk)
     query, *carried = attended(
-        some((0, 1), first),
+        some((0, 1), first) + some(outer, first[:-1]),
         queries,
         (len(queries),),
         attend_kernel,
         [jax.ShapeDtypeStruct((total_rows, cols), BF16), *state],
     )
-    carried = attended(some(outer, first[:-1]), [query, *carried], (0,), attend_kernel, state)
     lead = width // 3
     left_rows = video_rows + text_rows * (width // lead)
     shapes = [

time: 79.8 us -> 79.7 us (level)
    pallas_call x12 -> x11, Pallas kernels: 17.6 us -> 17.2 us  [call(): pl.pallas_call(kernel, out_shape=outs, in_specs=[SMEM if i in smem else H...]
  transfers between devices with their start and end apart: 43 -> 43, of which waited for: 15 -> 15; matrix products, arithmetic and copies ran while one was open for 1% -> 1% of each run, Pallas kernels for 17% -> 16%
where the time goes in v8:
time: 79.7 us; the launch traced here: 79.6 us
  starting transfers between devices  40.6 us (51%)
  waiting for transfers between devices  20.5 us (26%)
  Pallas kernels  17.2 us (22%)
  between operations  0.85 us (1%)
    pallas_call x11, Pallas kernels, call(): pl.pallas_call(kernel, out_shape=outs, in_specs=[SMEM if i in smem else H...  17.2 us
    ppermute x15, starting transfers between devices, across(): return lax.ppermute(block, 'blk', [(i, i ^ distance) for i in range(n)])  10.5 us
    ppermute x4, starting transfers between devices, local(): fa = lax.ppermute(tied(fa, *due) if due else fa, 'uly', ahead)  9.18 us
    ppermute x4, starting transfers between devices, local(): fa = lax.ppermute(fa, 'uly', ahead)  6.51 us
    ppermute x3, starting transfers between devices, local(): fb = lax.ppermute(tied(fb, *due) if due else fb, 'uly', ahead)  5.89 us
    ppermute x4, waiting for transfers between devices, local(): fa = lax.ppermute(fa, 'uly', ahead)  5.02 us
    ppermute x3, starting transfers between devices, local(): fb = lax.ppermute(fb, 'uly', ahead)  4.89 us
    ppermute x3, waiting for transfers between devices, local(): fb = lax.ppermute(fb, 'uly', ahead)  4.56 us
  transfers between devices with their start and end apart: 43, of which 15 were waited for; matrix products, arithmetic and copies ran while one was open for 1% of the time, Pallas kernels for 16%

profile of v8, /device:TPU:0, one launch (start us, length us, event | category | flops | bytes accessed | tf_op | source)
XLA Modules:
  0.0 79.6 jit_solution(9226307448696653535)
XLA Ops:
  2.1 3.1 %collective-permute-start.1 = (bf16[56,1536]{1,0:T(8,128)(2,1)S(1)}, bf16[56,1536]{1,0:T(8,128)(2,1)S(1)}, u32[]{:S(2)}, u32[]{:S(2)}) collective-permute-start(bf16[56,1536]{1,0:T(8,128)(2,1)S(1)} %get-tuple-element.48.refs_0_), channel_id=1, source_target_pairs={{0,2},{2,4},{4,6},{6,7},{7,5},{5,3},{3,1},{1,0},{8,10},{10,12},{12... | collective-permute-start | bytes 516104 | tf_op jit(solution)/shard_map/ppermute | solution.py:359
  5.2 2.0 %collective-permute-start = (bf16[56,1536]{1,0:T(8,128)(2,1)S(1)}, bf16[56,1536]{1,0:T(8,128)(2,1)S(1)}, u32[]{:S(2)}, u32[]{:S(2)}) collective-permute-start(bf16[56,1536]{1,0:T(8,128)(2,1)S(1)} %get-tuple-element.47.refs_1_), channel_id=1, source_target_pairs={{0,2},{2,4},{4,6},{6,7},{7,5},{5,3},{3,1},{1,0},{8,10},{10,12},{12... | collective-permute-start | bytes 516104 | tf_op jit(solution)/shard_map/ppermute | solution.py:364
  7.2 3.8 %shard_map.114 = (bf16[3,3072,256]{2,1,0:T(8,128)(2,1)S(1)}, bf16[3,3072,256]{2,1,0:T(8,128)(2,1)S(1)}, f32[2,128]{1,0:T(2,128)S(1)}, f32[2,128]{1,0:T(2,128)S(1)}) custom-call(bf16[3,3072,256]{2,1,0:T(8,128)(2,1)} %bitcast.3, bf16[3,3072,256]{2,1,0:T(8,128)(2,1)} %bitcast.4, f32[2,128]{1,0:T(2,128)} %refs_2_.3, f32[2,128]{1,0:T(2,128)} %refs_3_.3), custom_call_target="tpu_custom_call" | custom-call | bytes 9439232 | tf_op jit(solution)/shard_map/pallas_call | solution.py:23
  11.0 2.1 %collective-permute-start.4 = (bf16[56,1536]{1,0:T(8,128)(2,1)S(1)}, bf16[56,1536]{1,0:T(8,128)(2,1)S(1)}, u32[]{:S(2)}, u32[]{:S(2)}) collective-permute-start(bf16[56,1536]{1,0:T(8,128)(2,1)S(1)} %collective-permute-done.1.refs_2_), channel_id=1, source_target_pairs={{0,2},{2,4},{4,6},{6,7},{7,5},{5,3},{3,1},{1,0},{8,10},{10,12},{12... | collective-permute-start | bytes 516104 | tf_op jit(solution)/shard_map/ppermute | solution.py:359
  13.6 1.9 %collective-permute-start.5 = (bf16[56,1536]{1,0:T(8,128)(2,1)S(1)}, bf16[56,1536]{1,0:T(8,128)(2,1)S(1)}, u32[]{:S(2)}, u32[]{:S(2)}) collective-permute-start(bf16[56,1536]{1,0:T(8,128)(2,1)S(1)} %collective-permute-done.refs_3_), channel_id=1, source_target_pairs={{0,2},{2,4},{4,6},{6,7},{7,5},{5,3},{3,1},{1,0},{8,10},{10,12},{12... | collective-permute-start | bytes 516104 | tf_op jit(solution)/shard_map/ppermute | solution.py:364
  18.4 2.0 %collective-permute-start.8 = (bf16[56,1536]{1,0:T(8,128)(2,1)S(1)}, bf16[56,1536]{1,0:T(8,128)(2,1)S(1)}, u32[]{:S(2)}, u32[]{:S(2)}) collective-permute-start(bf16[56,1536]{1,0:T(8,128)(2,1)S(1)} %collective-permute-done.4.refs_0_), channel_id=1, source_target_pairs={{0,2},{2,4},{4,6},{6,7},{7,5},{5,3},{3,1},{1,0},{8,10},{10,12},{12... | collective-permute-start | bytes 516104 | tf_op jit(solution)/shard_map/ppermute | solution.py:359
  20.4 1.6 %collective-permute-done.5.refs_1_ = bf16[56,1536]{1,0:T(8,128)(2,1)S(1)} collective-permute-done((bf16[56,1536]{1,0:T(8,128)(2,1)S(1)}, bf16[56,1536]{1,0:T(8,128)(2,1)S(1)}, u32[]{:S(2)}, u32[]{:S(2)}) %collective-permute-start.5) | collective-permute-done | bytes 172064 | tf_op jit(solution)/shard_map/ppermute | solution.py:364
  22.1 2.0 %collective-permute-start.9 = (bf16[56,1536]{1,0:T(8,128)(2,1)S(1)}, bf16[56,1536]{1,0:T(8,128)(2,1)S(1)}, u32[]{:S(2)}, u32[]{:S(2)}) collective-permute-start(bf16[56,1536]{1,0:T(8,128)(2,1)S(1)} %collective-permute-done.5.refs_1_), channel_id=1, source_target_pairs={{0,2},{2,4},{4,6},{6,7},{7,5},{5,3},{3,1},{1,0},{8,10},{10,12},{12... | collective-permute-start | bytes 516104 | tf_op jit(solution)/shard_map/ppermute | solution.py:364
  25.8 2.0 %collective-permute-start.12 = (bf16[56,1536]{1,0:T(8,128)(2,1)S(1)}, bf16[56,1536]{1,0:T(8,128)(2,1)S(1)}, u32[]{:S(2)}, u32[]{:S(2)}) collective-permute-start(bf16[56,1536]{1,0:T(8,128)(2,1)S(1)} %collective-permute-done.8.refs_0_), channel_id=1, source_target_pairs={{0,2},{2,4},{4,6},{6,7},{7,5},{5,3},{3,1},{1,0},{8,10},{10,12},{12... | collective-permute-start | bytes 516104 | tf_op jit(solution)/shard_map/ppermute | solution.py:359
  27.8 1.9 %collective-permute-start.17 = (bf16[168,512]{1,0:T(8,128)(2,1)S(1)}, bf16[168,512]{1,0:T(8,128)(2,1)S(1)}, u32[]{:S(2)}, u32[]{:S(2)}) collective-permute-start(bf16[168,512]{1,0:T(8,128)(2,1)S(1)} %get-tuple-element.63.refs_4_), channel_id=1, source_target_pairs={{0,16},{8,24},{16,0},{24,8},{1,17},{9,25},{17,1},{25,9},{2,18},{10... | collective-permute-start | bytes 516104 | tf_op jit(solution)/shard_map/ppermute | solution.py:43
  29.7 1.7 %collective-permute-start.18 = (bf16[112,512]{1,0:T(8,128)(2,1)S(1)}, bf16[112,512]{1,0:T(8,128)(2,1)S(1)}, u32[]{:S(2)}, u32[]{:S(2)}) collective-permute-start(bf16[112,512]{1,0:T(8,128)(2,1)S(1)} %get-tuple-element.64.refs_5_), channel_id=1, source_target_pairs={{0,16},{8,24},{16,0},{24,8},{1,17},{9,25},{17,1},{25,9},{2,18},{10... | collective-permute-start | bytes 344072 | tf_op jit(solution)/shard_map/ppermute | solution.py:43
  40.1 2.7 %shard_map.119 = (bf16[448,256]{1,0:T(8,128)(2,1)S(1)}, f32[4,448]{1,0:T(4,128)S(1)}, f32[256,448]{1,0:T(8,128)S(1)}) custom-call(bf16[168,256]{1,0:T(8,128)(2,1)S(1)} %get-tuple-element.54.refs_0_, bf16[112,256]{1,0:T(8,128)(2,1)S(1)} %get-tuple-element.57.refs_1_, bf16[112,256]{1,0:T(8,128)(2,1)S(1)} %get-tuple-element.60.refs_2_, ...), custom_call_target="tpu_custom_call" | custom-call | flops 616562688 | bytes 1605632 | tf_op jit(solution)/shard_map/pallas_call | solution.py:23
  43.5 1.9 %shard_map.120 = (bf16[384,256]{1,0:T(8,128)(2,1)S(1)}, bf16[72,1024]{1,0:T(8,128)(2,1)S(1)}, bf16[72,1024]{1,0:T(8,128)(2,1)S(1)}, bf16[72,1024]{1,0:T(8,128)(2...) custom-call(bf16[448,256]{1,0:T(8,128)(2,1)S(1)} %get-tuple-element., ...), custom_call_target="tpu_custom_call" | custom-call | flops 910163968 | bytes 4299776 | tf_op jit(solution)/shard_map/pallas_call | solution.py:23
  48.0 1.6 %collective-permute-start.33 = (bf16[48,2048]{1,0:T(8,128)(2,1)S(1)}, bf16[48,2048]{1,0:T(8,128)(2,1)S(1)}, u32[]{:S(2)}, u32[]{:S(2)}) collective-permute-start(bf16[48,2048]{1,0:T(8,128)(2,1)S(1)} %get-tuple-element.82), channel_id=1, source_target_pairs={{0,2},{2,4},{4,6},{6,7},{7,5},{5,3},{3,1},{1,0},{8,10},{10,12},{12... | collective-permute-start | bytes 589832 | tf_op jit(solution)/shard_map/ppermute | solution.py:455
  50.1 2.0 %collective-permute-done.26 = bf16[72,1024]{1,0:T(8,128)(2,1)S(1)} collective-permute-done((bf16[72,1024]{1,0:T(8,128)(2,1)S(1)}, bf16[72,1024]{1,0:T(8,128)(2,1)S(1)}, u32[]{:S(2)}, u32[]{:S(2)}) %collective-permute-start.26) | collective-permute-done | bytes 147488 | tf_op jit(solution)/shard_map/ppermute | solution.py:450
  52.2 1.6 %collective-permute-start.27 = (bf16[72,1024]{1,0:T(8,128)(2,1)S(1)}, bf16[72,1024]{1,0:T(8,128)(2,1)S(1)}, u32[]{:S(2)}, u32[]{:S(2)}) collective-permute-start(bf16[72,1024]{1,0:T(8,128)(2,1)S(1)} %add_convert_fusion.9), channel_id=1, source_target_pairs={{0,2},{2,4},{4,6},{6,7},{7,5},{5,3},{3,1},{1,0},{8,10},{10,12},{12... | collective-permute-start | bytes 442376 | tf_op jit(solution)/shard_map/ppermute | solution.py:450
  54.3 2.0 %collective-permute-done.33 = bf16[48,2048]{1,0:T(8,128)(2,1)S(1)} collective-permute-done((bf16[48,2048]{1,0:T(8,128)(2,1)S(1)}, bf16[48,2048]{1,0:T(8,128)(2,1)S(1)}, u32[]{:S(2)}, u32[]{:S(2)}) %collective-permute-start.33) | collective-permute-done | bytes 196640 | tf_op jit(solution)/shard_map/ppermute | solution.py:455
  56.4 1.6 %collective-permute-start.34 = (bf16[48,2048]{1,0:T(8,128)(2,1)S(1)}, bf16[48,2048]{1,0:T(8,128)(2,1)S(1)}, u32[]{:S(2)}, u32[]{:S(2)}) collective-permute-start(bf16[48,2048]{1,0:T(8,128)(2,1)S(1)} %add_convert_fusion.4), channel_id=1, source_target_pairs={{0,2},{2,4},{4,6},{6,7},{7,5},{5,3},{3,1},{1,0},{8,10},{10,12},{12... | collective-permute-start | bytes 589832 | tf_op jit(solution)/shard_map/ppermute | solution.py:455
  59.5 1.6 %collective-permute-start.28 = (bf16[72,1024]{1,0:T(8,128)(2,1)S(1)}, bf16[72,1024]{1,0:T(8,128)(2,1)S(1)}, u32[]{:S(2)}, u32[]{:S(2)}) collective-permute-start(bf16[72,1024]{1,0:T(8,128)(2,1)S(1)} %add_convert_fusion.8), channel_id=1, source_target_pairs={{0,2},{2,4},{4,6},{6,7},{7,5},{5,3},{3,1},{1,0},{8,10},{10,12},{12... | collective-permute-start | bytes 442376 | tf_op jit(solution)/shard_map/ppermute | solution.py:450
  61.7 2.6 %collective-permute-done.34 = bf16[48,2048]{1,0:T(8,128)(2,1)S(1)} collective-permute-done((bf16[48,2048]{1,0:T(8,128)(2,1)S(1)}, bf16[48,2048]{1,0:T(8,128)(2,1)S(1)}, u32[]{:S(2)}, u32[]{:S(2)}) %collective-permute-start.34) | collective-permute-done | bytes 196640 | tf_op jit(solution)/shard_map/ppermute | solution.py:455
  64.3 1.6 %collective-permute-start.35 = (bf16[48,2048]{1,0:T(8,128)(2,1)S(1)}, bf16[48,2048]{1,0:T(8,128)(2,1)S(1)}, u32[]{:S(2)}, u32[]{:S(2)}) collective-permute-start(bf16[48,2048]{1,0:T(8,128)(2,1)S(1)} %add_convert_fusion.3), channel_id=1, source_target_pairs={{0,2},{2,4},{4,6},{6,7},{7,5},{5,3},{3,1},{1,0},{8,10},{10,12},{12... | collective-permute-start | bytes 589832 | tf_op jit(solution)/shard_map/ppermute | solution.py:455
  67.5 1.6 %collective-permute-start.29 = (bf16[72,1024]{1,0:T(8,128)(2,1)S(1)}, bf16[72,1024]{1,0:T(8,128)(2,1)S(1)}, u32[]{:S(2)}, u32[]{:S(2)}) collective-permute-start(bf16[72,1024]{1,0:T(8,128)(2,1)S(1)} %add_convert_fusion.7), channel_id=1, source_target_pairs={{0,2},{2,4},{4,6},{6,7},{7,5},{5,3},{3,1},{1,0},{8,10},{10,12},{12... | collective-permute-start | bytes 442376 | tf_op jit(solution)/shard_map/ppermute | solution.py:450
  69.1 2.6 %collective-permute-done.38 = bf16[48,2048]{1,0:T(8,128)(2,1)S(1)} collective-permute-done((bf16[48,2048]{1,0:T(8,128)(2,1)S(1)}, bf16[48,2048]{1,0:T(8,128)(2,1)S(1)}, u32[]{:S(2)}, u32[]{:S(2)}) %collective-permute-start.38) | collective-permute-done | bytes 196640 | tf_op jit(solution)/shard_map/ppermute | solution.py:451
  75.4 2.3 %collective-permute-done.41.refs_2_ = bf16[8,3072]{1,0:T(8,128)(2,1)S(1)} collective-permute-done((bf16[8,3072]{1,0:T(8,128)(2,1)S(1)}, bf16[8,3072]{1,0:T(8,128)(2,1)S(1)}, u32[]{:S(2)}, u32[]{:S(2)}) %collective-permute-start.41) | collective-permute-done | bytes 49184 | tf_op jit(solution)/shard_map/ppermute | solution.py:43
  (91 shorter events, 28.8 us)
Async XLA Ops:
  2.1 8.9 %collective-permute-start.1 = (bf16[56,1536]{1,0:T(8,128)(2,1)S(1)}, bf16[56,1536]{1,0:T(8,128)(2,1)S(1)}, u32[]{:S(2)}, u32[]{:S(2)}) collective-permute-start(bf16[56,1536]{1,0:T(8,128)(2,1)S(1)} %get-tuple-element.48.refs_0_), channel_id=1, source_target_pairs={{0,2},{2,4},{4,6},{6,7},{7,5},{5,3},{3,1},{1,0},{8,10},{10,12},{12... | collective-permute-start | bytes 516104 | tf_op jit(solution)/shard_map/ppermute | solution.py:359
  5.2 7.9 %collective-permute-start.3 = (bf16[56,1536]{1,0:T(8,128)(2,1)S(1)}, bf16[56,1536]{1,0:T(8,128)(2,1)S(1)}, u32[]{:S(2)}, u32[]{:S(2)}) collective-permute-start(bf16[56,1536]{1,0:T(8,128)(2,1)S(1)} %get-tuple-element.47.refs_1_), channel_id=1, source_target_pairs={{2,0},{4,2},{6,4},{7,6},{5,7},{3,5},{1,3},{0,1},{10,8},{12,10},{14... | collective-permute-start | bytes 516104 | tf_op jit(solution)/shard_map/ppermute | solution.py:360
  5.2 8.4 %collective-permute-start = (bf16[56,1536]{1,0:T(8,128)(2,1)S(1)}, bf16[56,1536]{1,0:T(8,128)(2,1)S(1)}, u32[]{:S(2)}, u32[]{:S(2)}) collective-permute-start(bf16[56,1536]{1,0:T(8,128)(2,1)S(1)} %get-tuple-element.47.refs_1_), channel_id=1, source_target_pairs={{0,2},{2,4},{4,6},{6,7},{7,5},{5,3},{3,1},{1,0},{8,10},{10,12},{12... | collective-permute-start | bytes 516104 | tf_op jit(solution)/shard_map/ppermute | solution.py:364
  7.2 8.3 %collective-permute-start.2 = (bf16[56,1536]{1,0:T(8,128)(2,1)S(1)}, bf16[56,1536]{1,0:T(8,128)(2,1)S(1)}, u32[]{:S(2)}, u32[]{:S(2)}) collective-permute-start(bf16[56,1536]{1,0:T(8,128)(2,1)S(1)} %get-tuple-element.48.refs_0_), channel_id=1, source_target_pairs={{2,0},{4,2},{6,4},{7,6},{5,7},{3,5},{1,3},{0,1},{10,8},{12,10},{14... | collective-permute-start | bytes 516104 | tf_op jit(solution)/shard_map/ppermute | solution.py:365
  11.0 7.4 %collective-permute-start.4 = (bf16[56,1536]{1,0:T(8,128)(2,1)S(1)}, bf16[56,1536]{1,0:T(8,128)(2,1)S(1)}, u32[]{:S(2)}, u32[]{:S(2)}) collective-permute-start(bf16[56,1536]{1,0:T(8,128)(2,1)S(1)} %collective-permute-done.1.refs_2_), channel_id=1, source_target_pairs={{0,2},{2,4},{4,6},{6,7},{7,5},{5,3},{3,1},{1,0},{8,10},{10,12},{12... | collective-permute-start | bytes 516104 | tf_op jit(solution)/shard_map/ppermute | solution.py:359
  13.1 7.3 %collective-permute-start.7 = (bf16[56,1536]{1,0:T(8,128)(2,1)S(1)}, bf16[56,1536]{1,0:T(8,128)(2,1)S(1)}, u32[]{:S(2)}, u32[]{:S(2)}) collective-permute-start(bf16[56,1536]{1,0:T(8,128)(2,1)S(1)} %collective-permute-done.3.refs_5_), channel_id=1, source_target_pairs={{2,0},{4,2},{6,4},{7,6},{5,7},{3,5},{1,3},{0,1},{10,8},{12,10},{14... | collective-permute-start | bytes 516104 | tf_op jit(solution)/shard_map/ppermute | solution.py:360
  13.6 8.5 %collective-permute-start.5 = (bf16[56,1536]{1,0:T(8,128)(2,1)S(1)}, bf16[56,1536]{1,0:T(8,128)(2,1)S(1)}, u32[]{:S(2)}, u32[]{:S(2)}) collective-permute-start(bf16[56,1536]{1,0:T(8,128)(2,1)S(1)} %collective-permute-done.refs_3_), channel_id=1, source_target_pairs={{0,2},{2,4},{4,6},{6,7},{7,5},{5,3},{3,1},{1,0},{8,10},{10,12},{12... | collective-permute-start | bytes 516104 | tf_op jit(solution)/shard_map/ppermute | solution.py:364
  15.5 8.6 %collective-permute-start.6 = (bf16[56,1536]{1,0:T(8,128)(2,1)S(1)}, bf16[56,1536]{1,0:T(8,128)(2,1)S(1)}, u32[]{:S(2)}, u32[]{:S(2)}) collective-permute-start(bf16[56,1536]{1,0:T(8,128)(2,1)S(1)} %collective-permute-done.2.refs_4_), channel_id=1, source_target_pairs={{2,0},{4,2},{6,4},{7,6},{5,7},{3,5},{1,3},{0,1},{10,8},{12,10},{14... | collective-permute-start | bytes 516104 | tf_op jit(solution)/shard_map/ppermute | solution.py:365
  18.4 7.4 %collective-permute-start.8 = (bf16[56,1536]{1,0:T(8,128)(2,1)S(1)}, bf16[56,1536]{1,0:T(8,128)(2,1)S(1)}, u32[]{:S(2)}, u32[]{:S(2)}) collective-permute-start(bf16[56,1536]{1,0:T(8,128)(2,1)S(1)} %collective-permute-done.4.refs_0_), channel_id=1, source_target_pairs={{0,2},{2,4},{4,6},{6,7},{7,5},{5,3},{3,1},{1,0},{8,10},{10,12},{12... | collective-permute-start | bytes 516104 | tf_op jit(solution)/shard_map/ppermute | solution.py:359
  20.4 7.4 %collective-permute-start.11 = (bf16[56,1536]{1,0:T(8,128)(2,1)S(1)}, bf16[56,1536]{1,0:T(8,128)(2,1)S(1)}, u32[]{:S(2)}, u32[]{:S(2)}) collective-permute-start(bf16[56,1536]{1,0:T(8,128)(2,1)S(1)} %collective-permute-done.7.refs_3_), channel_id=1, source_target_pairs={{2,0},{4,2},{6,4},{7,6},{5,7},{3,5},{1,3},{0,1},{10,8},{12,10},{14... | collective-permute-start | bytes 516104 | tf_op jit(solution)/shard_map/ppermute | solution.py:360
  22.1 7.7 %collective-permute-start.9 = (bf16[56,1536]{1,0:T(8,128)(2,1)S(1)}, bf16[56,1536]{1,0:T(8,128)(2,1)S(1)}, u32[]{:S(2)}, u32[]{:S(2)}) collective-permute-start(bf16[56,1536]{1,0:T(8,128)(2,1)S(1)} %collective-permute-done.5.refs_1_), channel_id=1, source_target_pairs={{0,2},{2,4},{4,6},{6,7},{7,5},{5,3},{3,1},{1,0},{8,10},{10,12},{12... | collective-permute-start | bytes 516104 | tf_op jit(solution)/shard_map/ppermute | solution.py:364
  24.1 7.3 %collective-permute-start.10 = (bf16[56,1536]{1,0:T(8,128)(2,1)S(1)}, bf16[56,1536]{1,0:T(8,128)(2,1)S(1)}, u32[]{:S(2)}, u32[]{:S(2)}) collective-permute-start(bf16[56,1536]{1,0:T(8,128)(2,1)S(1)} %collective-permute-done.6.refs_2_), channel_id=1, source_target_pairs={{2,0},{4,2},{6,4},{7,6},{5,7},{3,5},{1,3},{0,1},{10,8},{12,10},{14... | collective-permute-start | bytes 516104 | tf_op jit(solution)/shard_map/ppermute | solution.py:365
  25.8 8.5 %collective-permute-start.12 = (bf16[56,1536]{1,0:T(8,128)(2,1)S(1)}, bf16[56,1536]{1,0:T(8,128)(2,1)S(1)}, u32[]{:S(2)}, u32[]{:S(2)}) collective-permute-start(bf16[56,1536]{1,0:T(8,128)(2,1)S(1)} %collective-permute-done.8.refs_0_), channel_id=1, source_target_pairs={{0,2},{2,4},{4,6},{6,7},{7,5},{5,3},{3,1},{1,0},{8,10},{10,12},{12... | collective-permute-start | bytes 516104 | tf_op jit(solution)/shard_map/ppermute | solution.py:359
  27.8 8.1 %collective-permute-start.17 = (bf16[168,512]{1,0:T(8,128)(2,1)S(1)}, bf16[168,512]{1,0:T(8,128)(2,1)S(1)}, u32[]{:S(2)}, u32[]{:S(2)}) collective-permute-start(bf16[168,512]{1,0:T(8,128)(2,1)S(1)} %get-tuple-element.63.refs_4_), channel_id=1, source_target_pairs={{0,16},{8,24},{16,0},{24,8},{1,17},{9,25},{17,1},{25,9},{2,18},{10... | collective-permute-start | bytes 516104 | tf_op jit(solution)/shard_map/ppermute | solution.py:43
  48.0 8.3 %collective-permute-start.33 = (bf16[48,2048]{1,0:T(8,128)(2,1)S(1)}, bf16[48,2048]{1,0:T(8,128)(2,1)S(1)}, u32[]{:S(2)}, u32[]{:S(2)}) collective-permute-start(bf16[48,2048]{1,0:T(8,128)(2,1)S(1)} %get-tuple-element.82), channel_id=1, source_target_pairs={{0,2},{2,4},{4,6},{6,7},{7,5},{5,3},{3,1},{1,0},{8,10},{10,12},{12... | collective-permute-start | bytes 589832 | tf_op jit(solution)/shard_map/ppermute | solution.py:455
  49.7 8.4 %collective-permute-start.36 = (bf16[48,2048]{1,0:T(8,128)(2,1)S(1)}, bf16[48,2048]{1,0:T(8,128)(2,1)S(1)}, u32[]{:S(2)}, u32[]{:S(2)}) collective-permute-start(bf16[48,2048]{1,0:T(8,128)(2,1)S(1)} %get-tuple-element.85), channel_id=1, source_target_pairs={{2,0},{4,2},{6,4},{7,6},{5,7},{3,5},{1,3},{0,1},{10,8},{12,10},{14... | collective-permute-start | bytes 589832 | tf_op jit(solution)/shard_map/ppermute | solution.py:451
  52.2 7.3 %collective-permute-start.27 = (bf16[72,1024]{1,0:T(8,128)(2,1)S(1)}, bf16[72,1024]{1,0:T(8,128)(2,1)S(1)}, u32[]{:S(2)}, u32[]{:S(2)}) collective-permute-start(bf16[72,1024]{1,0:T(8,128)(2,1)S(1)} %add_convert_fusion.9), channel_id=1, source_target_pairs={{0,2},{2,4},{4,6},{6,7},{7,5},{5,3},{3,1},{1,0},{8,10},{10,12},{12... | collective-permute-start | bytes 442376 | tf_op jit(solution)/shard_map/ppermute | solution.py:450
  53.8 7.3 %collective-permute-start.31 = (bf16[72,1024]{1,0:T(8,128)(2,1)S(1)}, bf16[72,1024]{1,0:T(8,128)(2,1)S(1)}, u32[]{:S(2)}, u32[]{:S(2)}) collective-permute-start(bf16[72,1024]{1,0:T(8,128)(2,1)S(1)} %add_convert_fusion.6), channel_id=1, source_target_pairs={{2,0},{4,2},{6,4},{7,6},{5,7},{3,5},{1,3},{0,1},{10,8},{12,10},{14... | collective-permute-start | bytes 442376 | tf_op jit(solution)/shard_map/ppermute | solution.py:456
  56.4 7.9 %collective-permute-start.34 = (bf16[48,2048]{1,0:T(8,128)(2,1)S(1)}, bf16[48,2048]{1,0:T(8,128)(2,1)S(1)}, u32[]{:S(2)}, u32[]{:S(2)}) collective-permute-start(bf16[48,2048]{1,0:T(8,128)(2,1)S(1)} %add_convert_fusion.4), channel_id=1, source_target_pairs={{0,2},{2,4},{4,6},{6,7},{7,5},{5,3},{3,1},{1,0},{8,10},{10,12},{12... | collective-permute-start | bytes 589832 | tf_op jit(solution)/shard_map/ppermute | solution.py:455
  58.1 7.9 %collective-permute-start.37 = (bf16[48,2048]{1,0:T(8,128)(2,1)S(1)}, bf16[48,2048]{1,0:T(8,128)(2,1)S(1)}, u32[]{:S(2)}, u32[]{:S(2)}) collective-permute-start(bf16[48,2048]{1,0:T(8,128)(2,1)S(1)} %add_convert_fusion.2), channel_id=1, source_target_pairs={{2,0},{4,2},{6,4},{7,6},{5,7},{3,5},{1,3},{0,1},{10,8},{12,10},{14... | collective-permute-start | bytes 589832 | tf_op jit(solution)/shard_map/ppermute | solution.py:451
  59.5 7.9 %collective-permute-start.28 = (bf16[72,1024]{1,0:T(8,128)(2,1)S(1)}, bf16[72,1024]{1,0:T(8,128)(2,1)S(1)}, u32[]{:S(2)}, u32[]{:S(2)}) collective-permute-start(bf16[72,1024]{1,0:T(8,128)(2,1)S(1)} %add_convert_fusion.8), channel_id=1, source_target_pairs={{0,2},{2,4},{4,6},{6,7},{7,5},{5,3},{3,1},{1,0},{8,10},{10,12},{12... | collective-permute-start | bytes 442376 | tf_op jit(solution)/shard_map/ppermute | solution.py:450
  61.2 11.1 %collective-permute-start.32 = (bf16[72,1024]{1,0:T(8,128)(2,1)S(1)}, bf16[72,1024]{1,0:T(8,128)(2,1)S(1)}, u32[]{:S(2)}, u32[]{:S(2)}) collective-permute-start(bf16[72,1024]{1,0:T(8,128)(2,1)S(1)} %add_convert_fusion.5), channel_id=1, source_target_pairs={{2,0},{4,2},{6,4},{7,6},{5,7},{3,5},{1,3},{0,1},{10,8},{12,10},{14... | collective-permute-start | bytes 442376 | tf_op jit(solution)/shard_map/ppermute | solution.py:456
  64.3 11.1 %collective-permute-start.35 = (bf16[48,2048]{1,0:T(8,128)(2,1)S(1)}, bf16[48,2048]{1,0:T(8,128)(2,1)S(1)}, u32[]{:S(2)}, u32[]{:S(2)}) collective-permute-start(bf16[48,2048]{1,0:T(8,128)(2,1)S(1)} %add_convert_fusion.3), channel_id=1, source_target_pairs={{0,2},{2,4},{4,6},{6,7},{7,5},{5,3},{3,1},{1,0},{8,10},{10,12},{12... | collective-permute-start | bytes 589832 | tf_op jit(solution)/shard_map/ppermute | solution.py:455
  71.8 6.8 %collective-permute-start.39 = (bf16[48,2048]{1,0:T(8,128)(2,1)S(1)}, bf16[48,2048]{1,0:T(8,128)(2,1)S(1)}, u32[]{:S(2)}, u32[]{:S(2)}) collective-permute-start(bf16[48,2048]{1,0:T(8,128)(2,1)S(1)} %add_convert_fusion), channel_id=1, source_target_pairs={{2,0},{4,2},{6,4},{7,6},{5,7},{3,5},{1,3},{0,1},{10,8},{12,10},{14... | collective-permute-start | bytes 589832 | tf_op jit(solution)/shard_map/ppermute | solution.py:451
  (23 other events, 169.9 us)
